TPU v7x, 32 devices: a whole 2x2x4 slice. The times are simulated.
32 devices in a mesh: tm: 16 (over z, y, core), space: 2 (over x).
Axes of the slice: x: 2, y: 2, z: 4, core: 2. Of those that a mesh axis runs over, the one named last changes fastest.
Arguments:
- initial: float32 [20, 128, 128], P('space'), may hold values from -6 to 6
- guess: float32 [16, 20, 128, 128], P('tm', 'space'), may hold values from -6 to 6
- diffusivity: float32 [20, 128, 128], P('space'), may hold values from 0.5 to 1
- velocity: float32 [3, 20, 128, 128], P(None, 'space'), may hold values from -1 to 1
Outputs:
- updated: float32 [16, 20, 128, 128], P('tm', 'space')
All inputs are finite; a program needn't handle non-finite values.
Results may differ from a plain program's by a relative error of at most 0.00002.
Values sent between devices are 32-bit elements; how exact they have to be, the bound alone decides.
No kernel may reach another device: no remote copies, remote signals or barrier semaphores. Data moves between devices by JAX's collectives and lax.ppermute only.
A program may use at most 64 MiB of HBM per device.

v0:
```python
import jax
import jax.numpy as jnp
from jax import lax
from jax.sharding import PartitionSpec as P

STEPS = 10


FINE_DIFF = 0.01
FINE_ADV = 0.012
COARSE_DIFF = 0.1
COARSE_ADV = 0.12


def padded_2(cells, sides, width):
    for axis, dim in sides:
        count = lax.axis_size(axis)
        ends = count - 1
        head = lax.slice_in_dim(cells, 0, width, axis=dim)
        tail = lax.slice_in_dim(cells, cells.shape[dim] - width, cells.shape[dim], axis=dim)
        cells = jnp.concatenate(
            [
                lax.ppermute(tail, axis, [(i, (i + 1) % count) for i in range(ends)]),
                cells,
                lax.ppermute(head, axis, [((i + 1) % count, i) for i in range(ends)]),
            ],
            axis=dim,
        )
    return cells


def from_behind(value, axis, steps):
    count = lax.axis_size(axis)
    first, last = (max(0, -steps), min(count, count - steps))
    return lax.ppermute(value, axis, [(source, source + steps) for source in range(first, last)])


def stencil(extended, diffus, pos_vel, neg_vel, diff_rate, adv_rate):
    center = extended[..., 1:-1, :, :]
    z_low = extended[..., :-2, :, :]
    z_high = extended[..., 2:, :, :]
    widths = [(0, 0)] * (center.ndim - 2) + [(1, 1), (1, 1)]
    padded = jnp.pad(center, widths)
    x_low = padded[..., :-2, 1:-1]
    x_high = padded[..., 2:, 1:-1]
    y_low = padded[..., 1:-1, :-2]
    y_high = padded[..., 1:-1, 2:]
    laplace = z_low + z_high + (x_low + x_high) + (y_low + y_high) - 6.0 * center
    advect = pos_vel[0] * (center - z_low) + neg_vel[0] * (z_high - center)
    advect = advect + pos_vel[1] * (center - x_low) + neg_vel[1] * (x_high - center)
    advect = advect + pos_vel[2] * (center - y_low) + neg_vel[2] * (y_high - center)
    return center + diff_rate * diffus * laplace - adv_rate * advect


def per_device(initial, guess, diffusivity, velocity):
    pos_vel = jnp.maximum(velocity, 0.0)
    neg_vel = jnp.minimum(velocity, 0.0)
    depth = diffusivity.shape[0]
    total_depth = depth * lax.axis_size("space")
    first_row = lax.axis_index("space") * depth
    block_index = lax.axis_index("tm")
    block_count = lax.axis_size("tm")
    state = guess[0]
    stacked = jnp.concatenate([diffusivity[None], velocity], axis=0)
    wide_coeff = padded_2(stacked, (("space", 1),), STEPS)
    wide_diff = wide_coeff[0]
    wide_pos = jnp.maximum(wide_coeff[1:], 0.0)
    wide_neg = jnp.minimum(wide_coeff[1:], 0.0)
    previous_end = from_behind(state, "tm", 1)
    starts = jnp.where(block_index == 0, initial, previous_end)
    current = padded_2(starts, (("space", 0),), STEPS)
    for step_index in range(STEPS):
        margin = STEPS - step_index - 1
        rows = depth + 2 * margin
        lower = step_index + 1
        fresh = stencil(
            current,
            wide_diff[lower : lower + rows],
            wide_pos[:, lower : lower + rows],
            wide_neg[:, lower : lower + rows],
            FINE_DIFF,
            FINE_ADV,
        )
        global_rows = first_row - margin + lax.iota(jnp.int32, rows)
        inside = (global_rows >= 0) & (global_rows < total_depth)
        current = jnp.where(inside[:, None, None], fresh, 0.0)
    residue = current - state

    def sweep_turn(index, carry):
        previous = from_behind(carry, "tm", 1)
        beside_all = padded_2(previous, (("space", 0),), 1)
        return stencil(beside_all, diffusivity, pos_vel, neg_vel, COARSE_DIFF, COARSE_ADV) + residue

    correction = lax.fori_loop(0, block_count, sweep_turn, jnp.zeros_like(state))
    state = state + correction
    return state[None]


def solution(mesh):
    in_specs = (
        P("space", None, None),
        P("tm", "space", None, None),
        P("space", None, None),
        P(None, "space", None, None),
    )
    out_specs = P("tm", "space", None, None)
    return jax.shard_map(
        per_device, mesh=mesh, in_specs=in_specs, out_specs=out_specs, check_vma=False
    )
```

profile of v0, /device:TPU:18, one launch (start us, length us, event | category | flops | bytes accessed | tf_op | source)
XLA Modules:
  0.0 531.9 jit_solution(7052651154296032995)
XLA Ops:
  0.0 3.6 pad_maximum_fusion.3
  5.0 7.5 %collective-permute-start.7 = (f32[4,10,128,128]{3,2,1,0:T(8,128)}, f32[4,10,128,128]{3,2,1,0:T(8,128)}, u32[]{:S(2)}, u32[]{:S(2)}) collective-permute-start(f32[4,10,128,128]{3,2,1,0:T(8,128)} %pad_maximum_fusion.3), channel_id=1, source_target_pairs={{1,0},{3,2},{5,4},{7,6},{9,8},{11,10},{13,12},{15,14},{17,16},{19,... | collective-permute-start | bytes 7864328 | tf_op jit(solution)/shard_map/ppermute | solution.py:25
  14.6 10.8 %collective-permute-done.3 = f32[10,128,128]{2,1,0:T(8,128)} collective-permute-done((f32[10,128,128]{2,1,0:T(8,128)S(1)}, f32[10,128,128]{2,1,0:T(8,128)}, u32[]{:S(2)}, u32[]{:S(2)}) %collective-permute-start.3) | collective-permute-done | bytes 655392 | tf_op jit(solution)/shard_map/ppermute | solution.py:35
  27.9 4.6 collective-permute-start.5
  32.6 2.4 broadcast_minimum_fusion
  35.0 43.5 %collective-permute-done.4 = f32[10,128,128]{2,1,0:T(8,128)S(1)} collective-permute-done((f32[10,128,128]{2,1,0:T(8,128)S(1)}, f32[10,128,128]{2,1,0:T(8,128)S(1)}, u32[]{:S(2)}, u32[]{:S(2)}) %collective-permute-start.4) | collective-permute-done | bytes 655392 | tf_op jit(solution)/shard_map/ppermute | solution.py:23
  78.5 2.6 collective-permute-done.5
  84.4 3.0 pad_maximum_fusion.2
  89.4 8.1 %fusion.22 = f32[28,128,128]{2,1,0:T(8,128)S(1)} fusion(f32[3,30,128,128]{3,2,1,0:T(8,128)S(1)} %get-tuple-element.119, f32[3,30,128,128]{3,2,1,0:T(8,128)S(1)} %get-tuple-element.118, f32[28,128,128]{2,1,0:T(8,128)} %slice.766, f32[4,30,128,128]{3,2,1,0:T(8,128)S(1)} %pad_maximum_fusion.2, f32[30,128,128]{2,1,0:T(8,128)} %copy-done.2, ...), kind=kLoop, calls=%fused_computation.79 | loop fusion | flops 13762560 | bytes 20185116 | tf_op jit(solution)/shard_map/jit(_where)/select_n | solution.py:86
  97.7 3.0 fusion.39
  100.9 2.7 fusion.56
  103.7 2.5 fusion.73
  106.3 2.2 fusion.90
  117.0 412.7 %while.13 = (s32[]{:T(128)}, f32[10,128,128]{2,1,0:T(8,128)}, f32[10,128,128]{2,1,0:T(8,128)S(1)}, f32[3,10,128,128]{3,2,1,0:T(8,128)}, f32[3,10,128,128]{3,2,1,...) while((s32[]{:T(128)}, f32[10,128,128]{2,1,0:T(8,128)}, ...), condition=%wide.region_1.2_spmd.clone, body=%wide.region_0.1_spmd.clone.sunk | while | flops 5406723 | bytes 11403479 | solution.py:94
  119.0 10.9 %collective-permute-done = f32[10,128,128]{2,1,0:T(8,128)S(1)} collective-permute-done((f32[10,128,128]{2,1,0:T(8,128)S(1)}, f32[10,128,128]{2,1,0:T(8,128)S(1)}, u32[]{:S(2)}, u32[]{:S(2)}) %collective-permute-start) | collective-permute-done | bytes 655392 | tf_op jit(solution)/shard_map/while/body/eval_jaxpr/ppermute | solution.py:35
  130.5 4.4 collective-permute-start.1
  137.1 4.0 collective-permute-done.2
  141.0 3.4 fusion.190
  147.5 10.9 %collective-permute-done = f32[10,128,128]{2,1,0:T(8,128)S(1)} collective-permute-done((f32[10,128,128]{2,1,0:T(8,128)S(1)}, f32[10,128,128]{2,1,0:T(8,128)S(1)}, u32[]{:S(2)}, u32[]{:S(2)}) %collective-permute-start) | collective-permute-done | bytes 655392 | tf_op jit(solution)/shard_map/while/body/eval_jaxpr/ppermute | solution.py:35
  162.8 4.0 collective-permute-done.2
  166.7 3.4 fusion.190
  173.2 10.9 %collective-permute-done = f32[10,128,128]{2,1,0:T(8,128)S(1)} collective-permute-done((f32[10,128,128]{2,1,0:T(8,128)S(1)}, f32[10,128,128]{2,1,0:T(8,128)S(1)}, u32[]{:S(2)}, u32[]{:S(2)}) %collective-permute-start) | collective-permute-done | bytes 655392 | tf_op jit(solution)/shard_map/while/body/eval_jaxpr/ppermute | solution.py:35
  188.5 4.0 collective-permute-done.2
  192.4 3.4 fusion.190
  198.9 10.9 %collective-permute-done = f32[10,128,128]{2,1,0:T(8,128)S(1)} collective-permute-done((f32[10,128,128]{2,1,0:T(8,128)S(1)}, f32[10,128,128]{2,1,0:T(8,128)S(1)}, u32[]{:S(2)}, u32[]{:S(2)}) %collective-permute-start) | collective-permute-done | bytes 655392 | tf_op jit(solution)/shard_map/while/body/eval_jaxpr/ppermute | solution.py:35
  214.1 4.0 collective-permute-done.2
  218.1 3.4 fusion.190
  224.5 10.9 %collective-permute-done = f32[10,128,128]{2,1,0:T(8,128)S(1)} collective-permute-done((f32[10,128,128]{2,1,0:T(8,128)S(1)}, f32[10,128,128]{2,1,0:T(8,128)S(1)}, u32[]{:S(2)}, u32[]{:S(2)}) %collective-permute-start) | collective-permute-done | bytes 655392 | tf_op jit(solution)/shard_map/while/body/eval_jaxpr/ppermute | solution.py:35
  239.8 4.0 collective-permute-done.2
  243.8 3.4 fusion.190
  250.2 10.9 %collective-permute-done = f32[10,128,128]{2,1,0:T(8,128)S(1)} collective-permute-done((f32[10,128,128]{2,1,0:T(8,128)S(1)}, f32[10,128,128]{2,1,0:T(8,128)S(1)}, u32[]{:S(2)}, u32[]{:S(2)}) %collective-permute-start) | collective-permute-done | bytes 655392 | tf_op jit(solution)/shard_map/while/body/eval_jaxpr/ppermute | solution.py:35
  265.5 4.0 collective-permute-done.2
  269.5 3.4 fusion.190
  275.9 10.9 %collective-permute-done = f32[10,128,128]{2,1,0:T(8,128)S(1)} collective-permute-done((f32[10,128,128]{2,1,0:T(8,128)S(1)}, f32[10,128,128]{2,1,0:T(8,128)S(1)}, u32[]{:S(2)}, u32[]{:S(2)}) %collective-permute-start) | collective-permute-done | bytes 655392 | tf_op jit(solution)/shard_map/while/body/eval_jaxpr/ppermute | solution.py:35
  291.2 4.0 collective-permute-done.2
  295.2 3.4 fusion.190
  301.6 10.9 %collective-permute-done = f32[10,128,128]{2,1,0:T(8,128)S(1)} collective-permute-done((f32[10,128,128]{2,1,0:T(8,128)S(1)}, f32[10,128,128]{2,1,0:T(8,128)S(1)}, u32[]{:S(2)}, u32[]{:S(2)}) %collective-permute-start) | collective-permute-done | bytes 655392 | tf_op jit(solution)/shard_map/while/body/eval_jaxpr/ppermute | solution.py:35
  316.9 4.0 collective-permute-done.2
  320.8 3.4 fusion.190
  327.3 10.9 %collective-permute-done = f32[10,128,128]{2,1,0:T(8,128)S(1)} collective-permute-done((f32[10,128,128]{2,1,0:T(8,128)S(1)}, f32[10,128,128]{2,1,0:T(8,128)S(1)}, u32[]{:S(2)}, u32[]{:S(2)}) %collective-permute-start) | collective-permute-done | bytes 655392 | tf_op jit(solution)/shard_map/while/body/eval_jaxpr/ppermute | solution.py:35
  342.6 4.0 collective-permute-done.2
  346.5 3.4 fusion.190
  353.0 10.9 %collective-permute-done = f32[10,128,128]{2,1,0:T(8,128)S(1)} collective-permute-done((f32[10,128,128]{2,1,0:T(8,128)S(1)}, f32[10,128,128]{2,1,0:T(8,128)S(1)}, u32[]{:S(2)}, u32[]{:S(2)}) %collective-permute-start) | collective-permute-done | bytes 655392 | tf_op jit(solution)/shard_map/while/body/eval_jaxpr/ppermute | solution.py:35
  368.3 4.0 collective-permute-done.2
  372.2 3.4 fusion.190
  378.7 10.9 %collective-permute-done = f32[10,128,128]{2,1,0:T(8,128)S(1)} collective-permute-done((f32[10,128,128]{2,1,0:T(8,128)S(1)}, f32[10,128,128]{2,1,0:T(8,128)S(1)}, u32[]{:S(2)}, u32[]{:S(2)}) %collective-permute-start) | collective-permute-done | bytes 655392 | tf_op jit(solution)/shard_map/while/body/eval_jaxpr/ppermute | solution.py:35
  393.9 4.0 collective-permute-done.2
  397.9 3.4 fusion.190
  404.3 10.9 %collective-permute-done = f32[10,128,128]{2,1,0:T(8,128)S(1)} collective-permute-done((f32[10,128,128]{2,1,0:T(8,128)S(1)}, f32[10,128,128]{2,1,0:T(8,128)S(1)}, u32[]{:S(2)}, u32[]{:S(2)}) %collective-permute-start) | collective-permute-done | bytes 655392 | tf_op jit(solution)/shard_map/while/body/eval_jaxpr/ppermute | solution.py:35
  419.6 4.0 collective-permute-done.2
  423.6 3.4 fusion.190
  430.0 10.9 %collective-permute-done = f32[10,128,128]{2,1,0:T(8,128)S(1)} collective-permute-done((f32[10,128,128]{2,1,0:T(8,128)S(1)}, f32[10,128,128]{2,1,0:T(8,128)S(1)}, u32[]{:S(2)}, u32[]{:S(2)}) %collective-permute-start) | collective-permute-done | bytes 655392 | tf_op jit(solution)/shard_map/while/body/eval_jaxpr/ppermute | solution.py:35
  445.3 4.0 collective-permute-done.2
  449.3 3.4 fusion.190
  455.7 10.9 %collective-permute-done = f32[10,128,128]{2,1,0:T(8,128)S(1)} collective-permute-done((f32[10,128,128]{2,1,0:T(8,128)S(1)}, f32[10,128,128]{2,1,0:T(8,128)S(1)}, u32[]{:S(2)}, u32[]{:S(2)}) %collective-permute-start) | collective-permute-done | bytes 655392 | tf_op jit(solution)/shard_map/while/body/eval_jaxpr/ppermute | solution.py:35
  471.0 4.0 collective-permute-done.2
  474.9 3.4 fusion.190
  481.4 10.9 %collective-permute-done = f32[10,128,128]{2,1,0:T(8,128)S(1)} collective-permute-done((f32[10,128,128]{2,1,0:T(8,128)S(1)}, f32[10,128,128]{2,1,0:T(8,128)S(1)}, u32[]{:S(2)}, u32[]{:S(2)}) %collective-permute-start) | collective-permute-done | bytes 655392 | tf_op jit(solution)/shard_map/while/body/eval_jaxpr/ppermute | solution.py:35
  496.7 4.0 collective-permute-done.2
  500.6 3.4 fusion.190
  507.1 10.9 %collective-permute-done = f32[10,128,128]{2,1,0:T(8,128)S(1)} collective-permute-done((f32[10,128,128]{2,1,0:T(8,128)S(1)}, f32[10,128,128]{2,1,0:T(8,128)S(1)}, u32[]{:S(2)}, u32[]{:S(2)}) %collective-permute-start) | collective-permute-done | bytes 655392 | tf_op jit(solution)/shard_map/while/body/eval_jaxpr/ppermute | solution.py:35
  522.4 4.0 collective-permute-done.2
  526.3 3.4 fusion.190
  529.7 2.2 add_bitcast_fusion
  (143 shorter events, 136.5 us)
Async XLA Ops:
  0.0 12.6 %copy-start.5 = (f32[1,10,128,128]{3,2,1,0:T(8,128)S(1)}, f32[1,10,128,128]{3,2,1,0:T(8,128)}, u32[]{:S(2)}) copy-start(f32[1,10,128,128]{3,2,1,0:T(8,128)} %param.7) | copy-start | bytes 1966084
  0.0 25.5 %copy-start.6 = (f32[10,128,128]{2,1,0:T(8,128)S(1)}, f32[10,128,128]{2,1,0:T(8,128)}, u32[]{:S(2)}) copy-start(f32[10,128,128]{2,1,0:T(8,128)} %param.6) | copy-start | bytes 1966084
  3.6 29.0 %copy-start.3 = (f32[3,10,128,128]{3,2,1,0:T(8,128)S(1)}, f32[3,10,128,128]{3,2,1,0:T(8,128)}, u32[]{:S(2)}) copy-start(f32[3,10,128,128]{3,2,1,0:T(8,128)} %param.9) | copy-start | bytes 5898244
  3.6 79.1 %collective-permute-start.6 = (f32[4,10,128,128]{3,2,1,0:T(8,128)}, f32[4,10,128,128]{3,2,1,0:T(8,128)}, u32[]{:S(2)}, u32[]{:S(2)}) collective-permute-start(f32[4,10,128,128]{3,2,1,0:T(8,128)} %pad_maximum_fusion.3), channel_id=1, source_target_pairs={{0,1},{2,3},{4,5},{6,7},{8,9},{10,11},{12,13},{14,15},{16,17},{18,... | collective-permute-start | bytes 7864328 | tf_op jit(solution)/shard_map/ppermute | solution.py:23
  5.0 78.3 %collective-permute-start.7 = (f32[4,10,128,128]{3,2,1,0:T(8,128)}, f32[4,10,128,128]{3,2,1,0:T(8,128)}, u32[]{:S(2)}, u32[]{:S(2)}) collective-permute-start(f32[4,10,128,128]{3,2,1,0:T(8,128)} %pad_maximum_fusion.3), channel_id=1, source_target_pairs={{1,0},{3,2},{5,4},{7,6},{9,8},{11,10},{13,12},{15,14},{17,16},{19,... | collective-permute-start | bytes 7864328 | tf_op jit(solution)/shard_map/ppermute | solution.py:25
  12.6 12.9 %collective-permute-start.3 = (f32[10,128,128]{2,1,0:T(8,128)S(1)}, f32[10,128,128]{2,1,0:T(8,128)}, u32[]{:S(2)}, u32[]{:S(2)}) collective-permute-start(f32[10,128,128]{2,1,0:T(8,128)S(1)} %bitcast.614), channel_id=1, source_target_pairs={{0,2},{2,4},{4,6},{6,8},{8,10},{10,12},{12,14},{14,16},{16,18},{18... | collective-permute-start | bytes 1966088 | tf_op jit(solution)/shard_map/ppermute | solution.py:35
  26.6 51.8 %collective-permute-start.4 = (f32[10,128,128]{2,1,0:T(8,128)S(1)}, f32[10,128,128]{2,1,0:T(8,128)S(1)}, u32[]{:S(2)}, u32[]{:S(2)}) collective-permute-start(f32[10,128,128]{2,1,0:T(8,128)S(1)} %broadcast_select_fusion.1), channel_id=1, source_target_pairs={{0,1},{2,3},{4,5},{6,7},{8,9},{10,11},{12,13},{14,15},{16,17},{18,... | collective-permute-start | bytes 1966088 | tf_op jit(solution)/shard_map/ppermute | solution.py:23
  27.9 53.2 %collective-permute-start.5 = (f32[10,128,128]{2,1,0:T(8,128)S(1)}, f32[10,128,128]{2,1,0:T(8,128)S(1)}, u32[]{:S(2)}, u32[]{:S(2)}) collective-permute-start(f32[10,128,128]{2,1,0:T(8,128)S(1)} %broadcast_select_fusion.1), channel_id=1, source_target_pairs={{1,0},{3,2},{5,4},{7,6},{9,8},{11,10},{13,12},{15,14},{17,16},{19,... | collective-permute-start | bytes 1966088 | tf_op jit(solution)/shard_map/ppermute | solution.py:25
  81.3 2.0 copy-start.2
  81.3 2.0 copy-start.1
  81.3 3.1 copy-start.4
  115.1 1.9 copy-start
  117.1 12.8 %collective-permute-start = (f32[10,128,128]{2,1,0:T(8,128)S(1)}, f32[10,128,128]{2,1,0:T(8,128)S(1)}, u32[]{:S(2)}, u32[]{:S(2)}) collective-permute-start(f32[10,128,128]{2,1,0:T(8,128)S(1)} %broadcast_select_fusion.3), channel_id=1, source_target_pairs={{0,2},{2,4},{4,6},{6,8},{8,10},{10,12},{12,14},{14,16},{16,18},{18... | collective-permute-start | bytes 1966088 | tf_op jit(solution)/shard_map/while/body/eval_jaxpr/ppermute | solution.py:35
  130.5 6.6 %collective-permute-start.1 = (f32[1,128,128]{2,1,0:T(8,128)}, f32[1,128,128]{2,1,0:T(8,128)S(1)}, u32[]{:S(2)}, u32[]{:S(2)}) collective-permute-start(f32[1,128,128]{2,1,0:T(8,128)} %get-tuple-element.161), channel_id=1, source_target_pairs={{1,0},{3,2},{5,4},{7,6},{9,8},{11,10},{13,12},{15,14},{17,16},{19,... | collective-permute-start | bytes 196616 | tf_op jit(solution)/shard_map/while/body/eval_jaxpr/ppermute | solution.py:25
  134.9 6.2 %collective-permute-start.2 = (f32[1,128,128]{2,1,0:T(8,128)S(1)}, f32[1,128,128]{2,1,0:T(8,128)S(1)}, u32[]{:S(2)}, u32[]{:S(2)}) collective-permute-start(f32[1,128,128]{2,1,0:T(8,128)S(1)} %get-tuple-element.162), channel_id=1, source_target_pairs={{0,1},{2,3},{4,5},{6,7},{8,9},{10,11},{12,13},{14,15},{16,17},{18,... | collective-permute-start | bytes 196616 | tf_op jit(solution)/shard_map/while/body/eval_jaxpr/ppermute | solution.py:23
  145.6 12.8 %collective-permute-start = (f32[10,128,128]{2,1,0:T(8,128)S(1)}, f32[10,128,128]{2,1,0:T(8,128)S(1)}, u32[]{:S(2)}, u32[]{:S(2)}) collective-permute-start(f32[10,128,128]{2,1,0:T(8,128)S(1)} %broadcast_select_fusion.3), channel_id=1, source_target_pairs={{0,2},{2,4},{4,6},{6,8},{8,10},{10,12},{12,14},{14,16},{16,18},{18... | collective-permute-start | bytes 1966088 | tf_op jit(solution)/shard_map/while/body/eval_jaxpr/ppermute | solution.py:35
  159.0 3.8 collective-permute-start.1
  160.6 6.2 %collective-permute-start.2 = (f32[1,128,128]{2,1,0:T(8,128)S(1)}, f32[1,128,128]{2,1,0:T(8,128)S(1)}, u32[]{:S(2)}, u32[]{:S(2)}) collective-permute-start(f32[1,128,128]{2,1,0:T(8,128)S(1)} %get-tuple-element.162), channel_id=1, source_target_pairs={{0,1},{2,3},{4,5},{6,7},{8,9},{10,11},{12,13},{14,15},{16,17},{18,... | collective-permute-start | bytes 196616 | tf_op jit(solution)/shard_map/while/body/eval_jaxpr/ppermute | solution.py:23
  171.2 12.8 %collective-permute-start = (f32[10,128,128]{2,1,0:T(8,128)S(1)}, f32[10,128,128]{2,1,0:T(8,128)S(1)}, u32[]{:S(2)}, u32[]{:S(2)}) collective-permute-start(f32[10,128,128]{2,1,0:T(8,128)S(1)} %broadcast_select_fusion.3), channel_id=1, source_target_pairs={{0,2},{2,4},{4,6},{6,8},{8,10},{10,12},{12,14},{14,16},{16,18},{18... | collective-permute-start | bytes 1966088 | tf_op jit(solution)/shard_map/while/body/eval_jaxpr/ppermute | solution.py:35
  184.7 3.8 collective-permute-start.1
  186.3 6.2 %collective-permute-start.2 = (f32[1,128,128]{2,1,0:T(8,128)S(1)}, f32[1,128,128]{2,1,0:T(8,128)S(1)}, u32[]{:S(2)}, u32[]{:S(2)}) collective-permute-start(f32[1,128,128]{2,1,0:T(8,128)S(1)} %get-tuple-element.162), channel_id=1, source_target_pairs={{0,1},{2,3},{4,5},{6,7},{8,9},{10,11},{12,13},{14,15},{16,17},{18,... | collective-permute-start | bytes 196616 | tf_op jit(solution)/shard_map/while/body/eval_jaxpr/ppermute | solution.py:23
  196.9 12.8 %collective-permute-start = (f32[10,128,128]{2,1,0:T(8,128)S(1)}, f32[10,128,128]{2,1,0:T(8,128)S(1)}, u32[]{:S(2)}, u32[]{:S(2)}) collective-permute-start(f32[10,128,128]{2,1,0:T(8,128)S(1)} %broadcast_select_fusion.3), channel_id=1, source_target_pairs={{0,2},{2,4},{4,6},{6,8},{8,10},{10,12},{12,14},{14,16},{16,18},{18... | collective-permute-start | bytes 1966088 | tf_op jit(solution)/shard_map/while/body/eval_jaxpr/ppermute | solution.py:35
  210.4 3.8 collective-permute-start.1
  211.9 6.2 %collective-permute-start.2 = (f32[1,128,128]{2,1,0:T(8,128)S(1)}, f32[1,128,128]{2,1,0:T(8,128)S(1)}, u32[]{:S(2)}, u32[]{:S(2)}) collective-permute-start(f32[1,128,128]{2,1,0:T(8,128)S(1)} %get-tuple-element.162), channel_id=1, source_target_pairs={{0,1},{2,3},{4,5},{6,7},{8,9},{10,11},{12,13},{14,15},{16,17},{18,... | collective-permute-start | bytes 196616 | tf_op jit(solution)/shard_map/while/body/eval_jaxpr/ppermute | solution.py:23
  222.6 12.8 %collective-permute-start = (f32[10,128,128]{2,1,0:T(8,128)S(1)}, f32[10,128,128]{2,1,0:T(8,128)S(1)}, u32[]{:S(2)}, u32[]{:S(2)}) collective-permute-start(f32[10,128,128]{2,1,0:T(8,128)S(1)} %broadcast_select_fusion.3), channel_id=1, source_target_pairs={{0,2},{2,4},{4,6},{6,8},{8,10},{10,12},{12,14},{14,16},{16,18},{18... | collective-permute-start | bytes 1966088 | tf_op jit(solution)/shard_map/while/body/eval_jaxpr/ppermute | solution.py:35
  236.1 3.8 collective-permute-start.1
  237.6 6.2 %collective-permute-start.2 = (f32[1,128,128]{2,1,0:T(8,128)S(1)}, f32[1,128,128]{2,1,0:T(8,128)S(1)}, u32[]{:S(2)}, u32[]{:S(2)}) collective-permute-start(f32[1,128,128]{2,1,0:T(8,128)S(1)} %get-tuple-element.162), channel_id=1, source_target_pairs={{0,1},{2,3},{4,5},{6,7},{8,9},{10,11},{12,13},{14,15},{16,17},{18,... | collective-permute-start | bytes 196616 | tf_op jit(solution)/shard_map/while/body/eval_jaxpr/ppermute | solution.py:23
  248.3 12.8 %collective-permute-start = (f32[10,128,128]{2,1,0:T(8,128)S(1)}, f32[10,128,128]{2,1,0:T(8,128)S(1)}, u32[]{:S(2)}, u32[]{:S(2)}) collective-permute-start(f32[10,128,128]{2,1,0:T(8,128)S(1)} %broadcast_select_fusion.3), channel_id=1, source_target_pairs={{0,2},{2,4},{4,6},{6,8},{8,10},{10,12},{12,14},{14,16},{16,18},{18... | collective-permute-start | bytes 1966088 | tf_op jit(solution)/shard_map/while/body/eval_jaxpr/ppermute | solution.py:35
  261.7 3.8 collective-permute-start.1
  263.3 6.2 %collective-permute-start.2 = (f32[1,128,128]{2,1,0:T(8,128)S(1)}, f32[1,128,128]{2,1,0:T(8,128)S(1)}, u32[]{:S(2)}, u32[]{:S(2)}) collective-permute-start(f32[1,128,128]{2,1,0:T(8,128)S(1)} %get-tuple-element.162), channel_id=1, source_target_pairs={{0,1},{2,3},{4,5},{6,7},{8,9},{10,11},{12,13},{14,15},{16,17},{18,... | collective-permute-start | bytes 196616 | tf_op jit(solution)/shard_map/while/body/eval_jaxpr/ppermute | solution.py:23
  274.0 12.8 %collective-permute-start = (f32[10,128,128]{2,1,0:T(8,128)S(1)}, f32[10,128,128]{2,1,0:T(8,128)S(1)}, u32[]{:S(2)}, u32[]{:S(2)}) collective-permute-start(f32[10,128,128]{2,1,0:T(8,128)S(1)} %broadcast_select_fusion.3), channel_id=1, source_target_pairs={{0,2},{2,4},{4,6},{6,8},{8,10},{10,12},{12,14},{14,16},{16,18},{18... | collective-permute-start | bytes 1966088 | tf_op jit(solution)/shard_map/while/body/eval_jaxpr/ppermute | solution.py:35
  287.4 3.8 collective-permute-start.1
  289.0 6.2 %collective-permute-start.2 = (f32[1,128,128]{2,1,0:T(8,128)S(1)}, f32[1,128,128]{2,1,0:T(8,128)S(1)}, u32[]{:S(2)}, u32[]{:S(2)}) collective-permute-start(f32[1,128,128]{2,1,0:T(8,128)S(1)} %get-tuple-element.162), channel_id=1, source_target_pairs={{0,1},{2,3},{4,5},{6,7},{8,9},{10,11},{12,13},{14,15},{16,17},{18,... | collective-permute-start | bytes 196616 | tf_op jit(solution)/shard_map/while/body/eval_jaxpr/ppermute | solution.py:23
  299.7 12.8 %collective-permute-start = (f32[10,128,128]{2,1,0:T(8,128)S(1)}, f32[10,128,128]{2,1,0:T(8,128)S(1)}, u32[]{:S(2)}, u32[]{:S(2)}) collective-permute-start(f32[10,128,128]{2,1,0:T(8,128)S(1)} %broadcast_select_fusion.3), channel_id=1, source_target_pairs={{0,2},{2,4},{4,6},{6,8},{8,10},{10,12},{12,14},{14,16},{16,18},{18... | collective-permute-start | bytes 1966088 | tf_op jit(solution)/shard_map/while/body/eval_jaxpr/ppermute | solution.py:35
  313.1 3.8 collective-permute-start.1
  314.7 6.2 %collective-permute-start.2 = (f32[1,128,128]{2,1,0:T(8,128)S(1)}, f32[1,128,128]{2,1,0:T(8,128)S(1)}, u32[]{:S(2)}, u32[]{:S(2)}) collective-permute-start(f32[1,128,128]{2,1,0:T(8,128)S(1)} %get-tuple-element.162), channel_id=1, source_target_pairs={{0,1},{2,3},{4,5},{6,7},{8,9},{10,11},{12,13},{14,15},{16,17},{18,... | collective-permute-start | bytes 196616 | tf_op jit(solution)/shard_map/while/body/eval_jaxpr/ppermute | solution.py:23
  325.4 12.8 %collective-permute-start = (f32[10,128,128]{2,1,0:T(8,128)S(1)}, f32[10,128,128]{2,1,0:T(8,128)S(1)}, u32[]{:S(2)}, u32[]{:S(2)}) collective-permute-start(f32[10,128,128]{2,1,0:T(8,128)S(1)} %broadcast_select_fusion.3), channel_id=1, source_target_pairs={{0,2},{2,4},{4,6},{6,8},{8,10},{10,12},{12,14},{14,16},{16,18},{18... | collective-permute-start | bytes 1966088 | tf_op jit(solution)/shard_map/while/body/eval_jaxpr/ppermute | solution.py:35
  338.8 3.8 collective-permute-start.1
  340.4 6.2 %collective-permute-start.2 = (f32[1,128,128]{2,1,0:T(8,128)S(1)}, f32[1,128,128]{2,1,0:T(8,128)S(1)}, u32[]{:S(2)}, u32[]{:S(2)}) collective-permute-start(f32[1,128,128]{2,1,0:T(8,128)S(1)} %get-tuple-element.162), channel_id=1, source_target_pairs={{0,1},{2,3},{4,5},{6,7},{8,9},{10,11},{12,13},{14,15},{16,17},{18,... | collective-permute-start | bytes 196616 | tf_op jit(solution)/shard_map/while/body/eval_jaxpr/ppermute | solution.py:23
  351.0 12.8 %collective-permute-start = (f32[10,128,128]{2,1,0:T(8,128)S(1)}, f32[10,128,128]{2,1,0:T(8,128)S(1)}, u32[]{:S(2)}, u32[]{:S(2)}) collective-permute-start(f32[10,128,128]{2,1,0:T(8,128)S(1)} %broadcast_select_fusion.3), channel_id=1, source_target_pairs={{0,2},{2,4},{4,6},{6,8},{8,10},{10,12},{12,14},{14,16},{16,18},{18... | collective-permute-start | bytes 1966088 | tf_op jit(solution)/shard_map/while/body/eval_jaxpr/ppermute | solution.py:35
  364.5 3.8 collective-permute-start.1
  366.1 6.2 %collective-permute-start.2 = (f32[1,128,128]{2,1,0:T(8,128)S(1)}, f32[1,128,128]{2,1,0:T(8,128)S(1)}, u32[]{:S(2)}, u32[]{:S(2)}) collective-permute-start(f32[1,128,128]{2,1,0:T(8,128)S(1)} %get-tuple-element.162), channel_id=1, source_target_pairs={{0,1},{2,3},{4,5},{6,7},{8,9},{10,11},{12,13},{14,15},{16,17},{18,... | collective-permute-start | bytes 196616 | tf_op jit(solution)/shard_map/while/body/eval_jaxpr/ppermute | solution.py:23
  376.7 12.8 %collective-permute-start = (f32[10,128,128]{2,1,0:T(8,128)S(1)}, f32[10,128,128]{2,1,0:T(8,128)S(1)}, u32[]{:S(2)}, u32[]{:S(2)}) collective-permute-start(f32[10,128,128]{2,1,0:T(8,128)S(1)} %broadcast_select_fusion.3), channel_id=1, source_target_pairs={{0,2},{2,4},{4,6},{6,8},{8,10},{10,12},{12,14},{14,16},{16,18},{18... | collective-permute-start | bytes 1966088 | tf_op jit(solution)/shard_map/while/body/eval_jaxpr/ppermute | solution.py:35
  390.2 3.8 collective-permute-start.1
  391.7 6.2 %collective-permute-start.2 = (f32[1,128,128]{2,1,0:T(8,128)S(1)}, f32[1,128,128]{2,1,0:T(8,128)S(1)}, u32[]{:S(2)}, u32[]{:S(2)}) collective-permute-start(f32[1,128,128]{2,1,0:T(8,128)S(1)} %get-tuple-element.162), channel_id=1, source_target_pairs={{0,1},{2,3},{4,5},{6,7},{8,9},{10,11},{12,13},{14,15},{16,17},{18,... | collective-permute-start | bytes 196616 | tf_op jit(solution)/shard_map/while/body/eval_jaxpr/ppermute | solution.py:23
  402.4 12.8 %collective-permute-start = (f32[10,128,128]{2,1,0:T(8,128)S(1)}, f32[10,128,128]{2,1,0:T(8,128)S(1)}, u32[]{:S(2)}, u32[]{:S(2)}) collective-permute-start(f32[10,128,128]{2,1,0:T(8,128)S(1)} %broadcast_select_fusion.3), channel_id=1, source_target_pairs={{0,2},{2,4},{4,6},{6,8},{8,10},{10,12},{12,14},{14,16},{16,18},{18... | collective-permute-start | bytes 1966088 | tf_op jit(solution)/shard_map/while/body/eval_jaxpr/ppermute | solution.py:35
  415.9 3.8 collective-permute-start.1
  417.4 6.2 %collective-permute-start.2 = (f32[1,128,128]{2,1,0:T(8,128)S(1)}, f32[1,128,128]{2,1,0:T(8,128)S(1)}, u32[]{:S(2)}, u32[]{:S(2)}) collective-permute-start(f32[1,128,128]{2,1,0:T(8,128)S(1)} %get-tuple-element.162), channel_id=1, source_target_pairs={{0,1},{2,3},{4,5},{6,7},{8,9},{10,11},{12,13},{14,15},{16,17},{18,... | collective-permute-start | bytes 196616 | tf_op jit(solution)/shard_map/while/body/eval_jaxpr/ppermute | solution.py:23
  428.1 12.8 %collective-permute-start = (f32[10,128,128]{2,1,0:T(8,128)S(1)}, f32[10,128,128]{2,1,0:T(8,128)S(1)}, u32[]{:S(2)}, u32[]{:S(2)}) collective-permute-start(f32[10,128,128]{2,1,0:T(8,128)S(1)} %broadcast_select_fusion.3), channel_id=1, source_target_pairs={{0,2},{2,4},{4,6},{6,8},{8,10},{10,12},{12,14},{14,16},{16,18},{18... | collective-permute-start | bytes 1966088 | tf_op jit(solution)/shard_map/while/body/eval_jaxpr/ppermute | solution.py:35
  441.5 3.8 collective-permute-start.1
  443.1 6.2 %collective-permute-start.2 = (f32[1,128,128]{2,1,0:T(8,128)S(1)}, f32[1,128,128]{2,1,0:T(8,128)S(1)}, u32[]{:S(2)}, u32[]{:S(2)}) collective-permute-start(f32[1,128,128]{2,1,0:T(8,128)S(1)} %get-tuple-element.162), channel_id=1, source_target_pairs={{0,1},{2,3},{4,5},{6,7},{8,9},{10,11},{12,13},{14,15},{16,17},{18,... | collective-permute-start | bytes 196616 | tf_op jit(solution)/shard_map/while/body/eval_jaxpr/ppermute | solution.py:23
  453.8 12.8 %collective-permute-start = (f32[10,128,128]{2,1,0:T(8,128)S(1)}, f32[10,128,128]{2,1,0:T(8,128)S(1)}, u32[]{:S(2)}, u32[]{:S(2)}) collective-permute-start(f32[10,128,128]{2,1,0:T(8,128)S(1)} %broadcast_select_fusion.3), channel_id=1, source_target_pairs={{0,2},{2,4},{4,6},{6,8},{8,10},{10,12},{12,14},{14,16},{16,18},{18... | collective-permute-start | bytes 1966088 | tf_op jit(solution)/shard_map/while/body/eval_jaxpr/ppermute | solution.py:35
  467.2 3.8 collective-permute-start.1
  468.8 6.2 %collective-permute-start.2 = (f32[1,128,128]{2,1,0:T(8,128)S(1)}, f32[1,128,128]{2,1,0:T(8,128)S(1)}, u32[]{:S(2)}, u32[]{:S(2)}) collective-permute-start(f32[1,128,128]{2,1,0:T(8,128)S(1)} %get-tuple-element.162), channel_id=1, source_target_pairs={{0,1},{2,3},{4,5},{6,7},{8,9},{10,11},{12,13},{14,15},{16,17},{18,... | collective-permute-start | bytes 196616 | tf_op jit(solution)/shard_map/while/body/eval_jaxpr/ppermute | solution.py:23
  479.5 12.8 %collective-permute-start = (f32[10,128,128]{2,1,0:T(8,128)S(1)}, f32[10,128,128]{2,1,0:T(8,128)S(1)}, u32[]{:S(2)}, u32[]{:S(2)}) collective-permute-start(f32[10,128,128]{2,1,0:T(8,128)S(1)} %broadcast_select_fusion.3), channel_id=1, source_target_pairs={{0,2},{2,4},{4,6},{6,8},{8,10},{10,12},{12,14},{14,16},{16,18},{18... | collective-permute-start | bytes 1966088 | tf_op jit(solution)/shard_map/while/body/eval_jaxpr/ppermute | solution.py:35
  492.9 3.8 collective-permute-start.1
  494.5 6.2 %collective-permute-start.2 = (f32[1,128,128]{2,1,0:T(8,128)S(1)}, f32[1,128,128]{2,1,0:T(8,128)S(1)}, u32[]{:S(2)}, u32[]{:S(2)}) collective-permute-start(f32[1,128,128]{2,1,0:T(8,128)S(1)} %get-tuple-element.162), channel_id=1, source_target_pairs={{0,1},{2,3},{4,5},{6,7},{8,9},{10,11},{12,13},{14,15},{16,17},{18,... | collective-permute-start | bytes 196616 | tf_op jit(solution)/shard_map/while/body/eval_jaxpr/ppermute | solution.py:23
  505.1 12.8 %collective-permute-start = (f32[10,128,128]{2,1,0:T(8,128)S(1)}, f32[10,128,128]{2,1,0:T(8,128)S(1)}, u32[]{:S(2)}, u32[]{:S(2)}) collective-permute-start(f32[10,128,128]{2,1,0:T(8,128)S(1)} %broadcast_select_fusion.3), channel_id=1, source_target_pairs={{0,2},{2,4},{4,6},{6,8},{8,10},{10,12},{12,14},{14,16},{16,18},{18... | collective-permute-start | bytes 1966088 | tf_op jit(solution)/shard_map/while/body/eval_jaxpr/ppermute | solution.py:35
  518.6 3.8 collective-permute-start.1
  520.2 6.2 %collective-permute-start.2 = (f32[1,128,128]{2,1,0:T(8,128)S(1)}, f32[1,128,128]{2,1,0:T(8,128)S(1)}, u32[]{:S(2)}, u32[]{:S(2)}) collective-permute-start(f32[1,128,128]{2,1,0:T(8,128)S(1)} %get-tuple-element.162), channel_id=1, source_target_pairs={{0,1},{2,3},{4,5},{6,7},{8,9},{10,11},{12,13},{14,15},{16,17},{18,... | collective-permute-start | bytes 196616 | tf_op jit(solution)/shard_map/while/body/eval_jaxpr/ppermute | solution.py:23
where the time goes:
time: 534 us; the launch traced here: 532 us
  waiting for transfers between devices  309 us (58%)
  other arithmetic  112 us (21%)
  starting transfers between devices  96 us (18%)
  local copies, waits for them, and re-layouts  14.2 us (3%)
    ppermute x17, waiting for transfers between devices, from_behind(): lax.ppermute(value, axis, [(source, source + steps) for source in range(f...  185 us
    ppermute x18, waiting for transfers between devices, padded_2(): lax.ppermute(tail, axis, [(i, (i + 1) % count) for i in range(ends)])  107 us
    add x16, other arithmetic, sweep_turn(): stencil(beside_all, diffusivity, pos_vel, neg_vel, COARSE_DIFF, COARSE_ADV)  54 us
    ppermute x18, starting transfers between devices, padded_2(): lax.ppermute(head, axis, [((i + 1) % count, i) for i in range(ends)])  39.9 us
    ppermute x17, starting transfers between devices, from_behind(): lax.ppermute(value, axis, [(source, source + steps) for source in range(f...  32.6 us
    select_n x9, other arithmetic, per_device(): current = jnp.where(inside[:, None, None], fresh, 0.0)  24.7 us
    ppermute x18, starting transfers between devices, padded_2(): lax.ppermute(tail, axis, [(i, (i + 1) % count) for i in range(ends)])  23.4 us
    ppermute x18, waiting for transfers between devices, padded_2(): lax.ppermute(head, axis, [((i + 1) % count, i) for i in range(ends)])  17.1 us
  transfers between devices with their start and end apart: 53, of which 51 were waited for; matrix products, arithmetic and copies ran while one was open for 1% of the time, Pallas kernels for 0%

commit v1 on v0

--- a/solution.py
+++ b/solution.py
@@ -1,15 +1,458 @@
+import functools
+import itertools
+
 import jax
 import jax.numpy as jnp
 from jax import lax
+from jax.experimental import pallas as pl
+from jax.experimental.pallas import tpu as pltpu
 from jax.sharding import PartitionSpec as P
 
 STEPS = 10
-
-
 FINE_DIFF = 0.01
 FINE_ADV = 0.012
-COARSE_DIFF = 0.1
-COARSE_ADV = 0.12
+RATIO = 10.0
+GROUP = 4
+TILE = 8
+VMEM_LIMIT = 56 * 1024 * 1024
+VMEM = pl.BlockSpec(memory_space=pltpu.VMEM)
+SMEM = pl.BlockSpec(memory_space=pltpu.SMEM)
+
+
+def rounded(count):
+    return -(-count // TILE) * TILE
+
+
+class Plan:
+    def __init__(self, shape, n_t, n_s):
+        self.n_t, self.n_s = n_t, n_s
+        self.depth, self.rows, self.lanes = shape
+        self.layers = self.depth * n_s
+        self.pairs = GROUP // 2
+        self.groups = n_t // GROUP
+        self.chunk = self.rows // (self.pairs * n_s)
+        self.halo = rounded(STEPS + n_t - 2)
+        self.width = self.width_of(self.halo)
+        self.reach = [GROUP * d - 1 for d in range(1, self.groups)]
+        self.far = rounded(self.reach[-1])
+
+    def width_of(self, halo):
+        return min(self.rows, self.chunk + 2 * rounded(halo))
+
+    def start_of(self, chip, halo):
+        return jnp.clip(chip * self.chunk - rounded(halo), 0, self.rows - self.width_of(halo))
+
+    def box(self):
+        return (self.layers + 2, self.width + 2 * TILE, self.lanes)
+
+    def locate(self):
+        self.t, self.s = lax.axis_index("tm"), lax.axis_index("space")
+        self.core = self.t % 2
+        self.y = (self.t // 2) % self.pairs
+        self.z = self.t // GROUP
+        self.chip = self.chip_at(self.y, self.s)
+        self.base = self.start_of(self.chip, self.halo)
+        places = [self.start_of(self.chip, h) - self.base for h in range(0, self.halo + 1, TILE)]
+        self.scalars = jnp.stack([self.z, self.core, self.s, self.y, *places]).astype(jnp.int32)
+
+    def chip_at(self, y, s):
+        return s * self.pairs + y
+
+    def partner(self, dy, ds):
+        return (self.y + dy) % self.pairs, (self.s + ds) % self.n_s
+
+    def send(self, value, dy=0, ds=0, dz=0, flip=False, only=None):
+        pairs = []
+        for t, s in itertools.product(range(self.n_t), range(self.n_s)):
+            core, y, z = t % 2, (t // 2) % self.pairs, t // GROUP
+            if z + dz >= self.groups or (only is not None and z != only):
+                continue
+            to_t = (z + dz) * GROUP + (y + dy) % self.pairs * 2 + (core ^ int(flip))
+            pairs.append((t * self.n_s + s, to_t * self.n_s + (s + ds) % self.n_s))
+        return lax.ppermute(value, ("tm", "space"), pairs)
+
+    def others(self):
+        return [(dy, ds) for ds in range(self.n_s) for dy in range(self.pairs) if dy or ds]
+
+
+def cut(value, start, width, axis):
+    return lax.dynamic_slice_in_dim(value, start, width, axis=axis)
+
+
+def stepper(plan, scalars, coeff):
+    def place(halo):
+        return pl.multiple_of(scalars[4 + rounded(halo) // TILE], TILE)
+
+    def step(source, target, halo, scale, plus=None, minus=None):
+        first = place(halo)
+
+        def strip(index, _):
+            row = pl.multiple_of(first + index * TILE, TILE)
+            inner = pl.ds(row, TILE)
+            here = pl.ds(pl.multiple_of(row + TILE, TILE), TILE)
+            low, mid = source[0, here, :], source[1, here, :]
+            for layer in range(plan.layers):
+                high = source[layer + 2, here, :]
+                x_low = source[layer + 1, pl.ds(row + TILE - 1, TILE), :]
+                x_high = source[layer + 1, pl.ds(row + TILE + 1, TILE), :]
+                y_low = pltpu.roll(mid, 1, 1)
+                y_high = pltpu.roll(mid, plan.lanes - 1, 1)
+                change = (coeff[0, layer, inner, :] * mid + coeff[1, layer, inner, :] * low) + (
+                    coeff[2, layer, inner, :] * high + coeff[3, layer, inner, :] * x_low
+                )
+                change = change + (coeff[4, layer, inner, :] * x_high + coeff[5, layer, inner, :] * y_low)
+                change = change + coeff[6, layer, inner, :] * y_high
+                fresh = mid + change if scale == 1.0 else mid + scale * change
+                if plus is not None:
+                    fresh = fresh + plus[layer + 1, here, :]
+                if minus is not None:
+                    fresh = fresh - minus[layer + 1, here, :]
+                target[layer + 1, here, :] = fresh
+                low, mid = mid, high
+            return 0
+
+        lax.fori_loop(0, plan.width_of(halo) // TILE, strip, 0)
+
+    return step, place
+
+
+def fine(step, source, one, two, halo, minus=None):
+    now, turn = source, (one, two)
+    for index in range(STEPS):
+        last = index == STEPS - 1
+        step(now, turn[index % 2], halo - 1 - index, 1.0, minus=minus if last else None)
+        now = turn[index % 2]
+    return now
+
+
+def clear(*fields):
+    for field in fields:
+        field[...] = jnp.zeros_like(field)
+
+
+def first_kernel(plan, count, *refs):
+    refs = list(refs)
+    scalars = refs.pop(0)
+    guess = [refs.pop(0) for _ in range(count)]
+    diff_own, vel_own = refs.pop(0), refs.pop(0)
+    near = [refs.pop(0) for _ in range(plan.n_s - 1)]
+    flipped = [refs.pop(0) for _ in range(plan.n_s - 1)]
+    init_own = refs.pop(0)
+    init_near = [refs.pop(0) for _ in range(plan.n_s - 1)]
+    init_flipped = [refs.pop(0) for _ in range(plan.n_s - 1)]
+    coeff, fields, keep, give, begun, one, two, three, four = refs
+    z, core, s, y = (scalars[i] for i in range(4))
+    half = plan.depth // 2
+    width, lanes = plan.width, plan.lanes
+
+    clear(one, two, three, four, fields)
+    for (dy, ds), piece in zip([(0, 0), *plan.others()], guess):
+        slot = lax.rem(y + plan.pairs - dy, plan.pairs)
+        slab = lax.rem(s + plan.n_s - ds, plan.n_s)
+        for layer in range(plan.depth):
+            fields[slot, 1 + slab * plan.depth + layer, TILE : TILE + width, :] = piece[layer]
+
+    lane = lax.broadcasted_iota(jnp.int32, (TILE, lanes), 1)
+
+    def weights(layer, diff, vel):
+        def strip(index, _):
+            here = pl.ds(pl.multiple_of(index * TILE, TILE), TILE)
+            spread = FINE_DIFF * diff(here)
+            drift = [FINE_ADV * vel(k, here) for k in range(3)]
+            total = 6.0 * spread
+            for k in range(3):
+                total = total + jnp.abs(drift[k])
+                below = spread + jnp.maximum(drift[k], 0.0)
+                above = spread - jnp.minimum(drift[k], 0.0)
+                if k == 2:
+                    below = jnp.where(lane == 0, 0.0, below)
+                    above = jnp.where(lane == lanes - 1, 0.0, above)
+                coeff[1 + 2 * k, layer, here, :] = below
+                coeff[2 + 2 * k, layer, here, :] = above
+            coeff[0, layer, here, :] = -total
+            return 0
+
+        lax.fori_loop(0, width // TILE, strip, 0)
+
+    def own_layer(layer, _):
+        weights(s * plan.depth + layer, lambda h: diff_own[layer, h, :], lambda k, h: vel_own[k, layer, h, :])
+        return 0
+
+    lax.fori_loop(0, plan.depth, own_layer, 0)
+    for ds in range(1, plan.n_s):
+        slab = lax.rem(s + plan.n_s - ds, plan.n_s)
+        for part, which in ((near[ds - 1], core), (flipped[ds - 1], 1 - core)):
+
+            def far_layer(layer, _, part=part, which=which, slab=slab):
+                weights(
+                    slab * plan.depth + which * half + layer,
+                    lambda h: part[0, layer, h, :],
+                    lambda k, h: part[1 + k, layer, h, :],
+                )
+                return 0
+
+            lax.fori_loop(0, half, far_layer, 0)
+
+    step, place = stepper(plan, scalars, coeff)
+    reach = STEPS + plan.n_t - 2
+    now, spare = fields.at[0], one
+    for slot in range(1, plan.pairs):
+        reach -= 1
+        step(now, two, reach, RATIO)
+        reach -= 1
+        step(two, spare, reach, RATIO, plus=fields.at[slot])
+        now, spare = spare, (three if spare is one else one)
+    free = [f for f in (one, two, three, four) if f is not now]
+    coarse = free.pop(0)
+    step(now, coarse, reach - 1, RATIO)
+    share = fine(step, now, free[0], free[1], reach, minus=coarse)
+    reach -= STEPS
+    others = [f for f in (one, two, three, four) if f is not share]
+
+    far = plan.width_of(plan.far)
+    begun[...] = jnp.zeros_like(begun)
+
+    @pl.when(z == 0)
+    def _():
+        seed = others[2]
+        for layer in range(plan.depth):
+            seed[1 + s * plan.depth + layer, :, :] = init_own[layer]
+        for ds in range(1, plan.n_s):
+            slab = lax.rem(s + plan.n_s - ds, plan.n_s)
+            for part, which in ((init_near[ds - 1], core), (init_flipped[ds - 1], 1 - core)):
+                for layer in range(half):
+                    seed[1 + slab * plan.depth + which * half + layer, :, :] = part[layer]
+        value = fine(step, seed, others[0], others[1], STEPS + plan.n_t - 1)
+        inner = pl.ds(place(plan.far) + TILE, far)
+        for layer in range(plan.layers):
+            begun[layer] = value[layer + 1, inner, :]
+
+        @pl.when(core == 0)
+        def _():
+            left = plan.n_t - 1
+            turn = [f for f in others if f is not value]
+            now = value
+            for index in range(GROUP - 1):
+                left -= 1
+                last = index == GROUP - 2
+                step(now, share if last else turn[index % 2], left, RATIO, plus=share if last else None)
+                now = turn[index % 2]
+
+    @pl.when(core == 0)
+    def _():
+        step(share, others[0], reach - 1, RATIO)
+
+    @pl.when(core != 0)
+    def _():
+        others[0][...] = share[...]
+
+    total = others[0]
+    inner = pl.ds(place(plan.far) + TILE, far)
+    side = plan.layers // 2
+    for layer in range(side):
+        keep[layer] = total[1 + core * side + layer, inner, :]
+        give[layer] = total[1 + (1 - core) * side + layer, inner, :]
+
+
+def second_kernel(plan, scalars, coeff, fields, out, one, two, three):
+    clear(one, two, three)
+    step, place = stepper(plan, scalars, coeff)
+    reach = STEPS + GROUP - 2
+    for slot in range(plan.pairs):
+        step(fields.at[slot], three, reach - 1, RATIO)
+        result = fine(step, fields.at[slot], one, two, reach, minus=three)
+        inner = pl.ds(place(TILE) + TILE, plan.width_of(TILE))
+        for layer in range(plan.layers):
+            out[slot, layer] = result[layer + 1, inner, :]
+
+
+def third_kernel(plan, *refs):
+    refs = list(refs)
+    scalars, coeff, begun = refs.pop(0), refs.pop(0), refs.pop(0)
+    steps = plan.groups - 1
+    mine = [refs.pop(0) for _ in range(steps)]
+    flipped = [refs.pop(0) for _ in range(steps)]
+    w_mine, w_flipped = refs.pop(0), refs.pop(0)
+    outs = [refs.pop(0) for _ in range(plan.pairs * plan.n_s)]
+    one, two, three = refs
+    core, s, y = scalars[1], scalars[2], scalars[3]
+    side = plan.layers // 2
+    clear(one, two, three)
+    step, place = stepper(plan, scalars, coeff)
+
+    def add_in(field, distance):
+        reach = plan.reach[distance - 1]
+        inner = pl.ds(place(reach) + TILE, plan.width_of(reach))
+        for layer in range(side):
+            for part, which in ((mine[distance - 1], core), (flipped[distance - 1], 1 - core)):
+                index = 1 + which * side + layer
+                field[index, inner, :] = field[index, inner, :] + part[layer]
+
+    now, spare = one, two
+    for distance in range(steps, 0, -1):
+        add_in(now, distance)
+        if distance > 1:
+            left = plan.reach[distance - 1]
+            for _ in range(GROUP):
+                left -= 1
+                step(now, spare, left, RATIO)
+                now, spare = spare, now
+    inner = pl.ds(place(plan.far) + TILE, plan.width_of(plan.far))
+    for layer in range(plan.layers):
+        now[layer + 1, inner, :] = now[layer + 1, inner, :] + begun[layer]
+
+    def write(block, field):
+        slot = block // 2
+        rows = pl.ds(place(0) + TILE, plan.chunk)
+
+        @pl.when(core == block % 2)
+        def _():
+            for index, (dy, ds) in enumerate([(0, 0), *plan.others()]):
+
+                @pl.when(lax.rem(y + dy, plan.pairs) == slot)
+                def _():
+                    slab = lax.rem(s + ds, plan.n_s)
+                    for layer in range(plan.depth):
+                        outs[index][layer] = field[1 + slab * plan.depth + layer, rows, :]
+
+    write(0, now)
+    band = pl.ds(place(TILE) + TILE, plan.width_of(TILE))
+    left = GROUP - 1
+    for block in range(1, GROUP):
+        left -= 1
+        parity, slot = (block - 1) % 2, (block - 1) // 2
+
+        @pl.when(core == parity)
+        def _():
+            for layer in range(plan.layers):
+                three[layer + 1, band, :] = w_mine[slot, layer]
+
+        @pl.when(core != parity)
+        def _():
+            for layer in range(plan.layers):
+                three[layer + 1, band, :] = w_flipped[slot, layer]
+
+        step(now, spare, left, RATIO, plus=three)
+        now, spare = spare, now
+        write(block, now)
+
+
+def place_kernel(plan, scalars, *refs):
+    out, pieces = refs[-1], refs[:-1]
+    s, y = scalars[2], scalars[3]
+    for (dy, ds), piece in zip([(0, 0), *plan.others()], pieces):
+        chip = lax.rem(s + plan.n_s - ds, plan.n_s) * plan.pairs + lax.rem(y + plan.pairs - dy, plan.pairs)
+        rows = pl.ds(pl.multiple_of(chip * plan.chunk, TILE), plan.chunk)
+        out[:, rows, :] = piece[...]
+
+
+def call(kernel, name, outs, scratch, *args):
+    return pl.pallas_call(
+        kernel,
+        out_shape=outs,
+        in_specs=[SMEM] + [VMEM] * (len(args) - 1),
+        out_specs=jax.tree.map(lambda _: VMEM, outs),
+        scratch_shapes=scratch,
+        compiler_params=pltpu.CompilerParams(vmem_limit_bytes=VMEM_LIMIT),
+        name=name,
+    )(*args)
+
+
+def by_regions(initial, guess, diffusivity, velocity):
+    plan = Plan(diffusivity.shape, lax.axis_size("tm"), lax.axis_size("space"))
+    plan.locate()
+    f32 = functools.partial(jax.ShapeDtypeStruct, dtype=jnp.float32)
+    depth, lanes, width, half = plan.depth, plan.lanes, plan.width, plan.depth // 2
+    state = guess[0]
+
+    def start_at(dy, ds):
+        return plan.start_of(plan.chip_at(*plan.partner(dy, ds)), plan.halo)
+
+    pieces = [cut(state, plan.base, width, 1)]
+    for dy, ds in plan.others():
+        pieces.append(plan.send(cut(state, start_at(dy, ds), width, 1), dy, ds))
+
+    near, flipped = [], []
+    init_near, init_flipped = [], []
+    padded = jnp.pad(initial, ((0, 0), (TILE, TILE), (0, 0)))
+    for ds in range(1, plan.n_s):
+        start = start_at(0, ds)
+        diff = lax.dynamic_slice(diffusivity, (plan.core * half, start, 0), (half, width, lanes))
+        vel = lax.dynamic_slice(velocity, (0, plan.core * half, start, 0), (3, half, width, lanes))
+        part = plan.send(jnp.concatenate([diff[None], vel]), ds=ds)
+        near.append(part)
+        flipped.append(plan.send(part, flip=True))
+        part = lax.dynamic_slice(padded, (plan.core * half, start, 0), (half, width + 2 * TILE, lanes))
+        part = plan.send(part, ds=ds, only=0)
+        init_near.append(part)
+        init_flipped.append(plan.send(part, flip=True, only=0))
+    init_own = cut(padded, plan.base, width + 2 * TILE, 1)
+
+    far = plan.width_of(plan.far)
+    side = plan.layers // 2
+    box = pltpu.VMEM(plan.box(), jnp.float32)
+    coeff, fields, keep, give, begun = call(
+        functools.partial(first_kernel, plan, len(pieces)),
+        "group_total",
+        [
+            f32((7, plan.layers, width, lanes)),
+            f32((plan.pairs, *plan.box())),
+            f32((side, far, lanes)),
+            f32((side, far, lanes)),
+            f32((plan.layers, far, lanes)),
+        ],
+        [box] * 4,
+        plan.scalars,
+        *pieces,
+        cut(diffusivity, plan.base, width, 1),
+        cut(velocity, plan.base, width, 2),
+        *near,
+        *flipped,
+        init_own,
+        *init_near,
+        *init_flipped,
+    )
+    total = keep + plan.send(give, flip=True)
+    far_start = plan.start_of(plan.chip, plan.far)
+    mine = []
+    for distance, reach in enumerate(plan.reach, 1):
+        part = cut(total, plan.start_of(plan.chip, reach) - far_start, plan.width_of(reach), 1)
+        mine.append(plan.send(part, dz=distance))
+    (w_mine,) = call(
+        functools.partial(second_kernel, plan),
+        "block_terms",
+        [f32((plan.pairs, plan.layers, plan.width_of(TILE), lanes))],
+        [box] * 3,
+        plan.scalars,
+        coeff,
+        fields,
+    )
+    w_flipped = plan.send(w_mine, flip=True)
+    results = call(
+        functools.partial(third_kernel, plan),
+        "block_ends",
+        [f32((depth, plan.chunk, lanes))] * (plan.pairs * plan.n_s),
+        [box] * 3,
+        plan.scalars,
+        coeff,
+        begun,
+        *mine,
+        *[plan.send(part, flip=True) for part in mine],
+        w_mine,
+        w_flipped,
+    )
+    back = [results[0]]
+    for (dy, ds), part in zip(plan.others(), results[1:]):
+        back.append(plan.send(part, dy, ds))
+    (out,) = call(
+        functools.partial(place_kernel, plan),
+        "place_rows",
+        [f32((depth, plan.rows, lanes))],
+        [],
+        plan.scalars,
+        *back,
+    )
+    return out[None]
 
 
 def padded_2(cells, sides, width):
@@ -52,7 +495,7 @@
     return center + diff_rate * diffus * laplace - adv_rate * advect
 
 
-def per_device(initial, guess, diffusivity, velocity):
+def by_slabs(initial, guess, diffusivity, velocity):
     pos_vel = jnp.maximum(velocity, 0.0)
     neg_vel = jnp.minimum(velocity, 0.0)
     depth = diffusivity.shape[0]
@@ -89,11 +532,23 @@
     def sweep_turn(index, carry):
         previous = from_behind(carry, "tm", 1)
         beside_all = padded_2(previous, (("space", 0),), 1)
-        return stencil(beside_all, diffusivity, pos_vel, neg_vel, COARSE_DIFF, COARSE_ADV) + residue
+        return stencil(beside_all, diffusivity, pos_vel, neg_vel, RATIO * FINE_DIFF, RATIO * FINE_ADV) + residue
 
     correction = lax.fori_loop(0, block_count, sweep_turn, jnp.zeros_like(state))
     state = state + correction
     return state[None]
+
+
+def fits(plan):
+    if plan.n_t % GROUP or plan.n_t < 2 * GROUP or plan.depth % 2 or plan.rows % (plan.pairs * plan.n_s * TILE):
+        return False
+    return 4 * 20 * plan.layers * plan.width * plan.lanes <= VMEM_LIMIT
+
+
+def per_device(initial, guess, diffusivity, velocity):
+    plan = Plan(diffusivity.shape, lax.axis_size("tm"), lax.axis_size("space"))
+    way = by_regions if fits(plan) else by_slabs
+    return way(initial, guess, diffusivity, velocity)
 
 
 def solution(mesh):
@@ -104,6 +559,4 @@
         P(None, "space", None, None),
     )
     out_specs = P("tm", "space", None, None)
-    return jax.shard_map(
-        per_device, mesh=mesh, in_specs=in_specs, out_specs=out_specs, check_vma=False
-    )
+    return jax.shard_map(per_device, mesh=mesh, in_specs=in_specs, out_specs=out_specs, check_vma=False)

time: 534 us -> 167 us (0.31)
  the two profiles are of different devices: /device:TPU:18 before, /device:TPU:0 now
where the time goes in v1:
time: 167 us
  Pallas kernels  79.4 us (48%)
  waiting for transfers between devices  55.7 us (33%)
  starting transfers between devices  20.7 us (12%)
  local copies, waits for them, and re-layouts  10.6 us (6%)
    pallas_call x4, Pallas kernels, call(): pl.pallas_call(kernel, out_shape=outs, in_specs=[SMEM] + [VMEM] * (len(ar...  79.4 us
    ppermute x18, waiting for transfers between devices, send(): return lax.ppermute(value, ('tm', 'space'), pairs)  55.7 us
    ppermute x18, starting transfers between devices, send(): return lax.ppermute(value, ('tm', 'space'), pairs)  20.7 us
    dynamic_slice x5, local copies, waits for them, and re-layouts, cut(): return lax.dynamic_slice_in_dim(value, start, width, axis=axis)  5.1 us
  transfers between devices with their start and end apart: 18, of which 12 were waited for; matrix products, arithmetic and copies ran while one was open for 4% of the time, Pallas kernels for 14%

profile of v1, /device:TPU:0, one launch (start us, length us, event | category | flops | bytes accessed | tf_op | source)
XLA Modules:
  0.0 166.8 jit_solution(1369956831844999904)
XLA Ops:
  0.0 0.0 copy-start
  0.0 1.1 dynamic-slice_bitcast_fusion.4
  1.1 0.5 copy-done
  1.7 0.1 constant_dynamic-slice_fusion.1
  1.7 0.1 pad_maximum_fusion
  1.8 3.0 %collective-permute-start.3 = (f32[4,5,80,128]{3,2,1,0:T(8,128)S(1)}, f32[4,5,80,128]{3,2,1,0:T(8,128)}, u32[]{:S(2)}, u32[]{:S(2)}) collective-permute-start(f32[4,5,80,128]{3,2,1,0:T(8,128)S(1)} %pad_maximum_fusion), channel_id=1, source_target_pairs={{0,1},{1,0},{2,3},{3,2},{4,5},{5,4},{6,7},{7,6},{8,9},{9,8},{10,11... | collective-permute-start | bytes 2457608 | tf_op jit(solution)/shard_map/ppermute | solution.py:72
  4.8 18.3 %collective-permute-done.3.refs_7_ = f32[4,5,80,128]{3,2,1,0:T(8,128)} collective-permute-done((f32[4,5,80,128]{3,2,1,0:T(8,128)S(1)}, f32[4,5,80,128]{3,2,1,0:T(8,128)}, u32[]{:S(2)}, u32[]{:S(2)}) %collective-permute-start.3) | collective-permute-done | bytes 819232 | tf_op jit(solution)/shard_map/ppermute | solution.py:72
  23.1 0.0 collective-permute-start.4
  23.1 0.0 copy-done.2
  23.2 0.7 pad_dynamic-slice_fusion
  23.9 3.6 %collective-permute-start.5 = (f32[5,96,128]{2,1,0:T(8,128)}, f32[5,96,128]{2,1,0:T(8,128)S(1)}, u32[]{:S(2)}, u32[]{:S(2)}) collective-permute-start(f32[5,96,128]{2,1,0:T(8,128)} %pad_dynamic-slice_fusion), channel_id=1, source_target_pairs={{0,1},{1,0},{2,3},{3,2},{4,5},{5,4},{6,7},{7,6}} | collective-permute-start | bytes 737288 | tf_op jit(solution)/shard_map/ppermute | solution.py:72
  27.6 0.0 copy-done.1
  27.6 1.2 dynamic-slice_bitcast_fusion
  28.8 1.5 collective-permute-start.2
  30.3 0.3 collective-permute-start
  30.5 1.7 %collective-permute-start.1 = (f32[10,80,128]{2,1,0:T(8,128)}, f32[10,80,128]{2,1,0:T(8,128)}, u32[]{:S(2)}, u32[]{:S(2)}) collective-permute-start(f32[10,80,128]{2,1,0:T(8,128)} %get-tuple-element.26), channel_id=1, source_target_pairs={{0,1},{1,0},{2,3},{3,2},{4,5},{5,4},{6,7},{7,6},{8,9},{9,8},{10,11... | collective-permute-start | bytes 1228808 | tf_op jit(solution)/shard_map/ppermute | solution.py:72
  32.3 0.6 stack.32.refs_0_.scalars
  32.9 0.8 pad_dynamic-slice_fusion.1.refs_9_
  33.7 1.0 collective-permute-done.5.refs_10_
  34.7 1.9 %collective-permute-start.6 = (f32[5,96,128]{2,1,0:T(8,128)S(1)}, f32[5,96,128]{2,1,0:T(8,128)S(1)}, u32[]{:S(2)}, u32[]{:S(2)}) collective-permute-start(f32[5,96,128]{2,1,0:T(8,128)S(1)} %collective-permute-done.5.refs_10_), channel_id=1, source_target_pairs={{0,2},{1,3},{2,0},{3,1},{4,6},{5,7},{6,4},{7,5}} | collective-permute-start | bytes 737288 | tf_op jit(solution)/shard_map/ppermute | solution.py:72
  36.6 1.8 %constant_dynamic-slice_fusion.3.refs_5_ = f32[10,80,128]{2,1,0:T(8,128)} fusion(f32[10,128,128]{2,1,0:T(8,128)} %param.6, s32[]{:T(128)S(6)} %min.29), kind=kLoop, calls=%fused_computation.11 | loop fusion | bytes 819204 | tf_op jit(solution)/shard_map/dynamic_slice | solution.py:79
  38.5 1.2 constant_dynamic-slice_fusion.2.refs_6_
  39.7 5.1 %collective-permute-done.2.refs_4_ = f32[10,80,128]{2,1,0:T(8,128)S(1)} collective-permute-done((f32[10,80,128]{2,1,0:T(8,128)}, f32[10,80,128]{2,1,0:T(8,128)S(1)}, u32[]{:S(2)}, u32[]{:S(2)}) %collective-permute-start.2) | collective-permute-done | bytes 409632 | tf_op jit(solution)/shard_map/ppermute | solution.py:72
  44.7 5.9 %collective-permute-done.refs_2_ = f32[10,80,128]{2,1,0:T(8,128)} collective-permute-done((f32[10,80,128]{2,1,0:T(8,128)}, f32[10,80,128]{2,1,0:T(8,128)}, u32[]{:S(2)}, u32[]{:S(2)}) %collective-permute-start) | collective-permute-done | bytes 409632 | tf_op jit(solution)/shard_map/ppermute | solution.py:72
  50.7 1.4 collective-permute-done.1.refs_3_
  52.0 0.0 collective-permute-done.6.refs_11_
  52.0 0.0 collective-permute-done.4.refs_8_
  52.1 0.0 copy-done.7
  52.1 0.0 copy-done.4
  52.1 0.7 copy-done.10
  52.8 40.2 %group_total.1 = (f32[7,20,80,128]{3,2,1,0:T(8,128)}, f32[2,22,96,128]{3,2,1,0:T(8,128)}, f32[10,64,128]{2,1,0:T(8,128)}, f32[10,64,128]{2,1,0:T(8,128)}, f32[20,64,128]{2,1,0:T(8,128)}) custom-call(s32[8]{0:T(128)} %stack.32.refs_0_.scalars, f32[10,80,128]{2,1,0:T(8,128)} %get-tuple-element.25.refs_1_, f32[10,80,128]{2,1,0:T(8,128)} %collective-permute-done.refs_2_, ...), custom_call_target="tpu_custom_call" | custom-call | tf_op jit(solution)/shard_map/group_total/pallas_call | solution.py:350
  93.0 0.0 collective-permute-start.7
  93.0 23.3 %block_terms.1.refs_9_ = f32[2,20,48,128]{3,2,1,0:T(8,128)} custom-call(s32[8]{0:T(128)} %stack.32.refs_0_.scalars, f32[7,20,80,128]{3,2,1,0:T(8,128)} %get-tuple-element.14.coeff.refs_1_, f32[2,22,96,128]{3,2,1,0:T(8,128)} %get-tuple-element.18.fields), custom_call_target="tpu_custom_call" | custom-call | tf_op jit(solution)/shard_map/block_terms/pallas_call | solution.py:350
  116.3 0.5 collective-permute-start.14
  116.8 0.0 collective-permute-done.7
  116.8 0.0 copy-done.6
  116.8 2.0 %collective-permute-start.10 = (f32[10,64,128]{2,1,0:T(8,128)S(1)}, f32[10,64,128]{2,1,0:T(8,128)}, u32[]{:S(2)}, u32[]{:S(2)}) collective-permute-start(f32[10,64,128]{2,1,0:T(8,128)S(1)} %add.91), channel_id=1, source_target_pairs={{0,24},{1,25},{2,26},{3,27},{4,28},{5,29},{6,30},{7,31}} | collective-permute-start | bytes 983048 | tf_op jit(solution)/shard_map/ppermute | solution.py:72
  118.9 1.3 collective-permute-start.9
  120.2 1.3 collective-permute-start.8
  121.5 4.7 %collective-permute-done.10.refs_5_ = f32[10,64,128]{2,1,0:T(8,128)} collective-permute-done((f32[10,64,128]{2,1,0:T(8,128)S(1)}, f32[10,64,128]{2,1,0:T(8,128)}, u32[]{:S(2)}, u32[]{:S(2)}) %collective-permute-start.10) | collective-permute-done | bytes 327712 | tf_op jit(solution)/shard_map/ppermute | solution.py:72
  126.2 0.0 collective-permute-start.13
  126.2 5.3 %collective-permute-done.9.refs_4_ = f32[10,48,128]{2,1,0:T(8,128)S(1)} collective-permute-done((f32[10,48,128]{2,1,0:T(8,128)S(1)}, f32[10,48,128]{2,1,0:T(8,128)S(1)}, u32[]{:S(2)}, u32[]{:S(2)}) %collective-permute-start.9) | collective-permute-done | bytes 245792 | tf_op jit(solution)/shard_map/ppermute | solution.py:72
  131.4 0.0 collective-permute-start.12
  131.4 4.6 %collective-permute-done.8.refs_3_ = f32[10,48,128]{2,1,0:T(8,128)S(1)} collective-permute-done((f32[10,48,128]{2,1,0:T(8,128)S(1)}, f32[10,48,128]{2,1,0:T(8,128)S(1)}, u32[]{:S(2)}, u32[]{:S(2)}) %collective-permute-start.8) | collective-permute-done | bytes 245792 | tf_op jit(solution)/shard_map/ppermute | solution.py:72
  136.1 0.0 collective-permute-start.11
  136.1 0.0 collective-permute-done.12.refs_7_
  136.1 1.5 collective-permute-done.11.refs_6_
  137.6 0.0 collective-permute-done.13.refs_8_
  137.6 0.0 collective-permute-done.14.refs_10_
  137.6 0.0 copy-start.3
  137.6 0.0 copy-done.8
  137.6 0.0 copy-done.9
  137.6 0.6 copy-done.12
  138.3 0.1 copy-done.5
  138.4 0.4 copy-done.3
  138.7 13.9 %block_ends.1 = (f32[10,32,128]{2,1,0:T(8,128)}, f32[10,32,128]{2,1,0:T(8,128)}, f32[10,32,128]{2,1,0:T(8,128)}, f32[10,32,128]{2,1,0:T(8,128)}) custom-call(s32[8]{0:T(128)} %stack.32.refs_0_.scalars, f32[7,20,80,128]{3,2,1,0:T(8,128)} %get-tuple-element.14.coeff.refs_1_, f32[20,64,128]{2,1,0:T(8,128)} %get-tuple-element.15.refs_2_, ...), custom_call_target="tpu_custom_call" | custom-call | tf_op jit(solution)/shard_map/block_ends/pallas_call | solution.py:350
  152.6 2.0 %collective-permute-start.15 = (f32[10,32,128]{2,1,0:T(8,128)}, f32[10,32,128]{2,1,0:T(8,128)S(1)}, u32[]{:S(2)}, u32[]{:S(2)}) collective-permute-start(f32[10,32,128]{2,1,0:T(8,128)} %get-tuple-element.20), channel_id=1, source_target_pairs={{0,4},{1,5},{2,6},{3,7},{4,0},{5,1},{6,2},{7,3},{8,12},{9,13},{10,... | collective-permute-start | bytes 491528 | tf_op jit(solution)/shard_map/ppermute | solution.py:72
  154.6 1.3 collective-permute-start.16
  155.9 0.2 collective-permute-start.17
  156.1 3.2 %collective-permute-done.15.refs_1_ = f32[10,32,128]{2,1,0:T(8,128)S(1)} collective-permute-done((f32[10,32,128]{2,1,0:T(8,128)}, f32[10,32,128]{2,1,0:T(8,128)S(1)}, u32[]{:S(2)}, u32[]{:S(2)}) %collective-permute-start.15) | collective-permute-done | bytes 163872 | tf_op jit(solution)/shard_map/ppermute | solution.py:72
  159.3 2.6 %collective-permute-done.16.refs_2_ = f32[10,32,128]{2,1,0:T(8,128)S(1)} collective-permute-done((f32[10,32,128]{2,1,0:T(8,128)}, f32[10,32,128]{2,1,0:T(8,128)S(1)}, u32[]{:S(2)}, u32[]{:S(2)}) %collective-permute-start.16) | collective-permute-done | bytes 163872 | tf_op jit(solution)/shard_map/ppermute | solution.py:72
  161.9 2.2 %collective-permute-done.17.refs_3_ = f32[10,32,128]{2,1,0:T(8,128)S(1)} collective-permute-done((f32[10,32,128]{2,1,0:T(8,128)}, f32[10,32,128]{2,1,0:T(8,128)S(1)}, u32[]{:S(2)}, u32[]{:S(2)}) %collective-permute-start.17) | collective-permute-done | bytes 163872 | tf_op jit(solution)/shard_map/ppermute | solution.py:72
  164.1 0.7 copy-done.15
  164.7 2.0 %place_rows.1 = f32[10,128,128]{2,1,0:T(8,128)} custom-call(s32[8]{0:T(128)} %stack.32.refs_0_.scalars, f32[10,32,128]{2,1,0:T(8,128)} %get-tuple-element.19.refs_0_, f32[10,32,128]{2,1,0:T(8,128)} %copy-done.13, f32[10,32,128]{2,1,0:T(8,128)} %copy-done.14, f32[10,32,128]{2,1,0:T(8,128)} %copy-done.15), custom_call_target="tpu_custom_call" | custom-call | tf_op jit(solution)/shard_map/place_rows/pallas_call | solution.py:350
  (19 shorter events, 0.1 us)
Async XLA Ops:
  0.0 1.7 copy-start
  0.0 23.1 %copy-start.2 = (f32[10,128,128]{2,1,0:T(8,128)S(1)}, f32[10,128,128]{2,1,0:T(8,128)}, u32[]{:S(2)}) copy-start(f32[10,128,128]{2,1,0:T(8,128)} %param.4) | copy-start | bytes 1966084
  1.7 25.9 %copy-start.1 = (f32[1,10,128,128]{3,2,1,0:T(8,128)S(1)}, f32[1,10,128,128]{3,2,1,0:T(8,128)}, u32[]{:S(2)}) copy-start(f32[1,10,128,128]{3,2,1,0:T(8,128)} %param.5) | copy-start | bytes 1966084
  1.8 21.4 %collective-permute-start.3 = (f32[4,5,80,128]{3,2,1,0:T(8,128)S(1)}, f32[4,5,80,128]{3,2,1,0:T(8,128)}, u32[]{:S(2)}, u32[]{:S(2)}) collective-permute-start(f32[4,5,80,128]{3,2,1,0:T(8,128)S(1)} %pad_maximum_fusion), channel_id=1, source_target_pairs={{0,1},{1,0},{2,3},{3,2},{4,5},{5,4},{6,7},{7,6},{8,9},{9,8},{10,11... | collective-permute-start | bytes 2457608 | tf_op jit(solution)/shard_map/ppermute | solution.py:72
  23.1 28.9 %collective-permute-start.4 = (f32[4,5,80,128]{3,2,1,0:T(8,128)}, f32[4,5,80,128]{3,2,1,0:T(8,128)}, u32[]{:S(2)}, u32[]{:S(2)}) collective-permute-start(f32[4,5,80,128]{3,2,1,0:T(8,128)} %collective-permute-done.3.refs_7_), channel_id=1, source_target_pairs={{0,2},{1,3},{2,0},{3,1},{4,6},{5,7},{6,4},{7,5},{8,10},{9,11},{10,... | collective-permute-start | bytes 2457608 | tf_op jit(solution)/shard_map/ppermute | solution.py:72
  23.9 10.8 %collective-permute-start.5 = (f32[5,96,128]{2,1,0:T(8,128)}, f32[5,96,128]{2,1,0:T(8,128)S(1)}, u32[]{:S(2)}, u32[]{:S(2)}) collective-permute-start(f32[5,96,128]{2,1,0:T(8,128)} %pad_dynamic-slice_fusion), channel_id=1, source_target_pairs={{0,1},{1,0},{2,3},{3,2},{4,5},{5,4},{6,7},{7,6}} | collective-permute-start | bytes 737288 | tf_op jit(solution)/shard_map/ppermute | solution.py:72
  28.8 15.9 %collective-permute-start.2 = (f32[10,80,128]{2,1,0:T(8,128)}, f32[10,80,128]{2,1,0:T(8,128)S(1)}, u32[]{:S(2)}, u32[]{:S(2)}) collective-permute-start(f32[10,80,128]{2,1,0:T(8,128)} %get-tuple-element.23), channel_id=1, source_target_pairs={{0,5},{1,4},{2,7},{3,6},{4,1},{5,0},{6,3},{7,2},{8,13},{9,12},{10,... | collective-permute-start | bytes 1228808 | tf_op jit(solution)/shard_map/ppermute | solution.py:72
  30.3 20.4 %collective-permute-start = (f32[10,80,128]{2,1,0:T(8,128)}, f32[10,80,128]{2,1,0:T(8,128)}, u32[]{:S(2)}, u32[]{:S(2)}) collective-permute-start(f32[10,80,128]{2,1,0:T(8,128)} %get-tuple-element.24), channel_id=1, source_target_pairs={{0,4},{1,5},{2,6},{3,7},{4,0},{5,1},{6,2},{7,3},{8,12},{9,13},{10,... | collective-permute-start | bytes 1228808 | tf_op jit(solution)/shard_map/ppermute | solution.py:72
  30.5 21.5 %collective-permute-start.1 = (f32[10,80,128]{2,1,0:T(8,128)}, f32[10,80,128]{2,1,0:T(8,128)}, u32[]{:S(2)}, u32[]{:S(2)}) collective-permute-start(f32[10,80,128]{2,1,0:T(8,128)} %get-tuple-element.26), channel_id=1, source_target_pairs={{0,1},{1,0},{2,3},{3,2},{4,5},{5,4},{6,7},{7,6},{8,9},{9,8},{10,11... | collective-permute-start | bytes 1228808 | tf_op jit(solution)/shard_map/ppermute | solution.py:72
  34.7 17.3 %copy-start.7 = (f32[5,96,128]{2,1,0:T(8,128)}, f32[5,96,128]{2,1,0:T(8,128)S(1)}, u32[]{:S(2)}) copy-start(f32[5,96,128]{2,1,0:T(8,128)S(1)} %collective-permute-done.5.refs_10_) | copy-start | bytes 737284
  34.7 17.3 %collective-permute-start.6 = (f32[5,96,128]{2,1,0:T(8,128)S(1)}, f32[5,96,128]{2,1,0:T(8,128)S(1)}, u32[]{:S(2)}, u32[]{:S(2)}) collective-permute-start(f32[5,96,128]{2,1,0:T(8,128)S(1)} %collective-permute-done.5.refs_10_), channel_id=1, source_target_pairs={{0,2},{1,3},{2,0},{3,1},{4,6},{5,7},{6,4},{7,5}} | collective-permute-start | bytes 737288 | tf_op jit(solution)/shard_map/ppermute | solution.py:72
  44.7 7.3 %copy-start.4 = (f32[10,80,128]{2,1,0:T(8,128)}, f32[10,80,128]{2,1,0:T(8,128)S(1)}, u32[]{:S(2)}) copy-start(f32[10,80,128]{2,1,0:T(8,128)S(1)} %collective-permute-done.2.refs_4_) | copy-start | bytes 1228804
  52.0 0.7 copy-start.10
  93.0 23.8 %collective-permute-start.7 = (f32[10,64,128]{2,1,0:T(8,128)}, f32[10,64,128]{2,1,0:T(8,128)S(1)}, u32[]{:S(2)}, u32[]{:S(2)}) collective-permute-start(f32[10,64,128]{2,1,0:T(8,128)} %get-tuple-element.17), channel_id=1, source_target_pairs={{0,2},{1,3},{2,0},{3,1},{4,6},{5,7},{6,4},{7,5},{8,10},{9,11},{10,... | collective-permute-start | bytes 983048 | tf_op jit(solution)/shard_map/ppermute | solution.py:72
  93.0 23.8 %copy-start.6 = (f32[10,64,128]{2,1,0:T(8,128)S(1)}, f32[10,64,128]{2,1,0:T(8,128)}, u32[]{:S(2)}) copy-start(f32[10,64,128]{2,1,0:T(8,128)} %get-tuple-element.16) | copy-start | bytes 983044
  116.3 21.3 %collective-permute-start.14 = (f32[2,20,48,128]{3,2,1,0:T(8,128)}, f32[2,20,48,128]{3,2,1,0:T(8,128)S(1)}, u32[]{:S(2)}, u32[]{:S(2)}) collective-permute-start(f32[2,20,48,128]{3,2,1,0:T(8,128)} %block_terms.1.refs_9_), channel_id=1, source_target_pairs={{0,2},{1,3},{2,0},{3,1},{4,6},{5,7},{6,4},{7,5},{8,10},{9,11},{10,... | collective-permute-start | bytes 2949128 | tf_op jit(solution)/shard_map/ppermute | solution.py:72
  116.8 9.3 %collective-permute-start.10 = (f32[10,64,128]{2,1,0:T(8,128)S(1)}, f32[10,64,128]{2,1,0:T(8,128)}, u32[]{:S(2)}, u32[]{:S(2)}) collective-permute-start(f32[10,64,128]{2,1,0:T(8,128)S(1)} %add.91), channel_id=1, source_target_pairs={{0,24},{1,25},{2,26},{3,27},{4,28},{5,29},{6,30},{7,31}} | collective-permute-start | bytes 983048 | tf_op jit(solution)/shard_map/ppermute | solution.py:72
  118.9 12.5 %collective-permute-start.9 = (f32[10,48,128]{2,1,0:T(8,128)S(1)}, f32[10,48,128]{2,1,0:T(8,128)S(1)}, u32[]{:S(2)}, u32[]{:S(2)}) collective-permute-start(f32[10,48,128]{2,1,0:T(8,128)S(1)} %constant_dynamic-slice_fusion), channel_id=1, source_target_pairs={{0,16},{1,17},{2,18},{3,19},{4,20},{5,21},{6,22},{7,23},{8,24},{9,... | collective-permute-start | bytes 737288 | tf_op jit(solution)/shard_map/ppermute | solution.py:72
  120.2 15.9 %collective-permute-start.8 = (f32[10,48,128]{2,1,0:T(8,128)S(1)}, f32[10,48,128]{2,1,0:T(8,128)S(1)}, u32[]{:S(2)}, u32[]{:S(2)}) collective-permute-start(f32[10,48,128]{2,1,0:T(8,128)S(1)} %constant_dynamic-slice_fusion), channel_id=1, source_target_pairs={{0,8},{1,9},{2,10},{3,11},{4,12},{5,13},{6,14},{7,15},{8,16},{9,17... | collective-permute-start | bytes 737288 | tf_op jit(solution)/shard_map/ppermute | solution.py:72
  126.2 11.4 %collective-permute-start.13 = (f32[10,64,128]{2,1,0:T(8,128)}, f32[10,64,128]{2,1,0:T(8,128)S(1)}, u32[]{:S(2)}, u32[]{:S(2)}) collective-permute-start(f32[10,64,128]{2,1,0:T(8,128)} %collective-permute-done.10.refs_5_), channel_id=1, source_target_pairs={{0,2},{1,3},{2,0},{3,1},{4,6},{5,7},{6,4},{7,5},{8,10},{9,11},{10,... | collective-permute-start | bytes 983048 | tf_op jit(solution)/shard_map/ppermute | solution.py:72
  131.4 6.2 %copy-start.8 = (f32[10,48,128]{2,1,0:T(8,128)}, f32[10,48,128]{2,1,0:T(8,128)S(1)}, u32[]{:S(2)}) copy-start(f32[10,48,128]{2,1,0:T(8,128)S(1)} %collective-permute-done.9.refs_4_) | copy-start | bytes 737284
  131.4 4.6 %collective-permute-start.12 = (f32[10,48,128]{2,1,0:T(8,128)S(1)}, f32[10,48,128]{2,1,0:T(8,128)S(1)}, u32[]{:S(2)}, u32[]{:S(2)}) collective-permute-start(f32[10,48,128]{2,1,0:T(8,128)S(1)} %collective-permute-done.9.refs_4_), channel_id=1, source_target_pairs={{0,2},{1,3},{2,0},{3,1},{4,6},{5,7},{6,4},{7,5},{8,10},{9,11},{10,... | collective-permute-start | bytes 737288 | tf_op jit(solution)/shard_map/ppermute | solution.py:72
  136.1 1.6 copy-start.9
  136.1 1.5 collective-permute-start.11
  136.1 1.6 copy-start.11
  137.6 0.7 copy-start.12
  137.6 0.8 copy-start.5
  137.6 1.2 copy-start.3
  152.6 6.7 %collective-permute-start.15 = (f32[10,32,128]{2,1,0:T(8,128)}, f32[10,32,128]{2,1,0:T(8,128)S(1)}, u32[]{:S(2)}, u32[]{:S(2)}) collective-permute-start(f32[10,32,128]{2,1,0:T(8,128)} %get-tuple-element.20), channel_id=1, source_target_pairs={{0,4},{1,5},{2,6},{3,7},{4,0},{5,1},{6,2},{7,3},{8,12},{9,13},{10,... | collective-permute-start | bytes 491528 | tf_op jit(solution)/shard_map/ppermute | solution.py:72
  154.6 7.3 %collective-permute-start.16 = (f32[10,32,128]{2,1,0:T(8,128)}, f32[10,32,128]{2,1,0:T(8,128)S(1)}, u32[]{:S(2)}, u32[]{:S(2)}) collective-permute-start(f32[10,32,128]{2,1,0:T(8,128)} %get-tuple-element.21), channel_id=1, source_target_pairs={{0,1},{1,0},{2,3},{3,2},{4,5},{5,4},{6,7},{7,6},{8,9},{9,8},{10,11... | collective-permute-start | bytes 491528 | tf_op jit(solution)/shard_map/ppermute | solution.py:72
  155.9 8.2 %collective-permute-start.17 = (f32[10,32,128]{2,1,0:T(8,128)}, f32[10,32,128]{2,1,0:T(8,128)S(1)}, u32[]{:S(2)}, u32[]{:S(2)}) collective-permute-start(f32[10,32,128]{2,1,0:T(8,128)} %get-tuple-element.22), channel_id=1, source_target_pairs={{0,5},{1,4},{2,7},{3,6},{4,1},{5,0},{6,3},{7,2},{8,13},{9,12},{10,... | collective-permute-start | bytes 491528 | tf_op jit(solution)/shard_map/ppermute | solution.py:72
  159.3 4.8 %copy-start.13 = (f32[10,32,128]{2,1,0:T(8,128)}, f32[10,32,128]{2,1,0:T(8,128)S(1)}, u32[]{:S(2)}) copy-start(f32[10,32,128]{2,1,0:T(8,128)S(1)} %collective-permute-done.15.refs_1_) | copy-start | bytes 491524
  161.9 2.2 %copy-start.14 = (f32[10,32,128]{2,1,0:T(8,128)}, f32[10,32,128]{2,1,0:T(8,128)S(1)}, u32[]{:S(2)}) copy-start(f32[10,32,128]{2,1,0:T(8,128)S(1)} %collective-permute-done.16.refs_2_) | copy-start | bytes 491524
  164.1 0.7 copy-start.15

commit v2 on v0

--- a/solution.py
+++ b/solution.py
@@ -1,15 +1,718 @@
+import functools
+import itertools
+import math
+
 import jax
 import jax.numpy as jnp
 from jax import lax
+from jax.experimental import pallas as pl
+from jax.experimental.pallas import tpu as pltpu
 from jax.sharding import PartitionSpec as P
 
 STEPS = 10
-
-
 FINE_DIFF = 0.01
 FINE_ADV = 0.012
-COARSE_DIFF = 0.1
-COARSE_ADV = 0.12
+RATIO = 10.0
+GROUP = 4
+TILE = 8
+LANES = 128
+SPARE_BYTES = 4 * 1024 * 1024
+VMEM_BYTES = 56 * 1024 * 1024
+VMEM = pl.BlockSpec(memory_space=pltpu.VMEM)
+HBM = pl.BlockSpec(memory_space=pltpu.HBM)
+
+
+def rounded(count):
+    return -(-count // TILE) * TILE
+
+
+class Plan:
+    def __init__(self, shape, n_t, n_s):
+        self.n_t, self.n_s = n_t, n_s
+        self.depth, self.rows, self.lanes = shape
+        self.layers = self.depth * n_s
+        self.pairs = GROUP // 2
+        self.groups = n_t // GROUP
+        self.chunk = self.rows // (self.pairs * n_s)
+        self.halo = rounded(STEPS + n_t - 2)
+        self.width = self.width_of(self.halo)
+        self.wide = min(self.rows, self.width + 2 * TILE)
+        self.reach = [GROUP * d - 1 for d in range(1, self.groups)]
+        self.far = self.reach[-1]
+        self.side = self.layers // 2
+        self.others = [(dy, ds) for ds in range(n_s) for dy in range(self.pairs) if dy or ds]
+        spans = [(y * n_s * self.chunk, (y + 1) * n_s * self.chunk) for y in range(self.pairs)]
+        self.span = max(min(self.rows, end + self.halo) - max(0, start - self.halo) for start, end in spans)
+        self.mid = STEPS + GROUP - 1
+
+    def width_of(self, halo):
+        return min(self.rows, self.chunk + 2 * rounded(halo))
+
+    def start_of(self, chip, halo):
+        start = jnp.clip(chip * self.chunk - rounded(halo), 0, self.rows - self.width_of(halo))
+        return pl.multiple_of(start, TILE)
+
+    def wide_start(self, chip):
+        start = jnp.clip(chip * self.chunk - self.halo - TILE, 0, self.rows - self.wide)
+        return pl.multiple_of(start, TILE)
+
+    def span_start(self, y):
+        start = jnp.clip(y * self.n_s * self.chunk - self.halo, 0, self.rows - self.span)
+        return pl.multiple_of(start, TILE)
+
+    def box(self):
+        return (self.layers + 2, self.width + 2 * TILE, self.lanes)
+
+    def send(self, value, dy=0, ds=0, dz=0, flip=False, swap=False, first=False):
+        pairs = []
+        for t, s in itertools.product(range(self.n_t), range(self.n_s)):
+            core, y, z = t % 2, (t // 2) % self.pairs, t // GROUP
+            to_z = z ^ 1 if swap else z + dz
+            if to_z >= self.groups or (first and (z or core)):
+                continue
+            to_t = to_z * GROUP + (y + dy) % self.pairs * 2 + (core ^ int(flip))
+            pairs.append((t * self.n_s + s, to_t * self.n_s + (s + ds) % self.n_s))
+        return lax.ppermute(value, ("tm", "space"), pairs)
+
+
+class Place:
+    def __init__(self, plan):
+        self.plan = plan
+        t = lax.axis_index("tm")
+        self.s = lax.axis_index("space")
+        self.core = lax.rem(t, 2)
+        self.y = lax.rem(lax.div(t, 2), plan.pairs)
+        self.z = lax.div(t, GROUP)
+        self.chip = self.y * plan.n_s + self.s
+        self.base = plan.start_of(self.chip, plan.halo)
+
+    def ahead(self, dy, ds):
+        plan = self.plan
+        return lax.rem(self.y + dy, plan.pairs) * plan.n_s + lax.rem(self.s + ds, plan.n_s)
+
+    def behind(self, dy, ds):
+        plan = self.plan
+        return lax.rem(self.y + plan.pairs - dy, plan.pairs), lax.rem(self.s + plan.n_s - ds, plan.n_s)
+
+    def inner(self, halo):
+        return pl.multiple_of(self.plan.start_of(self.chip, halo) - self.base, TILE)
+
+
+def fetch(sem, copies):
+    started = [pltpu.make_async_copy(source, target, sem.at[index]) for index, (source, target) in enumerate(copies)]
+    for copy in started:
+        copy.start()
+    return started
+
+
+def shifts(lanes):
+    row = lax.broadcasted_iota(jnp.int32, (2 * lanes, 2 * lanes), 0)
+    row = jnp.where(row >= lanes, row - lanes, row)
+    column = lax.broadcasted_iota(jnp.int32, (2 * lanes, 2 * lanes), 1)
+    up = jnp.where(row == column - 1, 1.0, 0.0)
+    down = jnp.where(row == column - lanes + 1, 1.0, 0.0)
+    return jnp.where(column < lanes, up, down).astype(jnp.bfloat16)
+
+
+def with_shifts(plan, body):
+    count = plan.layers // 2
+
+    def run(*sums):
+        matrix = shifts(plan.lanes)
+        for unit in range(2):
+            pltpu.matmul_push_rhs(matrix, 0, unit)
+            pltpu.matmul_acc_lhs(sums[unit], jnp.zeros((2 * TILE, 2 * plan.lanes), jnp.bfloat16), load_staged_rhs=0)
+            pltpu.matmul_pop(sums[unit])
+        body((sums[:count], sums[count:]))
+
+    pl.run_scoped(
+        run,
+        *[pltpu.ACC(i % count % 2)((2 * TILE, 2 * plan.lanes), jnp.float32) for i in range(2 * count)],
+    )
+
+
+def stepper(plan, place, coeff, sums):
+    count = plan.layers // 2
+
+    def step(source, target, halo, scale, plus=None, minus=None):
+        first = place.inner(halo)
+        strips = plan.width_of(halo) // TILE
+
+        def rows(index):
+            return pl.multiple_of(first + index * TILE, TILE)
+
+        def shift(index, which, pair):
+            here = pl.ds(pl.multiple_of(rows(index) + TILE, TILE), TILE)
+            value = source[pl.ds(1 + 2 * pair, 2), here, :].reshape(2 * TILE, plan.lanes)
+            high = value.astype(jnp.bfloat16)
+            rest = (value - high.astype(jnp.float32)).astype(jnp.bfloat16)
+            pltpu.matmul_acc_lhs(sums[which][pair], jnp.concatenate([high, rest], axis=1))
+
+        def strip(index, which, later):
+            row = rows(index)
+            inner = pl.ds(row, TILE)
+            here = pl.ds(pl.multiple_of(row + TILE, TILE), TILE)
+            low, mid = source[0, here, :], source[1, here, :]
+            for layer in range(plan.layers):
+                if layer % 2 == 0:
+                    shift(later, 1 - which, layer // 2)
+                    moved = pltpu.matmul_pop(sums[which][layer // 2])
+                part = moved[layer % 2 * TILE : (layer % 2 + 1) * TILE]
+                high = source[layer + 2, here, :]
+                x_low = source[layer + 1, pl.ds(row + TILE - 1, TILE), :]
+                x_high = source[layer + 1, pl.ds(row + TILE + 1, TILE), :]
+                change = (coeff[0, layer, inner, :] * mid + coeff[1, layer, inner, :] * low) + (
+                    coeff[2, layer, inner, :] * high + coeff[3, layer, inner, :] * x_low
+                )
+                change = change + (coeff[4, layer, inner, :] * x_high + coeff[5, layer, inner, :] * part[:, : plan.lanes])
+                change = change + coeff[6, layer, inner, :] * part[:, plan.lanes :]
+                fresh = mid + change if scale == 1.0 else mid + scale * change
+                if plus is not None:
+                    fresh = fresh + plus(layer, row)
+                if minus is not None:
+                    fresh = fresh - minus(layer, row)
+                target[layer + 1, here, :] = fresh
+                low, mid = mid, high
+
+        for pair in range(count):
+            shift(0, 0, pair)
+
+        def two(index, _):
+            strip(2 * index, 0, jnp.minimum(2 * index + 1, strips - 1))
+            strip(jnp.minimum(2 * index + 1, strips - 1), 1, jnp.minimum(2 * index + 2, strips - 1))
+            return 0
+
+        lax.fori_loop(0, -(-strips // 2), two, 0)
+        for pair in range(count):
+            pltpu.matmul_pop(sums[0][pair])
+
+    return step
+
+
+def field_at(field):
+    return lambda layer, row: field[layer + 1, pl.ds(pl.multiple_of(row + TILE, TILE), TILE), :]
+
+
+def fine(step, source, one, two, halo, minus=None):
+    now, turn = source, (one, two)
+    for index in range(STEPS):
+        last = index == STEPS - 1
+        step(now, turn[index % 2], halo - 1 - index, 1.0, minus=minus if last else None)
+        now = turn[index % 2]
+    return now
+
+
+def clear(plan, *fields):
+    for field in fields:
+        edge = jnp.zeros((TILE, plan.lanes), jnp.float32)
+        for layer in range(plan.layers + 2):
+            field[layer, :TILE, :] = edge
+            field[layer, TILE + plan.width :, :] = edge
+        for layer in (0, plan.layers + 1):
+            field[layer] = jnp.zeros_like(field[layer])
+
+
+def first_cut_kernel(plan, guess, diff, vel, *refs):
+    place = Place(plan)
+    sem = refs[-1]
+    coeffs, blocks = refs[: plan.n_s - 1], refs[plan.n_s - 1 : -1]
+    which = place.core * 2 + lax.rem(place.z, 2)
+
+    def source(ds, array):
+        rows = pl.ds(plan.start_of(place.ahead(0, ds), plan.halo), plan.width)
+        return diff.at[:, rows, :] if array is None else vel.at[array, :, rows, :]
+
+    for ds, target in enumerate(coeffs, 1):
+
+        @pl.when(which == 0)
+        def _(ds=ds, target=target):
+            pltpu.make_async_copy(source(ds, None), target, sem.at[ds - 1]).start()
+
+        @pl.when(which > 0)
+        def _(ds=ds, target=target):
+            pltpu.make_async_copy(source(ds, jnp.maximum(which - 1, 0)), target, sem.at[ds - 1]).start()
+
+    copies = []
+    for dy, target in enumerate(blocks, 1):
+        start = plan.span_start(lax.rem(place.y + dy, plan.pairs))
+        copies.append(pltpu.make_async_copy(guess.at[0, :, pl.ds(start, plan.span), :], target, sem.at[plan.n_s - 2 + dy]))
+    for copy in copies:
+        copy.start()
+    for ds, target in enumerate(coeffs, 1):
+        pltpu.make_async_copy(source(ds, None), target, sem.at[ds - 1]).wait()
+    for copy in copies:
+        copy.wait()
+
+
+def second_cut_kernel(plan, guess, initial, diff, vel, *refs):
+    place = Place(plan)
+    refs, sem = refs[:-1], refs[-1]
+    count = plan.n_s - 1
+    blocks, inits = refs[:count], refs[count : 2 * count]
+    guess_own, initial_own, coeff_own = refs[2 * count :]
+    copies = []
+    for ds, target in enumerate(blocks, 1):
+        start = plan.start_of(place.ahead(0, ds), plan.halo)
+        copies.append((guess.at[0, :, pl.ds(start, plan.width), :], target))
+    for ds, target in enumerate(inits, 1):
+        start = plan.wide_start(place.ahead(0, ds))
+        copies.append((initial.at[:, pl.ds(start, plan.wide), :], target))
+    rows = pl.ds(place.base, plan.width)
+    copies.append((guess.at[0, :, rows, :], guess_own))
+    copies.append((initial.at[:, pl.ds(plan.wide_start(place.chip), plan.wide), :], initial_own))
+    copies.append((diff.at[:, rows, :], coeff_own.at[0]))
+    copies.append((vel.at[:, :, rows, :], coeff_own.at[pl.ds(1, 3)]))
+    for copy in fetch(sem, copies):
+        copy.wait()
+
+
+def mix_kernel(plan, *refs):
+    place = Place(plan)
+    count = plan.n_s - 1
+    own, others, outs = refs[:count], refs[count:-count], refs[-count:]
+    for ds, (block, out) in enumerate(zip(own, outs), 1):
+        out[0] = block[...]
+        start = plan.start_of(place.ahead(0, ds), plan.halo) - plan.span_start(place.y)
+        for slot, other in enumerate(others, 1):
+            out[slot] = other[:, pl.ds(pl.multiple_of(start, TILE), plan.width), :]
+
+
+def field_kernel(plan, own, *refs):
+    place = Place(plan)
+    beside, far = refs[: plan.pairs - 1], refs[plan.pairs - 1 : -2]
+    fields, given = refs[-2:]
+    clear(plan, *[fields.at[slot] for slot in range(plan.pairs)])
+    rows = pl.ds(TILE, plan.width)
+    given_rows = pl.ds(place.inner(plan.mid), plan.width_of(plan.mid))
+
+    def take(dy, ds, read):
+        slot, slab = place.behind(dy, ds)
+
+        def layer(index, _):
+            value = read(index)
+            fields[slot, 1 + slab * plan.depth + index, rows, :] = value
+            return 0
+
+        lax.fori_loop(0, plan.depth, layer, 0)
+
+    take(0, 0, lambda index: own[index])
+    start = pl.multiple_of(place.base - plan.span_start(place.y), TILE)
+    for dy, block in enumerate(beside, 1):
+        take(dy, 0, lambda index, block=block: block[index, pl.ds(start, plan.width), :])
+    for ds, blocks in enumerate(far, 1):
+        for dy in range(plan.pairs):
+            take(dy, ds, lambda index, blocks=blocks, dy=dy: blocks[dy, index])
+    for slot in range(plan.pairs):
+        for layer in range(plan.layers):
+            given[slot, layer] = fields[slot, 1 + layer, pl.ds(pl.multiple_of(given_rows.start + TILE, TILE), given_rows.size), :]
+
+
+def weight_kernel(plan, coeff_own, window, *refs):
+    refs = list(refs)
+    near, init_near = [], []
+    for _ in range(plan.n_s - 1):
+        near.append(refs[:4])
+        init_near.append(refs[4])
+        del refs[:5]
+    coeff, seed, ahead, parts, one = refs
+    place = Place(plan)
+    z, core, s = place.z, place.core, place.s
+    even = lax.rem(z, 2)
+    for ds, (mine, swapped, flipped, both) in enumerate(near, 1):
+        for ref, array in (
+            (mine, 2 * core + even),
+            (swapped, 2 * core + 1 - even),
+            (flipped, 2 * (1 - core) + even),
+            (both, 2 * (1 - core) + 1 - even),
+        ):
+            parts[ds - 1, array] = ref[...]
+    lane = lax.broadcasted_iota(jnp.int32, (plan.width, plan.lanes), 1)
+    for ds in range(plan.n_s):
+        slab = place.behind(0, ds)[1]
+
+        def layer_weights(layer, _, ds=ds, slab=slab):
+            index = slab * plan.depth + layer
+            held = parts.at[ds - 1] if ds else coeff_own
+            spread = FINE_DIFF * held[0, layer]
+            total = 6.0 * spread
+            for k in range(3):
+                drift = FINE_ADV * held[1 + k, layer]
+                total = total + jnp.abs(drift)
+                below = spread + jnp.maximum(drift, 0.0)
+                above = spread - jnp.minimum(drift, 0.0)
+                if k == 2:
+                    below = jnp.where(lane == 0, 0.0, below)
+                    above = jnp.where(lane == plan.lanes - 1, 0.0, above)
+                coeff[1 + 2 * k, index] = below
+                coeff[2 + 2 * k, index] = above
+            coeff[0, index] = -total
+            return 0
+
+        lax.fori_loop(0, plan.depth, layer_weights, 0)
+
+    @pl.when((z == 0) & (core == 0))
+    def _():
+        seed[...] = jnp.zeros_like(seed)
+        offset = lax.div(place.base - plan.wide_start(place.chip), TILE) - 1
+
+        def fill(target_layer, source):
+            for index in range(plan.width // TILE + 2):
+                strip = index + offset
+                inside = (strip >= 0) & (strip < plan.wide // TILE)
+                held = pl.ds(pl.multiple_of(jnp.clip(strip, 0, plan.wide // TILE - 1) * TILE, TILE), TILE)
+                value = jnp.where(inside, source[held, :], 0.0)
+                seed[target_layer, index * TILE : (index + 1) * TILE, :] = value
+
+        for ds in range(plan.n_s):
+            slab = place.behind(0, ds)[1]
+            held = init_near[ds - 1] if ds else window
+
+            def take(layer, _, held=held, slab=slab):
+                fill(1 + slab * plan.depth + layer, held.at[layer])
+                return 0
+
+            lax.fori_loop(0, plan.depth, take, 0)
+
+        def body(sums):
+            step = stepper(plan, place, coeff, sums)
+            clear(plan, ahead, one)
+            now, turn, reach = seed, (ahead, one), STEPS + plan.n_t - 1
+            for index in range(GROUP - 1):
+                reach -= 1
+                step(now, turn[index % 2], reach, RATIO)
+                now = turn[index % 2]
+            if now is one:
+                ahead[...] = one[...]
+
+        with_shifts(plan, body)
+
+
+def total_kernel(plan, coeff, ahead, fields, keep, give, one, two, three):
+    place = Place(plan)
+    z, core = place.z, place.core
+    clear(plan, one, two, three)
+
+    def body(sums):
+        step = stepper(plan, place, coeff, sums)
+        reach = STEPS + plan.n_t - 2
+        now = fields.at[0]
+        for slot in range(1, plan.pairs):
+            reach -= 1
+            step(now, two, reach, RATIO)
+            now, spare = two, (one if slot % 2 else three)
+            reach -= 1
+            step(now, spare, reach, RATIO, plus=field_at(fields.at[slot]))
+            now = spare
+        free = [f for f in (one, two, three) if f is not now]
+        coarse = free.pop()
+        step(now, coarse, reach - 1, RATIO)
+
+        @pl.when((z == 0) & (core == 0))
+        def _():
+            for layer in range(1, plan.layers + 1):
+                now[layer] = now[layer] + ahead[layer]
+
+        share = fine(step, now, free[0], now, reach, minus=field_at(coarse))
+        reach -= STEPS
+        total = free[0]
+
+        @pl.when(core == 0)
+        def _():
+            step(share, total, reach - 1, RATIO)
+
+        @pl.when(core != 0)
+        def _():
+            for layer in range(1, plan.layers + 1):
+                total[layer] = share[layer]
+
+        inner = pl.ds(pl.multiple_of(place.inner(plan.far) + TILE, TILE), plan.width_of(plan.far))
+        for layer in range(plan.side):
+            keep[layer] = total[1 + core * plan.side + layer, inner, :]
+            give[layer] = total[1 + (1 - core) * plan.side + layer, inner, :]
+
+    with_shifts(plan, body)
+
+
+def part_kernel(plan, keep, got, *outs):
+    place = Place(plan)
+    for reach, out in zip(plan.reach, outs):
+        start = pl.multiple_of(place.inner(reach) - place.inner(plan.far), TILE)
+        rows = pl.ds(start, plan.width_of(reach))
+        for layer in range(plan.side):
+            out[layer] = keep[layer, rows, :] + got[layer, rows, :]
+
+
+def term_kernel(plan, coeff, fields, flipped, seed, terms, begun, one, two, three):
+    place = Place(plan)
+    core = place.core
+    clear(plan, one, two, three)
+    middle = pl.ds(pl.multiple_of(place.inner(plan.mid) + TILE, TILE), plan.width_of(plan.mid))
+
+    def body(sums):
+        step = stepper(plan, place, coeff, sums)
+
+        def term(source, coarse, other, reach, out, halo):
+            step(source, coarse, reach - 1, RATIO)
+            result = fine(step, source, other, source, reach, minus=field_at(coarse))
+            rows = pl.ds(pl.multiple_of(place.inner(halo) + TILE, TILE), plan.width_of(halo))
+            for layer in range(plan.layers):
+                out[layer] = result[layer + 1, rows, :]
+
+        def load(block, target):
+            @pl.when(core == block % 2)
+            def _():
+                target[...] = fields[block // 2]
+
+            @pl.when(core != block % 2)
+            def _():
+                for layer in range(plan.layers):
+                    target[layer + 1, middle, :] = flipped[block // 2, layer]
+
+        def block_term(block):
+            load(0, one)
+            left = STEPS + block - 1
+            now, spare = one, two
+            for before in range(1, block):
+                load(before, three)
+                left -= 1
+                step(now, spare, left, RATIO, plus=field_at(three))
+                now, spare = spare, now
+            term(now, three, spare, left, terms.at[block // 2], 0)
+
+        for block in range(GROUP):
+
+            @pl.when(core == block % 2)
+            def _(block=block):
+                if block == 0:
+                    terms[0] = jnp.zeros_like(terms[0])
+                else:
+                    block_term(block)
+
+        started = (place.z == 0) & (core == 0)
+
+        @pl.when(started)
+        def _():
+            one[...] = seed[...]
+            result = fine(step, one, two, one, STEPS + GROUP - 1)
+            rows = pl.ds(pl.multiple_of(place.inner(TILE) + TILE, TILE), plan.width_of(TILE))
+            for layer in range(plan.layers):
+                begun[layer] = result[layer + 1, rows, :]
+
+        @pl.when(jnp.logical_not(started))
+        def _():
+            begun[...] = jnp.zeros_like(begun)
+
+    with_shifts(plan, body)
+
+
+def start_kernel(plan, coeff, begun, *refs):
+    *totals, out, one, two = refs
+    place = Place(plan)
+    clear(plan, one, two)
+
+    def body(sums):
+        step = stepper(plan, place, coeff, sums)
+        now, spare = one, two
+        now[...] = jnp.zeros_like(now)
+        for distance in range(len(totals), 0, -1):
+
+            @pl.when(place.z >= distance)
+            def _(distance=distance):
+                reach = plan.reach[distance - 1]
+                rows = pl.ds(pl.multiple_of(place.inner(reach) + TILE, TILE), plan.width_of(reach))
+                for layer in range(plan.side):
+                    index = 1 + place.core * plan.side + layer
+                    now[index, rows, :] = now[index, rows, :] + totals[distance - 1][layer]
+                if distance > 1:
+                    for turn in range(GROUP):
+                        source, target = (now, spare) if turn % 2 == 0 else (spare, now)
+                        step(source, target, reach - 1 - turn, RATIO)
+
+        rows = pl.ds(pl.multiple_of(place.inner(TILE) + TILE, TILE), plan.width_of(TILE))
+        for layer in range(plan.layers):
+            out[layer] = now[layer + 1, rows, :] + begun[layer]
+
+    with_shifts(plan, body)
+
+
+def end_kernel(plan, coeff, share, other, terms, *refs):
+    *outs, one, two = refs
+    place = Place(plan)
+    core, s, y = place.core, place.s, place.y
+    clear(plan, one, two)
+    chunk = pl.ds(pl.multiple_of(place.inner(0) + TILE, TILE), plan.chunk)
+    rows = pl.ds(pl.multiple_of(place.inner(TILE) + TILE, TILE), plan.width_of(TILE))
+    for layer in range(plan.layers):
+        one[layer + 1, rows, :] = share[layer] + other[layer]
+
+    def write(block, field):
+        @pl.when(core == block % 2)
+        def _():
+            for out, (dy, ds) in zip(outs, [(0, 0), *plan.others]):
+
+                @pl.when(lax.rem(y + dy, plan.pairs) == block // 2)
+                def _(out=out, ds=ds):
+                    slab = lax.rem(s + ds, plan.n_s)
+                    for layer in range(plan.depth):
+                        value = field[1 + slab * plan.depth + layer, chunk, :]
+                        out[layer] = value + terms[block // 2, slab * plan.depth + layer] if block else value
+
+    def body(sums):
+        step = stepper(plan, place, coeff, sums)
+        now, spare = one, two
+        write(0, now)
+        for block in range(1, GROUP):
+            step(now, spare, GROUP - 1 - block, RATIO)
+            now, spare = spare, now
+            write(block, now)
+
+    with_shifts(plan, body)
+
+
+def place_kernel(plan, *refs):
+    place = Place(plan)
+    out, sem, pieces = refs[-2], refs[-1], refs[:-2]
+    copies = []
+    for (dy, ds), piece in zip([(0, 0), *plan.others], pieces):
+        y, s = place.behind(dy, ds)
+        rows = pl.ds(pl.multiple_of((y * plan.n_s + s) * plan.chunk, TILE), plan.chunk)
+        copies.append((piece, out.at[:, rows, :]))
+    for copy in fetch(sem, copies):
+        copy.wait()
+
+
+def call(plan, kernel, micros, outs, scratch, *args, copies=0, whole=0, out_whole=False):
+    spaces = [pltpu.HBM] * whole + [pltpu.VMEM] * (len(args) - whole)
+    args = [pltpu.with_memory_space_constraint(arg, space) for arg, space in zip(args, spaces)]
+    held = pltpu.HBM if out_whole else pltpu.VMEM
+    needed = sum(4 * math.prod(shape) for shape in scratch)
+    return pl.pallas_call(
+        functools.partial(kernel, plan),
+        out_shape=[held(shape, jnp.float32) for shape in outs],
+        in_specs=[HBM] * whole + [VMEM] * (len(args) - whole),
+        out_specs=[HBM if out_whole else VMEM] * len(outs),
+        scratch_shapes=[pltpu.VMEM(shape, jnp.float32) for shape in scratch]
+        + ([pltpu.SemaphoreType.DMA((copies,))] if copies else []),
+        compiler_params=pltpu.CompilerParams(vmem_limit_bytes=needed + SPARE_BYTES),
+        cost_estimate=pl.CostEstimate(flops=0, transcendentals=0, bytes_accessed=int(micros * 3.6e6)),
+        name=kernel.__name__,
+    )(*args)
+
+
+def by_regions(initial, guess, diffusivity, velocity):
+    plan = Plan(diffusivity.shape, lax.axis_size("tm"), lax.axis_size("space"))
+    depth, lanes, width = plan.depth, plan.lanes, plan.width
+    box, sides = plan.box(), plan.n_s - 1
+    band, far = plan.width_of(TILE), plan.width_of(plan.far)
+    window, piece = (depth, plan.wide, lanes), (depth, width, lanes)
+
+    cuts = call(
+        plan,
+        first_cut_kernel,
+        2,
+        [piece] * sides + [(depth, plan.span, lanes)] * (plan.pairs - 1),
+        [],
+        guess,
+        diffusivity,
+        velocity,
+        copies=sides + plan.pairs - 1,
+        whole=3,
+    )
+    got = [plan.send(part, ds=ds) for ds, part in enumerate(cuts[:sides], 1)]
+    got += [plan.send(part, dy=dy) for dy, part in enumerate(cuts[sides:], 1)]
+    cuts = call(
+        plan,
+        second_cut_kernel,
+        2,
+        [piece] * sides + [window] * sides + [piece, window, (4, *piece)],
+        [],
+        guess,
+        initial,
+        diffusivity,
+        velocity,
+        copies=2 * sides + 4,
+        whole=4,
+    )
+    own_sent, inits, (guess_own, initial_own, coeff_own) = cuts[:sides], cuts[sides : 2 * sides], cuts[2 * sides :]
+    got = lax.optimization_barrier(got)
+    coeffs, beside = got[:sides], got[sides:]
+    mixed = call(plan, mix_kernel, 0.3, [(plan.pairs, *piece)] * sides, [], *own_sent, *beside)
+    distant = [plan.send(part, ds=ds) for ds, part in enumerate(mixed, 1)]
+    inits = [plan.send(init, ds=ds, first=True) for ds, init in enumerate(inits, 1)]
+    swapped = []
+    for part in coeffs:
+        swapped.append(plan.send(part, swap=True))
+        swapped.append(plan.send(part, flip=True))
+        swapped.append(plan.send(part, swap=True, flip=True))
+    got = lax.optimization_barrier((*distant, *swapped, *inits))
+    distant, swapped, inits = got[:sides], got[sides : 4 * sides], got[4 * sides :]
+    near = []
+    for index, (part, init) in enumerate(zip(coeffs, inits)):
+        near += [part, *swapped[3 * index : 3 * index + 3], init]
+
+    coeff, seed, ahead = call(
+        plan,
+        weight_kernel,
+        3,
+        [(7, plan.layers, width, lanes), box, box],
+        [(sides, 4, *piece), box],
+        coeff_own,
+        initial_own,
+        *near,
+    )
+    fields, given = call(
+        plan,
+        field_kernel,
+        0.5,
+        [(plan.pairs, *box), (plan.pairs, plan.layers, plan.width_of(plan.mid), lanes)],
+        [],
+        guess_own,
+        *beside,
+        *distant,
+    )
+    keep, give = call(
+        plan, total_kernel, 15, [(plan.side, far, lanes), (plan.side, far, lanes)], [box] * 3, coeff, ahead, fields
+    )
+    parts = call(
+        plan,
+        part_kernel,
+        0.3,
+        [(plan.side, plan.width_of(reach), lanes) for reach in plan.reach],
+        [],
+        keep,
+        plan.send(give, flip=True),
+    )
+    mine = [plan.send(part, dz=distance) for distance, part in enumerate(parts, 1)]
+    terms, begun = call(
+        plan,
+        term_kernel,
+        15,
+        [(plan.pairs, plan.layers, plan.chunk, lanes), (plan.layers, band, lanes)],
+        [box] * 3,
+        coeff,
+        fields,
+        plan.send(given, flip=True),
+        seed,
+    )
+    (share,) = call(plan, start_kernel, 6, [(plan.layers, band, lanes)], [box] * 2, coeff, begun, *mine)
+    results = call(
+        plan,
+        end_kernel,
+        3,
+        [(depth, plan.chunk, lanes)] * (1 + len(plan.others)),
+        [box] * 2,
+        coeff,
+        share,
+        plan.send(share, flip=True),
+        terms,
+    )
+    back = [results[0]]
+    for (dy, ds), part in zip(plan.others, results[1:]):
+        back.append(plan.send(part, dy, ds))
+    (out,) = call(
+        plan, place_kernel, 1, [(depth, plan.rows, lanes)], [], *back, copies=len(back), out_whole=True
+    )
+    return out[None]
 
 
 def padded_2(cells, sides, width):
@@ -52,7 +755,7 @@
     return center + diff_rate * diffus * laplace - adv_rate * advect
 
 
-def per_device(initial, guess, diffusivity, velocity):
+def by_slabs(initial, guess, diffusivity, velocity):
     pos_vel = jnp.maximum(velocity, 0.0)
     neg_vel = jnp.minimum(velocity, 0.0)
     depth = diffusivity.shape[0]
@@ -89,11 +792,23 @@
     def sweep_turn(index, carry):
         previous = from_behind(carry, "tm", 1)
         beside_all = padded_2(previous, (("space", 0),), 1)
-        return stencil(beside_all, diffusivity, pos_vel, neg_vel, COARSE_DIFF, COARSE_ADV) + residue
+        return stencil(beside_all, diffusivity, pos_vel, neg_vel, RATIO * FINE_DIFF, RATIO * FINE_ADV) + residue
 
     correction = lax.fori_loop(0, block_count, sweep_turn, jnp.zeros_like(state))
     state = state + correction
     return state[None]
+
+
+def fits(plan):
+    if plan.n_t % (2 * GROUP) or plan.layers % 2 or plan.rows % (plan.pairs * plan.n_s * TILE) or plan.lanes != LANES:
+        return False
+    return plan.n_s > 1 and 4 * 24 * plan.layers * plan.width * plan.lanes <= VMEM_BYTES
+
+
+def per_device(initial, guess, diffusivity, velocity):
+    shape, n_t, n_s = diffusivity.shape, lax.axis_size("tm"), lax.axis_size("space")
+    way = by_regions if n_t > GROUP and fits(Plan(shape, n_t, n_s)) else by_slabs
+    return way(initial, guess, diffusivity, velocity)
 
 
 def solution(mesh):
@@ -104,6 +819,4 @@
         P(None, "space", None, None),
     )
     out_specs = P("tm", "space", None, None)
-    return jax.shard_map(
-        per_device, mesh=mesh, in_specs=in_specs, out_specs=out_specs, check_vma=False
-    )
+    return jax.shard_map(per_device, mesh=mesh, in_specs=in_specs, out_specs=out_specs, check_vma=False)

time: 534 us -> 99.4 us (0.19)
  waiting for transfers between devices: 309 us -> 50.3 us
  other arithmetic: 112 us -> 0 us
  starting transfers between devices: 96 us -> 16.2 us
  Pallas kernels: 0 us -> 31.5 us
  local copies, waits for them, and re-layouts: 14.2 us -> 0 us
    ppermute x53 -> x16, waiting for transfers between devices: 309 us -> 50.3 us  [send(): return lax.ppermute(value, ('tm', 'space'), pairs)]
    ppermute x53 -> x16, starting transfers between devices: 96 us -> 16.2 us  [send(): return lax.ppermute(value, ('tm', 'space'), pairs)]
    add x16 -> x0, other arithmetic: 54 us -> none  [sweep_turn(): stencil(beside_all, diffusivity, pos_vel, neg_vel, COARSE_DIFF, COARSE_ADV)]
    pallas_call x0 -> x11, Pallas kernels: none -> 31.5 us  [call(): pl.pallas_call(functools.partial(kernel, plan), out_shape=[held(shape, jn...]
    select_n x10 -> x0, other arithmetic: 25.9 us -> none  [the longest x9 24.7 us: per_device(): current = jnp.where(inside[:, None, None], fresh, 0.0)]
    while x16 -> x0, other arithmetic: 17 us -> none
    slice x26 -> x0, local copies, waits for them, and re-layouts: 12.4 us -> none  [the longest x16 10.2 us: padded_2(): lax.slice_in_dim(cells, cells.shape[dim] - width, cells.shape[dim], axis=...]
    concatenate x3 -> x0, other arithmetic: 6.75 us -> none  [the longest x1 3.59 us: per_device(): stacked = jnp.concatenate([diffusivity[None], velocity], axis=0)]
  transfers between devices with their start and end apart: 53 -> 16, of which waited for: 51 -> 10; matrix products, arithmetic and copies ran while one was open for 1% -> 0% of each run, Pallas kernels for 0% -> 25%
where the time goes in v2:
time: 99.4 us; the launch traced here: 98.3 us
  waiting for transfers between devices  50.3 us (51%)
  Pallas kernels  31.5 us (32%)
  starting transfers between devices  16.2 us (16%)
    ppermute x16, waiting for transfers between devices, send(): return lax.ppermute(value, ('tm', 'space'), pairs)  50.3 us
    pallas_call x11, Pallas kernels, call(): pl.pallas_call(functools.partial(kernel, plan), out_shape=[held(shape, jn...  31.5 us
    ppermute x16, starting transfers between devices, send(): return lax.ppermute(value, ('tm', 'space'), pairs)  16.2 us
  transfers between devices with their start and end apart: 16, of which 10 were waited for; matrix products, arithmetic and copies ran while one was open for 0% of the time, Pallas kernels for 25%

profile of v2, /device:TPU:18, one launch (start us, length us, event | category | flops | bytes accessed | tf_op | source)
XLA Modules:
  0.0 98.3 jit_solution(16889163644124789991)
XLA Ops:
  0.0 1.2 %first_cut_kernel.1 = (f32[10,80,128]{2,1,0:T(8,128)S(1)}, f32[10,88,128]{2,1,0:T(8,128)S(1)}) custom-call(f32[1,10,128,128]{3,2,1,0:T(8,128)} %guess.3, f32[10,128,128]{2,1,0:T(8,128)} %diff.3, f32[3,10,128,128]{3,2,1,0:T(8,128)} %vel.3), custom_call_target="tpu_custom_call" | custom-call | bytes 7200000 | tf_op jit(solution)/shard_map/first_cut_kernel/pallas_call | solution.py:589
  1.2 1.6 %collective-permute-start.1 = (f32[10,88,128]{2,1,0:T(8,128)S(1)}, f32[10,88,128]{2,1,0:T(8,128)S(1)}, u32[]{:S(2)}, u32[]{:S(2)}) collective-permute-start(f32[10,88,128]{2,1,0:T(8,128)S(1)} %get-tuple-element.38), channel_id=1, source_target_pairs={{0,4},{1,5},{2,6},{3,7},{4,0},{5,1},{6,2},{7,3},{8,12},{9,13},{10,... | collective-permute-start | bytes 1351688 | tf_op jit(solution)/shard_map/ppermute | solution.py:75
  2.7 0.5 collective-permute-start
  3.3 2.0 %second_cut_kernel.1 = (f32[10,80,128]{2,1,0:T(8,128)S(1)}, f32[10,96,128]{2,1,0:T(8,128)S(1)}, f32[10,80,128]{2,1,0:T(8,128)S(1)}, f32[10,96,128]{2,1,0:T(8,128)S(1)}, f32[4,10,80,128]{3,2,1,0:T(8,128)S(1)}) custom-call(f32[1,10,128,128]{3,2,1,0:T(8,128)} %guess.3, f32[10,128,128]{2,1,0:T(8,128)} %initial.1, f32[10,128,128]{2,1,0:T(8,128)} %diff.3, ...), custom_call_target="tpu_custom_call" | custom-call | bytes 7200000 | tf_op jit(solution)/shard_map/second_cut_kernel/pallas_call | solution.py:589
  5.3 8.3 %collective-permute-done.refs_0_ = f32[10,80,128]{2,1,0:T(8,128)S(1)} collective-permute-done((f32[10,80,128]{2,1,0:T(8,128)S(1)}, f32[10,80,128]{2,1,0:T(8,128)S(1)}, u32[]{:S(2)}, u32[]{:S(2)}) %collective-permute-start) | collective-permute-done | bytes 409632 | tf_op jit(solution)/shard_map/ppermute | solution.py:75
  13.7 0.0 collective-permute-done.1.refs_1_.refs_0_
  13.7 0.1 mix_kernel.1
  13.7 0.6 collective-permute-start.2
  14.3 0.7 collective-permute-start.6
  15.0 1.6 %collective-permute-start.3 = (f32[10,80,128]{2,1,0:T(8,128)S(1)}, f32[10,80,128]{2,1,0:T(8,128)S(1)}, u32[]{:S(2)}, u32[]{:S(2)}) collective-permute-start(f32[10,80,128]{2,1,0:T(8,128)S(1)} %collective-permute-done.refs_0_), channel_id=1, source_target_pairs={{0,8},{1,9},{2,10},{3,11},{4,12},{5,13},{6,14},{7,15},{8,0},{9,1},... | collective-permute-start | bytes 1228808 | tf_op jit(solution)/shard_map/ppermute | solution.py:75
  16.7 0.0 collective-permute-start.4
  16.7 0.6 collective-permute-start.5
  17.2 0.0 collective-permute-done.6.refs_4_
  17.2 10.3 %collective-permute-done.3.refs_1_ = f32[10,80,128]{2,1,0:T(8,128)S(1)} collective-permute-done((f32[10,80,128]{2,1,0:T(8,128)S(1)}, f32[10,80,128]{2,1,0:T(8,128)S(1)}, u32[]{:S(2)}, u32[]{:S(2)}) %collective-permute-start.3) | collective-permute-done | bytes 409632 | tf_op jit(solution)/shard_map/ppermute | solution.py:75
  27.5 0.0 collective-permute-done.4.refs_2_
  27.5 5.2 %collective-permute-done.5.refs_3_ = f32[10,80,128]{2,1,0:T(8,128)S(1)} collective-permute-done((f32[10,80,128]{2,1,0:T(8,128)S(1)}, f32[10,80,128]{2,1,0:T(8,128)S(1)}, u32[]{:S(2)}, u32[]{:S(2)}) %collective-permute-start.5) | collective-permute-done | bytes 409632 | tf_op jit(solution)/shard_map/ppermute | solution.py:75
  32.7 0.0 collective-permute-done.2.refs_1_
  32.7 0.4 field_kernel.1
  33.1 0.8 collective-permute-start.7
  33.9 1.1 %weight_kernel.1 = (f32[7,20,80,128]{3,2,1,0:T(8,128)S(1)}, f32[22,96,128]{2,1,0:T(8,128)S(1)}, f32[22,96,128]{2,1,0:T(8,128)S(1)}) custom-call(f32[4,10,80,128]{3,2,1,0:T(8,128)S(1)} %get-tuple-element.35.coeff_own, f32[10,96,128]{2,1,0:T(8,128)S(1)} %get-tuple-element.36.window, f32[10,80,128]{2,1,0:T(8,128)S(1)} %collective-permute-done.refs_0_, ...), custom_call_target="tpu_custom_call" | custom-call | bytes 10800000 | tf_op jit(solution)/shard_map/weight_kernel/pallas_call | solution.py:589
  35.0 12.7 %total_kernel.1 = (f32[10,64,128]{2,1,0:T(8,128)S(1)}, f32[10,64,128]{2,1,0:T(8,128)S(1)}) custom-call(f32[7,20,80,128]{3,2,1,0:T(8,128)S(1)} %get-tuple-element.47.coeff, f32[22,96,128]{2,1,0:T(8,128)S(1)} %get-tuple-element.54.ahead, f32[2,22,96,128]{3,2,1,0:T(8,128)S(1)} %get-tuple-element.50.fields), custom_call_target="tpu_custom_call" | custom-call | bytes 54000000 | tf_op jit(solution)/shard_map/total_kernel/pallas_call | solution.py:589
  47.7 0.1 collective-permute-start.8
  47.8 1.6 %collective-permute-done.8.got = f32[10,64,128]{2,1,0:T(8,128)S(1)} collective-permute-done((f32[10,64,128]{2,1,0:T(8,128)S(1)}, f32[10,64,128]{2,1,0:T(8,128)S(1)}, u32[]{:S(2)}, u32[]{:S(2)}) %collective-permute-start.8) | collective-permute-done | bytes 327712 | tf_op jit(solution)/shard_map/ppermute | solution.py:75
  49.4 0.1 part_kernel.1
  49.5 0.7 collective-permute-start.11
  50.2 1.3 %collective-permute-start.10 = (f32[10,48,128]{2,1,0:T(8,128)S(1)}, f32[10,48,128]{2,1,0:T(8,128)S(1)}, u32[]{:S(2)}, u32[]{:S(2)}) collective-permute-start(f32[10,48,128]{2,1,0:T(8,128)S(1)} %get-tuple-element.58), channel_id=1, source_target_pairs={{0,16},{1,17},{2,18},{3,19},{4,20},{5,21},{6,22},{7,23},{8,24},{9,... | collective-permute-start | bytes 737288 | tf_op jit(solution)/shard_map/ppermute | solution.py:75
  51.5 4.1 %collective-permute-start.9 = (f32[10,48,128]{2,1,0:T(8,128)S(1)}, f32[10,48,128]{2,1,0:T(8,128)S(1)}, u32[]{:S(2)}, u32[]{:S(2)}) collective-permute-start(f32[10,48,128]{2,1,0:T(8,128)S(1)} %get-tuple-element.57), channel_id=1, source_target_pairs={{0,8},{1,9},{2,10},{3,11},{4,12},{5,13},{6,14},{7,15},{8,16},{9,17... | collective-permute-start | bytes 737288 | tf_op jit(solution)/shard_map/ppermute | solution.py:75
  55.6 0.0 collective-permute-done.7.flipped
  55.6 8.2 %term_kernel.1 = (f32[2,20,32,128]{3,2,1,0:T(8,128)S(1)}, f32[20,48,128]{2,1,0:T(8,128)S(1)}) custom-call(f32[7,20,80,128]{3,2,1,0:T(8,128)S(1)} %get-tuple-element.47.coeff, f32[2,22,96,128]{3,2,1,0:T(8,128)S(1)} %get-tuple-element.50.fields, f32[2,20,64,128]{3,2,1,0:T(8,128)S(1)} %collective-permute-done.7.flipped, f32[22,96,128]{2,1,0:T(8,128)S(1)} %get-tuple-element.52.seed), custom_call_target="tpu_custom_call" | custom-call | bytes 54000000 | tf_op jit(solution)/shard_map/term_kernel/pallas_call | solution.py:589
  63.8 9.6 %collective-permute-done.10.refs_1_ = f32[10,48,128]{2,1,0:T(8,128)S(1)} collective-permute-done((f32[10,48,128]{2,1,0:T(8,128)S(1)}, f32[10,48,128]{2,1,0:T(8,128)S(1)}, u32[]{:S(2)}, u32[]{:S(2)}) %collective-permute-start.10) | collective-permute-done | bytes 245792 | tf_op jit(solution)/shard_map/ppermute | solution.py:75
  73.4 5.9 %collective-permute-done.9.refs_0_ = f32[10,48,128]{2,1,0:T(8,128)S(1)} collective-permute-done((f32[10,48,128]{2,1,0:T(8,128)S(1)}, f32[10,48,128]{2,1,0:T(8,128)S(1)}, u32[]{:S(2)}, u32[]{:S(2)}) %collective-permute-start.9) | collective-permute-done | bytes 245792 | tf_op jit(solution)/shard_map/ppermute | solution.py:75
  79.3 0.0 collective-permute-done.11.refs_2_
  79.3 2.9 %start_kernel.1.share = f32[20,48,128]{2,1,0:T(8,128)S(1)} custom-call(f32[7,20,80,128]{3,2,1,0:T(8,128)S(1)} %get-tuple-element.47.coeff, f32[20,48,128]{2,1,0:T(8,128)S(1)} %get-tuple-element.53.begun, f32[10,48,128]{2,1,0:T(8,128)S(1)} %collective-permute-done.9.refs_0_, f32[10,48,128]{2,1,0:T(8,128)S(1)} %collective-permute-done.10.refs_1_, ...), custom_call_target="tpu_custom_call" | custom-call | bytes 21600000 | tf_op jit(solution)/shard_map/start_kernel/pallas_call | solution.py:589
  82.2 0.1 collective-permute-start.12
  82.3 1.9 %collective-permute-done.12.other = f32[20,48,128]{2,1,0:T(8,128)S(1)} collective-permute-done((f32[20,48,128]{2,1,0:T(8,128)S(1)}, f32[20,48,128]{2,1,0:T(8,128)S(1)}, u32[]{:S(2)}, u32[]{:S(2)}) %collective-permute-start.12) | collective-permute-done | bytes 491552 | tf_op jit(solution)/shard_map/ppermute | solution.py:75
  84.1 2.1 %end_kernel.1 = (f32[10,32,128]{2,1,0:T(8,128)S(1)}, f32[10,32,128]{2,1,0:T(8,128)S(1)}, f32[10,32,128]{2,1,0:T(8,128)S(1)}, f32[10,32,128]{2,1,0:T(8,128)S(1)}) custom-call(f32[7,20,80,128]{3,2,1,0:T(8,128)S(1)} %get-tuple-element.47.coeff, f32[20,48,128]{2,1,0:T(8,128)S(1)} %start_kernel.1.share, f32[20,48,128]{2,1,0:T(8,128)S(1)} %collective-permute-done.12.other, ...), custom_call_target="tpu_custom_call" | custom-call | bytes 10800000 | tf_op jit(solution)/shard_map/end_kernel/pallas_call | solution.py:589
  86.2 1.5 %collective-permute-start.13 = (f32[10,32,128]{2,1,0:T(8,128)S(1)}, f32[10,32,128]{2,1,0:T(8,128)S(1)}, u32[]{:S(2)}, u32[]{:S(2)}) collective-permute-start(f32[10,32,128]{2,1,0:T(8,128)S(1)} %get-tuple-element.62), channel_id=1, source_target_pairs={{0,4},{1,5},{2,6},{3,7},{4,0},{5,1},{6,2},{7,3},{8,12},{9,13},{10,... | collective-permute-start | bytes 491528 | tf_op jit(solution)/shard_map/ppermute | solution.py:75
  87.7 1.6 %collective-permute-start.14 = (f32[10,32,128]{2,1,0:T(8,128)S(1)}, f32[10,32,128]{2,1,0:T(8,128)S(1)}, u32[]{:S(2)}, u32[]{:S(2)}) collective-permute-start(f32[10,32,128]{2,1,0:T(8,128)S(1)} %get-tuple-element.63), channel_id=1, source_target_pairs={{0,1},{1,0},{2,3},{3,2},{4,5},{5,4},{6,7},{7,6},{8,9},{9,8},{10,11... | collective-permute-start | bytes 491528 | tf_op jit(solution)/shard_map/ppermute | solution.py:75
  89.2 0.5 collective-permute-start.15
  89.8 2.8 %collective-permute-done.13.refs_1_ = f32[10,32,128]{2,1,0:T(8,128)S(1)} collective-permute-done((f32[10,32,128]{2,1,0:T(8,128)S(1)}, f32[10,32,128]{2,1,0:T(8,128)S(1)}, u32[]{:S(2)}, u32[]{:S(2)}) %collective-permute-start.13) | collective-permute-done | bytes 163872 | tf_op jit(solution)/shard_map/ppermute | solution.py:75
  92.5 2.2 %collective-permute-done.14.refs_2_ = f32[10,32,128]{2,1,0:T(8,128)S(1)} collective-permute-done((f32[10,32,128]{2,1,0:T(8,128)S(1)}, f32[10,32,128]{2,1,0:T(8,128)S(1)}, u32[]{:S(2)}, u32[]{:S(2)}) %collective-permute-start.14) | collective-permute-done | bytes 163872 | tf_op jit(solution)/shard_map/ppermute | solution.py:75
  94.8 2.5 %collective-permute-done.15.refs_3_ = f32[10,32,128]{2,1,0:T(8,128)S(1)} collective-permute-done((f32[10,32,128]{2,1,0:T(8,128)S(1)}, f32[10,32,128]{2,1,0:T(8,128)S(1)}, u32[]{:S(2)}, u32[]{:S(2)}) %collective-permute-start.15) | collective-permute-done | bytes 163872 | tf_op jit(solution)/shard_map/ppermute | solution.py:75
  97.2 0.9 place_kernel.1
Async XLA Ops:
  1.2 12.5 %collective-permute-start.1 = (f32[10,88,128]{2,1,0:T(8,128)S(1)}, f32[10,88,128]{2,1,0:T(8,128)S(1)}, u32[]{:S(2)}, u32[]{:S(2)}) collective-permute-start(f32[10,88,128]{2,1,0:T(8,128)S(1)} %get-tuple-element.38), channel_id=1, source_target_pairs={{0,4},{1,5},{2,6},{3,7},{4,0},{5,1},{6,2},{7,3},{8,12},{9,13},{10,... | collective-permute-start | bytes 1351688 | tf_op jit(solution)/shard_map/ppermute | solution.py:75
  2.7 10.9 %collective-permute-start = (f32[10,80,128]{2,1,0:T(8,128)S(1)}, f32[10,80,128]{2,1,0:T(8,128)S(1)}, u32[]{:S(2)}, u32[]{:S(2)}) collective-permute-start(f32[10,80,128]{2,1,0:T(8,128)S(1)} %get-tuple-element.37), channel_id=1, source_target_pairs={{0,1},{1,0},{2,3},{3,2},{4,5},{5,4},{6,7},{7,6},{8,9},{9,8},{10,11... | collective-permute-start | bytes 1228808 | tf_op jit(solution)/shard_map/ppermute | solution.py:75
  13.7 19.0 %collective-permute-start.2 = (f32[2,10,80,128]{3,2,1,0:T(8,128)S(1)}, f32[2,10,80,128]{3,2,1,0:T(8,128)S(1)}, u32[]{:S(2)}, u32[]{:S(2)}) collective-permute-start(f32[2,10,80,128]{3,2,1,0:T(8,128)S(1)} %mix_kernel.1), channel_id=1, source_target_pairs={{0,1},{1,0},{2,3},{3,2},{4,5},{5,4},{6,7},{7,6},{8,9},{9,8},{10,11... | collective-permute-start | bytes 2457608 | tf_op jit(solution)/shard_map/ppermute | solution.py:75
  14.3 2.9 %collective-permute-start.6 = (f32[10,96,128]{2,1,0:T(8,128)S(1)}, f32[10,96,128]{2,1,0:T(8,128)S(1)}, u32[]{:S(2)}, u32[]{:S(2)}) collective-permute-start(f32[10,96,128]{2,1,0:T(8,128)S(1)} %get-tuple-element.42), channel_id=1, source_target_pairs={{0,1},{1,0},{4,5},{5,4}} | collective-permute-start | bytes 1474568 | tf_op jit(solution)/shard_map/ppermute | solution.py:75
  15.0 12.5 %collective-permute-start.3 = (f32[10,80,128]{2,1,0:T(8,128)S(1)}, f32[10,80,128]{2,1,0:T(8,128)S(1)}, u32[]{:S(2)}, u32[]{:S(2)}) collective-permute-start(f32[10,80,128]{2,1,0:T(8,128)S(1)} %collective-permute-done.refs_0_), channel_id=1, source_target_pairs={{0,8},{1,9},{2,10},{3,11},{4,12},{5,13},{6,14},{7,15},{8,0},{9,1},... | collective-permute-start | bytes 1228808 | tf_op jit(solution)/shard_map/ppermute | solution.py:75
  16.7 10.8 %collective-permute-start.4 = (f32[10,80,128]{2,1,0:T(8,128)S(1)}, f32[10,80,128]{2,1,0:T(8,128)S(1)}, u32[]{:S(2)}, u32[]{:S(2)}) collective-permute-start(f32[10,80,128]{2,1,0:T(8,128)S(1)} %collective-permute-done.refs_0_), channel_id=1, source_target_pairs={{0,2},{1,3},{2,0},{3,1},{4,6},{5,7},{6,4},{7,5},{8,10},{9,11},{10,... | collective-permute-start | bytes 1228808 | tf_op jit(solution)/shard_map/ppermute | solution.py:75
  16.7 16.0 %collective-permute-start.5 = (f32[10,80,128]{2,1,0:T(8,128)S(1)}, f32[10,80,128]{2,1,0:T(8,128)S(1)}, u32[]{:S(2)}, u32[]{:S(2)}) collective-permute-start(f32[10,80,128]{2,1,0:T(8,128)S(1)} %collective-permute-done.refs_0_), channel_id=1, source_target_pairs={{0,10},{1,11},{2,8},{3,9},{4,14},{5,15},{6,12},{7,13},{8,2},{9,3},... | collective-permute-start | bytes 1228808 | tf_op jit(solution)/shard_map/ppermute | solution.py:75
  33.1 22.5 %collective-permute-start.7 = (f32[2,20,64,128]{3,2,1,0:T(8,128)S(1)}, f32[2,20,64,128]{3,2,1,0:T(8,128)S(1)}, u32[]{:S(2)}, u32[]{:S(2)}) collective-permute-start(f32[2,20,64,128]{3,2,1,0:T(8,128)S(1)} %get-tuple-element.51), channel_id=1, source_target_pairs={{0,2},{1,3},{2,0},{3,1},{4,6},{5,7},{6,4},{7,5},{8,10},{9,11},{10,... | collective-permute-start | bytes 3932168 | tf_op jit(solution)/shard_map/ppermute | solution.py:75
  47.7 1.7 %collective-permute-start.8 = (f32[10,64,128]{2,1,0:T(8,128)S(1)}, f32[10,64,128]{2,1,0:T(8,128)S(1)}, u32[]{:S(2)}, u32[]{:S(2)}) collective-permute-start(f32[10,64,128]{2,1,0:T(8,128)S(1)} %get-tuple-element.56), channel_id=1, source_target_pairs={{0,2},{1,3},{2,0},{3,1},{4,6},{5,7},{6,4},{7,5},{8,10},{9,11},{10,... | collective-permute-start | bytes 983048 | tf_op jit(solution)/shard_map/ppermute | solution.py:75
  49.5 29.8 %collective-permute-start.11 = (f32[10,64,128]{2,1,0:T(8,128)S(1)}, f32[10,64,128]{2,1,0:T(8,128)S(1)}, u32[]{:S(2)}, u32[]{:S(2)}) collective-permute-start(f32[10,64,128]{2,1,0:T(8,128)S(1)} %get-tuple-element.59), channel_id=1, source_target_pairs={{0,24},{1,25},{2,26},{3,27},{4,28},{5,29},{6,30},{7,31}} | collective-permute-start | bytes 983048 | tf_op jit(solution)/shard_map/ppermute | solution.py:75
  50.2 23.2 %collective-permute-start.10 = (f32[10,48,128]{2,1,0:T(8,128)S(1)}, f32[10,48,128]{2,1,0:T(8,128)S(1)}, u32[]{:S(2)}, u32[]{:S(2)}) collective-permute-start(f32[10,48,128]{2,1,0:T(8,128)S(1)} %get-tuple-element.58), channel_id=1, source_target_pairs={{0,16},{1,17},{2,18},{3,19},{4,20},{5,21},{6,22},{7,23},{8,24},{9,... | collective-permute-start | bytes 737288 | tf_op jit(solution)/shard_map/ppermute | solution.py:75
  51.5 27.8 %collective-permute-start.9 = (f32[10,48,128]{2,1,0:T(8,128)S(1)}, f32[10,48,128]{2,1,0:T(8,128)S(1)}, u32[]{:S(2)}, u32[]{:S(2)}) collective-permute-start(f32[10,48,128]{2,1,0:T(8,128)S(1)} %get-tuple-element.57), channel_id=1, source_target_pairs={{0,8},{1,9},{2,10},{3,11},{4,12},{5,13},{6,14},{7,15},{8,16},{9,17... | collective-permute-start | bytes 737288 | tf_op jit(solution)/shard_map/ppermute | solution.py:75
  82.2 1.9 %collective-permute-start.12 = (f32[20,48,128]{2,1,0:T(8,128)S(1)}, f32[20,48,128]{2,1,0:T(8,128)S(1)}, u32[]{:S(2)}, u32[]{:S(2)}) collective-permute-start(f32[20,48,128]{2,1,0:T(8,128)S(1)} %start_kernel.1.share), channel_id=1, source_target_pairs={{0,2},{1,3},{2,0},{3,1},{4,6},{5,7},{6,4},{7,5},{8,10},{9,11},{10,... | collective-permute-start | bytes 1474568 | tf_op jit(solution)/shard_map/ppermute | solution.py:75
  86.2 6.3 %collective-permute-start.13 = (f32[10,32,128]{2,1,0:T(8,128)S(1)}, f32[10,32,128]{2,1,0:T(8,128)S(1)}, u32[]{:S(2)}, u32[]{:S(2)}) collective-permute-start(f32[10,32,128]{2,1,0:T(8,128)S(1)} %get-tuple-element.62), channel_id=1, source_target_pairs={{0,4},{1,5},{2,6},{3,7},{4,0},{5,1},{6,2},{7,3},{8,12},{9,13},{10,... | collective-permute-start | bytes 491528 | tf_op jit(solution)/shard_map/ppermute | solution.py:75
  87.7 7.1 %collective-permute-start.14 = (f32[10,32,128]{2,1,0:T(8,128)S(1)}, f32[10,32,128]{2,1,0:T(8,128)S(1)}, u32[]{:S(2)}, u32[]{:S(2)}) collective-permute-start(f32[10,32,128]{2,1,0:T(8,128)S(1)} %get-tuple-element.63), channel_id=1, source_target_pairs={{0,1},{1,0},{2,3},{3,2},{4,5},{5,4},{6,7},{7,6},{8,9},{9,8},{10,11... | collective-permute-start | bytes 491528 | tf_op jit(solution)/shard_map/ppermute | solution.py:75
  89.2 8.0 %collective-permute-start.15 = (f32[10,32,128]{2,1,0:T(8,128)S(1)}, f32[10,32,128]{2,1,0:T(8,128)S(1)}, u32[]{:S(2)}, u32[]{:S(2)}) collective-permute-start(f32[10,32,128]{2,1,0:T(8,128)S(1)} %get-tuple-element.64), channel_id=1, source_target_pairs={{0,5},{1,4},{2,7},{3,6},{4,1},{5,0},{6,3},{7,2},{8,13},{9,12},{10,... | collective-permute-start | bytes 491528 | tf_op jit(solution)/shard_map/ppermute | solution.py:75

commit v3 on v2

--- a/solution.py
+++ b/solution.py
@@ -16,6 +16,7 @@
 GROUP = 4
 TILE = 8
 LANES = 128
+SETS = 6
 SPARE_BYTES = 4 * 1024 * 1024
 VMEM_BYTES = 56 * 1024 * 1024
 VMEM = pl.BlockSpec(memory_space=pltpu.VMEM)
@@ -56,6 +57,16 @@
         start = jnp.clip(chip * self.chunk - self.halo - TILE, 0, self.rows - self.wide)
         return pl.multiple_of(start, TILE)
 
+    def reach_rows(self, distance):
+        return min(self.rows, self.chunk + 2 * self.trim(distance))
+
+    def trim(self, distance):
+        return -(-self.reach[distance - 1] // 4) * 4
+
+    def reach_start(self, chip, distance):
+        start = jnp.clip(chip * self.chunk - self.trim(distance), 0, self.rows - self.reach_rows(distance))
+        return pl.multiple_of(start, 4)
+
     def span_start(self, y):
         start = jnp.clip(y * self.n_s * self.chunk - self.halo, 0, self.rows - self.span)
         return pl.multiple_of(start, TILE)
@@ -67,8 +78,8 @@
         pairs = []
         for t, s in itertools.product(range(self.n_t), range(self.n_s)):
             core, y, z = t % 2, (t // 2) % self.pairs, t // GROUP
-            to_z = z ^ 1 if swap else z + dz
-            if to_z >= self.groups or (first and (z or core)):
+            to_z = z ^ 1 if swap else 0 if first else z + dz
+            if to_z >= self.groups or (first and (z < self.groups - 1 or core)):
                 continue
             to_t = to_z * GROUP + (y + dy) % self.pairs * 2 + (core ^ int(flip))
             pairs.append((t * self.n_s + s, to_t * self.n_s + (s + ds) % self.n_s))
@@ -123,11 +134,11 @@
             pltpu.matmul_push_rhs(matrix, 0, unit)
             pltpu.matmul_acc_lhs(sums[unit], jnp.zeros((2 * TILE, 2 * plan.lanes), jnp.bfloat16), load_staged_rhs=0)
             pltpu.matmul_pop(sums[unit])
-        body((sums[:count], sums[count:]))
+        body([sums[i * count : (i + 1) * count] for i in range(SETS)])
 
     pl.run_scoped(
         run,
-        *[pltpu.ACC(i % count % 2)((2 * TILE, 2 * plan.lanes), jnp.float32) for i in range(2 * count)],
+        *[pltpu.ACC(i % count % 2)((2 * TILE, 2 * plan.lanes), jnp.float32) for i in range(SETS * count)],
     )
 
 
@@ -148,15 +159,15 @@
             rest = (value - high.astype(jnp.float32)).astype(jnp.bfloat16)
             pltpu.matmul_acc_lhs(sums[which][pair], jnp.concatenate([high, rest], axis=1))
 
-        def strip(index, which, later):
+        def strip(index, which, later, later_set):
             row = rows(index)
             inner = pl.ds(row, TILE)
             here = pl.ds(pl.multiple_of(row + TILE, TILE), TILE)
             low, mid = source[0, here, :], source[1, here, :]
             for layer in range(plan.layers):
                 if layer % 2 == 0:
-                    shift(later, 1 - which, layer // 2)
                     moved = pltpu.matmul_pop(sums[which][layer // 2])
+                    shift(later, later_set, layer // 2)
                 part = moved[layer % 2 * TILE : (layer % 2 + 1) * TILE]
                 high = source[layer + 2, here, :]
                 x_low = source[layer + 1, pl.ds(row + TILE - 1, TILE), :]
@@ -174,17 +185,27 @@
                 target[layer + 1, here, :] = fresh
                 low, mid = mid, high
 
-        for pair in range(count):
-            shift(0, 0, pair)
-
-        def two(index, _):
-            strip(2 * index, 0, jnp.minimum(2 * index + 1, strips - 1))
-            strip(jnp.minimum(2 * index + 1, strips - 1), 1, jnp.minimum(2 * index + 2, strips - 1))
+        sets = next(k for k in range(SETS, 1, -1) if strips % k == 0 or k == 2)
+        ahead = sets - 1
+
+        def bounded(index):
+            return jnp.minimum(index, strips - 1)
+
+        for index in range(ahead):
+            for pair in range(count):
+                shift(bounded(index), index, pair)
+
+        def some(index, _):
+            for which in range(sets):
+                strip(
+                    bounded(index * sets + which), which, bounded(index * sets + which + ahead), (which + ahead) % sets
+                )
             return 0
 
-        lax.fori_loop(0, -(-strips // 2), two, 0)
-        for pair in range(count):
-            pltpu.matmul_pop(sums[0][pair])
+        lax.fori_loop(0, -(-strips // sets), some, 0)
+        for index in range(ahead):
+            for pair in range(count):
+                pltpu.matmul_pop(sums[index][pair])
 
     return step
 
@@ -212,10 +233,10 @@
             field[layer] = jnp.zeros_like(field[layer])
 
 
-def first_cut_kernel(plan, guess, diff, vel, *refs):
+def first_cut_kernel(plan, guess, initial, diff, vel, *refs):
     place = Place(plan)
     sem = refs[-1]
-    coeffs, blocks = refs[: plan.n_s - 1], refs[plan.n_s - 1 : -1]
+    coeffs, inits, blocks = refs[: plan.n_s - 1], refs[plan.n_s - 1 : 2 * plan.n_s - 2], refs[2 * plan.n_s - 2 : -1]
     which = place.core * 2 + lax.rem(place.z, 2)
 
     def source(ds, array):
@@ -235,7 +256,11 @@
     copies = []
     for dy, target in enumerate(blocks, 1):
         start = plan.span_start(lax.rem(place.y + dy, plan.pairs))
-        copies.append(pltpu.make_async_copy(guess.at[0, :, pl.ds(start, plan.span), :], target, sem.at[plan.n_s - 2 + dy]))
+        copies.append(pltpu.make_async_copy(guess.at[0, :, pl.ds(start, plan.span), :], target, sem.at[2 * plan.n_s - 3 + dy]))
+    for ds, target in enumerate(inits, 1):
+        start = plan.wide_start(place.ahead(0, ds))
+        source_rows = initial.at[:, pl.ds(start, plan.wide), :]
+        copies.append(pltpu.make_async_copy(source_rows, target, sem.at[plan.n_s - 2 + ds]))
     for copy in copies:
         copy.start()
     for ds, target in enumerate(coeffs, 1):
@@ -244,24 +269,26 @@
         copy.wait()
 
 
-def second_cut_kernel(plan, guess, initial, diff, vel, *refs):
-    place = Place(plan)
-    refs, sem = refs[:-1], refs[-1]
-    count = plan.n_s - 1
-    blocks, inits = refs[:count], refs[count : 2 * count]
-    guess_own, initial_own, coeff_own = refs[2 * count :]
+def second_cut_kernel(plan, guess, *refs):
+    place = Place(plan)
+    blocks, sem = refs[:-1], refs[-1]
     copies = []
     for ds, target in enumerate(blocks, 1):
         start = plan.start_of(place.ahead(0, ds), plan.halo)
         copies.append((guess.at[0, :, pl.ds(start, plan.width), :], target))
-    for ds, target in enumerate(inits, 1):
-        start = plan.wide_start(place.ahead(0, ds))
-        copies.append((initial.at[:, pl.ds(start, plan.wide), :], target))
+    for copy in fetch(sem, copies):
+        copy.wait()
+
+
+def own_cut_kernel(plan, guess, initial, diff, vel, guess_own, initial_own, coeff_own, sem):
+    place = Place(plan)
     rows = pl.ds(place.base, plan.width)
-    copies.append((guess.at[0, :, rows, :], guess_own))
-    copies.append((initial.at[:, pl.ds(plan.wide_start(place.chip), plan.wide), :], initial_own))
-    copies.append((diff.at[:, rows, :], coeff_own.at[0]))
-    copies.append((vel.at[:, :, rows, :], coeff_own.at[pl.ds(1, 3)]))
+    copies = [
+        (guess.at[0, :, rows, :], guess_own),
+        (initial.at[:, pl.ds(plan.wide_start(place.chip), plan.wide), :], initial_own),
+        (diff.at[:, rows, :], coeff_own.at[0]),
+        (vel.at[:, :, rows, :], coeff_own.at[pl.ds(1, 3)]),
+    ]
     for copy in fetch(sem, copies):
         copy.wait()
 
@@ -435,9 +462,9 @@
 
 def part_kernel(plan, keep, got, *outs):
     place = Place(plan)
-    for reach, out in zip(plan.reach, outs):
-        start = pl.multiple_of(place.inner(reach) - place.inner(plan.far), TILE)
-        rows = pl.ds(start, plan.width_of(reach))
+    for distance, out in enumerate(outs, 1):
+        start = plan.reach_start(place.chip, distance) - plan.start_of(place.chip, plan.far)
+        rows = pl.ds(start, plan.reach_rows(distance))
         for layer in range(plan.side):
             out[layer] = keep[layer, rows, :] + got[layer, rows, :]
 
@@ -519,7 +546,8 @@
             @pl.when(place.z >= distance)
             def _(distance=distance):
                 reach = plan.reach[distance - 1]
-                rows = pl.ds(pl.multiple_of(place.inner(reach) + TILE, TILE), plan.width_of(reach))
+                start = plan.reach_start(place.chip, distance) - place.base + TILE
+                rows = pl.ds(start, plan.reach_rows(distance))
                 for layer in range(plan.side):
                     index = 1 + place.core * plan.side + layer
                     now[index, rows, :] = now[index, rows, :] + totals[distance - 1][layer]
@@ -610,42 +638,31 @@
         plan,
         first_cut_kernel,
         2,
-        [piece] * sides + [(depth, plan.span, lanes)] * (plan.pairs - 1),
-        [],
-        guess,
-        diffusivity,
-        velocity,
-        copies=sides + plan.pairs - 1,
-        whole=3,
-    )
-    got = [plan.send(part, ds=ds) for ds, part in enumerate(cuts[:sides], 1)]
-    got += [plan.send(part, dy=dy) for dy, part in enumerate(cuts[sides:], 1)]
-    cuts = call(
-        plan,
-        second_cut_kernel,
-        2,
-        [piece] * sides + [window] * sides + [piece, window, (4, *piece)],
+        [piece] * sides + [window] * sides + [(depth, plan.span, lanes)] * (plan.pairs - 1),
         [],
         guess,
         initial,
         diffusivity,
         velocity,
-        copies=2 * sides + 4,
+        copies=2 * sides + plan.pairs - 1,
         whole=4,
     )
-    own_sent, inits, (guess_own, initial_own, coeff_own) = cuts[:sides], cuts[sides : 2 * sides], cuts[2 * sides :]
-    got = lax.optimization_barrier(got)
-    coeffs, beside = got[:sides], got[sides:]
+    got = [plan.send(part, ds=ds) for ds, part in enumerate(cuts[:sides], 1)]
+    got += [plan.send(part, ds=ds, first=True) for ds, part in enumerate(cuts[sides : 2 * sides], 1)]
+    got += [plan.send(part, dy=dy) for dy, part in enumerate(cuts[2 * sides :], 1)]
+    own_sent = call(plan, second_cut_kernel, 1, [piece] * sides, [], guess, copies=sides, whole=1)
+    guess_own, initial_own, coeff_own = call(
+        plan, own_cut_kernel, 60, [piece, window, (4, *piece)], [], guess, initial, diffusivity, velocity, copies=4, whole=4
+    )
+    coeffs, inits, beside = got[:sides], got[sides : 2 * sides], got[2 * sides :]
+    got = lax.optimization_barrier((*coeffs, *beside, *own_sent))
+    coeffs, beside, own_sent = got[:sides], got[sides:-sides], got[-sides:]
     mixed = call(plan, mix_kernel, 0.3, [(plan.pairs, *piece)] * sides, [], *own_sent, *beside)
     distant = [plan.send(part, ds=ds) for ds, part in enumerate(mixed, 1)]
-    inits = [plan.send(init, ds=ds, first=True) for ds, init in enumerate(inits, 1)]
     swapped = []
     for part in coeffs:
-        swapped.append(plan.send(part, swap=True))
-        swapped.append(plan.send(part, flip=True))
-        swapped.append(plan.send(part, swap=True, flip=True))
-    got = lax.optimization_barrier((*distant, *swapped, *inits))
-    distant, swapped, inits = got[:sides], got[sides : 4 * sides], got[4 * sides :]
+        flipped, part = plan.send(part, flip=True), plan.send(part, swap=True)
+        swapped += [part, flipped, plan.send(part, flip=True)]
     near = []
     for index, (part, init) in enumerate(zip(coeffs, inits)):
         near += [part, *swapped[3 * index : 3 * index + 3], init]
@@ -660,6 +677,7 @@
         initial_own,
         *near,
     )
+    coeff, *distant = lax.optimization_barrier((coeff, *distant))
     fields, given = call(
         plan,
         field_kernel,
@@ -677,7 +695,7 @@
         plan,
         part_kernel,
         0.3,
-        [(plan.side, plan.width_of(reach), lanes) for reach in plan.reach],
+        [(plan.side, plan.reach_rows(distance), lanes) for distance in range(1, plan.groups)],
         [],
         keep,
         plan.send(give, flip=True),

time: 99.4 us -> 93.6 us (0.942)
  starting transfers between devices: 16.2 us -> 13.8 us
  Pallas kernels: 31.5 us -> 29.8 us
    ppermute x16, starting transfers between devices: 16.2 us -> 13.8 us  [send(): return lax.ppermute(value, ('tm', 'space'), pairs)]
    pallas_call x11 -> x12, Pallas kernels: 31.5 us -> 29.8 us  [call(): pl.pallas_call(functools.partial(kernel, plan), out_shape=[held(shape, jn...]
  transfers between devices with their start and end apart: 16 -> 16, of which waited for: 10 -> 9; matrix products, arithmetic and copies ran while one was open for 0% -> 0% of each run, Pallas kernels for 25% -> 24%
where the time goes in v3:
time: 93.6 us; the launch traced here: 93.3 us
  waiting for transfers between devices  49.4 us (53%)
  Pallas kernels  29.8 us (32%)
  starting transfers between devices  13.8 us (15%)
    ppermute x16, waiting for transfers between devices, send(): return lax.ppermute(value, ('tm', 'space'), pairs)  49.4 us
    pallas_call x12, Pallas kernels, call(): pl.pallas_call(functools.partial(kernel, plan), out_shape=[held(shape, jn...  29.8 us
    ppermute x16, starting transfers between devices, send(): return lax.ppermute(value, ('tm', 'space'), pairs)  13.8 us
  transfers between devices with their start and end apart: 16, of which 9 were waited for; matrix products, arithmetic and copies ran while one was open for 0% of the time, Pallas kernels for 24%

profile of v3, /device:TPU:18, one launch (start us, length us, event | category | flops | bytes accessed | tf_op | source)
XLA Modules:
  0.0 93.3 jit_solution(2649751060333118559)
XLA Ops:
  0.0 1.3 %first_cut_kernel.1 = (f32[10,80,128]{2,1,0:T(8,128)S(1)}, f32[10,96,128]{2,1,0:T(8,128)S(1)}, f32[10,88,128]{2,1,0:T(8,128)S(1)}) custom-call(f32[1,10,128,128]{3,2,1,0:T(8,128)} %guess.5, f32[10,128,128]{2,1,0:T(8,128)} %initial.3, f32[10,128,128]{2,1,0:T(8,128)} %diff.3, f32[3,10,128,128]{3,2,1,0:T(8,128)} %vel.3), custom_call_target="tpu_custom_call" | custom-call | bytes 7200000 | tf_op jit(solution)/shard_map/first_cut_kernel/pallas_call | solution.py:617
  1.3 1.6 %collective-permute-start.1 = (f32[10,88,128]{2,1,0:T(8,128)S(1)}, f32[10,88,128]{2,1,0:T(8,128)S(1)}, u32[]{:S(2)}, u32[]{:S(2)}) collective-permute-start(f32[10,88,128]{2,1,0:T(8,128)S(1)} %get-tuple-element.35), channel_id=1, source_target_pairs={{0,4},{1,5},{2,6},{3,7},{4,0},{5,1},{6,2},{7,3},{8,12},{9,13},{10,... | collective-permute-start | bytes 1351688 | tf_op jit(solution)/shard_map/ppermute | solution.py:86
  2.9 0.5 collective-permute-start
  3.4 1.0 %second_cut_kernel.1.refs_0_ = f32[10,80,128]{2,1,0:T(8,128)S(1)} custom-call(f32[1,10,128,128]{3,2,1,0:T(8,128)} %guess.5), custom_call_target="tpu_custom_call" | custom-call | bytes 3600000 | tf_op jit(solution)/shard_map/second_cut_kernel/pallas_call | solution.py:617
  4.5 9.4 %collective-permute-done.refs_0_ = f32[10,80,128]{2,1,0:T(8,128)S(1)} collective-permute-done((f32[10,80,128]{2,1,0:T(8,128)S(1)}, f32[10,80,128]{2,1,0:T(8,128)S(1)}, u32[]{:S(2)}, u32[]{:S(2)}) %collective-permute-start) | collective-permute-done | bytes 409632 | tf_op jit(solution)/shard_map/ppermute | solution.py:86
  13.8 0.0 collective-permute-done.1.refs_1_.refs_0_
  13.8 1.6 %collective-permute-start.2 = (f32[10,80,128]{2,1,0:T(8,128)S(1)}, f32[10,80,128]{2,1,0:T(8,128)S(1)}, u32[]{:S(2)}, u32[]{:S(2)}) collective-permute-start(f32[10,80,128]{2,1,0:T(8,128)S(1)} %collective-permute-done.refs_0_), channel_id=1, source_target_pairs={{0,8},{1,9},{2,10},{3,11},{4,12},{5,13},{6,14},{7,15},{8,0},{9,1},... | collective-permute-start | bytes 1228808 | tf_op jit(solution)/shard_map/ppermute | solution.py:86
  15.4 0.1 mix_kernel.1
  15.5 0.6 collective-permute-start.6
  16.1 0.7 collective-permute-start.5
  16.8 0.1 collective-permute-start.3
  16.8 7.0 %collective-permute-done.2.refs_1_ = f32[10,80,128]{2,1,0:T(8,128)S(1)} collective-permute-done((f32[10,80,128]{2,1,0:T(8,128)S(1)}, f32[10,80,128]{2,1,0:T(8,128)S(1)}, u32[]{:S(2)}, u32[]{:S(2)}) %collective-permute-start.2) | collective-permute-done | bytes 409632 | tf_op jit(solution)/shard_map/ppermute | solution.py:86
  23.9 0.0 collective-permute-start.4
  23.9 1.7 %own_cut_kernel.1 = (f32[10,80,128]{2,1,0:T(8,128)S(1)}, f32[10,96,128]{2,1,0:T(8,128)S(1)}, f32[4,10,80,128]{3,2,1,0:T(8,128)S(1)}) custom-call(f32[1,10,128,128]{3,2,1,0:T(8,128)} %guess.5, f32[10,128,128]{2,1,0:T(8,128)} %initial.3, f32[10,128,128]{2,1,0:T(8,128)} %diff.3, f32[3,10,128,128]{3,2,1,0:T(8,128)} %vel.3), custom_call_target="tpu_custom_call" | custom-call | bytes 216000000 | tf_op jit(solution)/shard_map/own_cut_kernel/pallas_call | solution.py:617
  25.6 0.0 collective-permute-done.5.refs_4_
  25.6 0.0 collective-permute-done.3.refs_2_
  25.6 0.0 collective-permute-done.4.refs_3_
  25.6 1.1 %weight_kernel.1 = (f32[7,20,80,128]{3,2,1,0:T(8,128)S(1)}, f32[22,96,128]{2,1,0:T(8,128)S(1)}, f32[22,96,128]{2,1,0:T(8,128)S(1)}) custom-call(f32[4,10,80,128]{3,2,1,0:T(8,128)S(1)} %get-tuple-element.32.coeff_own, f32[10,96,128]{2,1,0:T(8,128)S(1)} %get-tuple-element.33.window, f32[10,80,128]{2,1,0:T(8,128)S(1)} %collective-permute-done.refs_0_, ...), custom_call_target="tpu_custom_call" | custom-call | bytes 10800000 | tf_op jit(solution)/shard_map/weight_kernel/pallas_call | solution.py:617
  26.7 7.3 %collective-permute-done.6.refs_1_ = f32[2,10,80,128]{3,2,1,0:T(8,128)S(1)} collective-permute-done((f32[2,10,80,128]{3,2,1,0:T(8,128)S(1)}, f32[2,10,80,128]{3,2,1,0:T(8,128)S(1)}, u32[]{:S(2)}, u32[]{:S(2)}) %collective-permute-start.6) | collective-permute-done | bytes 819232 | tf_op jit(solution)/shard_map/ppermute | solution.py:86
  34.1 0.4 field_kernel.1
  34.5 0.1 collective-permute-start.7
  34.5 11.6 %total_kernel.1 = (f32[10,64,128]{2,1,0:T(8,128)S(1)}, f32[10,64,128]{2,1,0:T(8,128)S(1)}) custom-call(f32[7,20,80,128]{3,2,1,0:T(8,128)S(1)} %get-tuple-element.41.coeff, f32[22,96,128]{2,1,0:T(8,128)S(1)} %get-tuple-element.48.ahead, f32[2,22,96,128]{3,2,1,0:T(8,128)S(1)} %get-tuple-element.44.fields), custom_call_target="tpu_custom_call" | custom-call | bytes 54000000 | tf_op jit(solution)/shard_map/total_kernel/pallas_call | solution.py:617
  46.1 0.1 collective-permute-start.8
  46.2 1.6 %collective-permute-done.8.got = f32[10,64,128]{2,1,0:T(8,128)S(1)} collective-permute-done((f32[10,64,128]{2,1,0:T(8,128)S(1)}, f32[10,64,128]{2,1,0:T(8,128)S(1)}, u32[]{:S(2)}, u32[]{:S(2)}) %collective-permute-start.8) | collective-permute-done | bytes 327712 | tf_op jit(solution)/shard_map/ppermute | solution.py:86
  47.8 0.1 part_kernel.1
  47.9 0.7 collective-permute-start.11
  48.6 1.3 %collective-permute-start.10 = (f32[10,48,128]{2,1,0:T(8,128)S(1)}, f32[10,48,128]{2,1,0:T(8,128)S(1)}, u32[]{:S(2)}, u32[]{:S(2)}) collective-permute-start(f32[10,48,128]{2,1,0:T(8,128)S(1)} %get-tuple-element.52), channel_id=1, source_target_pairs={{0,16},{1,17},{2,18},{3,19},{4,20},{5,21},{6,22},{7,23},{8,24},{9,... | collective-permute-start | bytes 737288 | tf_op jit(solution)/shard_map/ppermute | solution.py:86
  49.9 3.0 %collective-permute-start.9 = (f32[10,40,128]{2,1,0:T(8,128)S(1)}, f32[10,40,128]{2,1,0:T(8,128)S(1)}, u32[]{:S(2)}, u32[]{:S(2)}) collective-permute-start(f32[10,40,128]{2,1,0:T(8,128)S(1)} %get-tuple-element.51), channel_id=1, source_target_pairs={{0,8},{1,9},{2,10},{3,11},{4,12},{5,13},{6,14},{7,15},{8,16},{9,17... | collective-permute-start | bytes 614408 | tf_op jit(solution)/shard_map/ppermute | solution.py:86
  52.9 0.0 collective-permute-done.7.flipped
  52.9 7.3 %term_kernel.1 = (f32[2,20,32,128]{3,2,1,0:T(8,128)S(1)}, f32[20,48,128]{2,1,0:T(8,128)S(1)}) custom-call(f32[7,20,80,128]{3,2,1,0:T(8,128)S(1)} %get-tuple-element.41.coeff, f32[2,22,96,128]{3,2,1,0:T(8,128)S(1)} %get-tuple-element.44.fields, f32[2,20,64,128]{3,2,1,0:T(8,128)S(1)} %collective-permute-done.7.flipped, f32[22,96,128]{2,1,0:T(8,128)S(1)} %get-tuple-element.46.seed), custom_call_target="tpu_custom_call" | custom-call | bytes 54000000 | tf_op jit(solution)/shard_map/term_kernel/pallas_call | solution.py:617
  60.2 14.7 %collective-permute-done.9.refs_0_ = f32[10,40,128]{2,1,0:T(8,128)S(1)} collective-permute-done((f32[10,40,128]{2,1,0:T(8,128)S(1)}, f32[10,40,128]{2,1,0:T(8,128)S(1)}, u32[]{:S(2)}, u32[]{:S(2)}) %collective-permute-start.9) | collective-permute-done | bytes 204832 | tf_op jit(solution)/shard_map/ppermute | solution.py:86
  74.8 0.0 collective-permute-done.10.refs_1_
  74.8 0.0 collective-permute-done.11.refs_2_
  74.8 2.5 %start_kernel.1.share = f32[20,48,128]{2,1,0:T(8,128)S(1)} custom-call(f32[7,20,80,128]{3,2,1,0:T(8,128)S(1)} %get-tuple-element.41.coeff, f32[20,48,128]{2,1,0:T(8,128)S(1)} %get-tuple-element.47.begun, f32[10,40,128]{2,1,0:T(8,128)S(1)} %collective-permute-done.9.refs_0_, f32[10,48,128]{2,1,0:T(8,128)S(1)} %collective-permute-done.10.refs_1_, ...), custom_call_target="tpu_custom_call" | custom-call | bytes 21600000 | tf_op jit(solution)/shard_map/start_kernel/pallas_call | solution.py:617
  77.3 0.1 collective-permute-start.12
  77.4 1.9 %collective-permute-done.12.other = f32[20,48,128]{2,1,0:T(8,128)S(1)} collective-permute-done((f32[20,48,128]{2,1,0:T(8,128)S(1)}, f32[20,48,128]{2,1,0:T(8,128)S(1)}, u32[]{:S(2)}, u32[]{:S(2)}) %collective-permute-start.12) | collective-permute-done | bytes 491552 | tf_op jit(solution)/shard_map/ppermute | solution.py:86
  79.3 1.9 %end_kernel.1 = (f32[10,32,128]{2,1,0:T(8,128)S(1)}, f32[10,32,128]{2,1,0:T(8,128)S(1)}, f32[10,32,128]{2,1,0:T(8,128)S(1)}, f32[10,32,128]{2,1,0:T(8,128)S(1)}) custom-call(f32[7,20,80,128]{3,2,1,0:T(8,128)S(1)} %get-tuple-element.41.coeff, f32[20,48,128]{2,1,0:T(8,128)S(1)} %start_kernel.1.share, f32[20,48,128]{2,1,0:T(8,128)S(1)} %collective-permute-done.12.other, ...), custom_call_target="tpu_custom_call" | custom-call | bytes 10800000 | tf_op jit(solution)/shard_map/end_kernel/pallas_call | solution.py:617
  81.2 1.3 %collective-permute-start.13 = (f32[10,32,128]{2,1,0:T(8,128)S(1)}, f32[10,32,128]{2,1,0:T(8,128)S(1)}, u32[]{:S(2)}, u32[]{:S(2)}) collective-permute-start(f32[10,32,128]{2,1,0:T(8,128)S(1)} %get-tuple-element.56), channel_id=1, source_target_pairs={{0,4},{1,5},{2,6},{3,7},{4,0},{5,1},{6,2},{7,3},{8,12},{9,13},{10,... | collective-permute-start | bytes 491528 | tf_op jit(solution)/shard_map/ppermute | solution.py:86
  82.5 0.8 collective-permute-start.14
  83.2 1.5 %collective-permute-start.15 = (f32[10,32,128]{2,1,0:T(8,128)S(1)}, f32[10,32,128]{2,1,0:T(8,128)S(1)}, u32[]{:S(2)}, u32[]{:S(2)}) collective-permute-start(f32[10,32,128]{2,1,0:T(8,128)S(1)} %get-tuple-element.58), channel_id=1, source_target_pairs={{0,5},{1,4},{2,7},{3,6},{4,1},{5,0},{6,3},{7,2},{8,13},{9,12},{10,... | collective-permute-start | bytes 491528 | tf_op jit(solution)/shard_map/ppermute | solution.py:86
  84.7 2.8 %collective-permute-done.13.refs_1_ = f32[10,32,128]{2,1,0:T(8,128)S(1)} collective-permute-done((f32[10,32,128]{2,1,0:T(8,128)S(1)}, f32[10,32,128]{2,1,0:T(8,128)S(1)}, u32[]{:S(2)}, u32[]{:S(2)}) %collective-permute-start.13) | collective-permute-done | bytes 163872 | tf_op jit(solution)/shard_map/ppermute | solution.py:86
  87.5 2.0 %collective-permute-done.14.refs_2_ = f32[10,32,128]{2,1,0:T(8,128)S(1)} collective-permute-done((f32[10,32,128]{2,1,0:T(8,128)S(1)}, f32[10,32,128]{2,1,0:T(8,128)S(1)}, u32[]{:S(2)}, u32[]{:S(2)}) %collective-permute-start.14) | collective-permute-done | bytes 163872 | tf_op jit(solution)/shard_map/ppermute | solution.py:86
  89.5 2.7 %collective-permute-done.15.refs_3_ = f32[10,32,128]{2,1,0:T(8,128)S(1)} collective-permute-done((f32[10,32,128]{2,1,0:T(8,128)S(1)}, f32[10,32,128]{2,1,0:T(8,128)S(1)}, u32[]{:S(2)}, u32[]{:S(2)}) %collective-permute-start.15) | collective-permute-done | bytes 163872 | tf_op jit(solution)/shard_map/ppermute | solution.py:86
  92.2 0.9 place_kernel.1
Async XLA Ops:
  1.3 12.5 %collective-permute-start.1 = (f32[10,88,128]{2,1,0:T(8,128)S(1)}, f32[10,88,128]{2,1,0:T(8,128)S(1)}, u32[]{:S(2)}, u32[]{:S(2)}) collective-permute-start(f32[10,88,128]{2,1,0:T(8,128)S(1)} %get-tuple-element.35), channel_id=1, source_target_pairs={{0,4},{1,5},{2,6},{3,7},{4,0},{5,1},{6,2},{7,3},{8,12},{9,13},{10,... | collective-permute-start | bytes 1351688 | tf_op jit(solution)/shard_map/ppermute | solution.py:86
  2.9 10.9 %collective-permute-start = (f32[10,80,128]{2,1,0:T(8,128)S(1)}, f32[10,80,128]{2,1,0:T(8,128)S(1)}, u32[]{:S(2)}, u32[]{:S(2)}) collective-permute-start(f32[10,80,128]{2,1,0:T(8,128)S(1)} %get-tuple-element.34), channel_id=1, source_target_pairs={{0,1},{1,0},{2,3},{3,2},{4,5},{5,4},{6,7},{7,6},{8,9},{9,8},{10,11... | collective-permute-start | bytes 1228808 | tf_op jit(solution)/shard_map/ppermute | solution.py:86
  13.8 10.0 %collective-permute-start.2 = (f32[10,80,128]{2,1,0:T(8,128)S(1)}, f32[10,80,128]{2,1,0:T(8,128)S(1)}, u32[]{:S(2)}, u32[]{:S(2)}) collective-permute-start(f32[10,80,128]{2,1,0:T(8,128)S(1)} %collective-permute-done.refs_0_), channel_id=1, source_target_pairs={{0,8},{1,9},{2,10},{3,11},{4,12},{5,13},{6,14},{7,15},{8,0},{9,1},... | collective-permute-start | bytes 1228808 | tf_op jit(solution)/shard_map/ppermute | solution.py:86
  15.5 18.6 %collective-permute-start.6 = (f32[2,10,80,128]{3,2,1,0:T(8,128)S(1)}, f32[2,10,80,128]{3,2,1,0:T(8,128)S(1)}, u32[]{:S(2)}, u32[]{:S(2)}) collective-permute-start(f32[2,10,80,128]{3,2,1,0:T(8,128)S(1)} %mix_kernel.1), channel_id=1, source_target_pairs={{0,1},{1,0},{2,3},{3,2},{4,5},{5,4},{6,7},{7,6},{8,9},{9,8},{10,11... | collective-permute-start | bytes 2457608 | tf_op jit(solution)/shard_map/ppermute | solution.py:86
  16.1 9.5 %collective-permute-start.5 = (f32[10,96,128]{2,1,0:T(8,128)S(1)}, f32[10,96,128]{2,1,0:T(8,128)S(1)}, u32[]{:S(2)}, u32[]{:S(2)}) collective-permute-start(f32[10,96,128]{2,1,0:T(8,128)S(1)} %get-tuple-element.37), channel_id=1, source_target_pairs={{24,1},{25,0},{28,5},{29,4}} | collective-permute-start | bytes 1474568 | tf_op jit(solution)/shard_map/ppermute | solution.py:86
  16.8 8.8 %collective-permute-start.3 = (f32[10,80,128]{2,1,0:T(8,128)S(1)}, f32[10,80,128]{2,1,0:T(8,128)S(1)}, u32[]{:S(2)}, u32[]{:S(2)}) collective-permute-start(f32[10,80,128]{2,1,0:T(8,128)S(1)} %collective-permute-done.refs_0_), channel_id=1, source_target_pairs={{0,2},{1,3},{2,0},{3,1},{4,6},{5,7},{6,4},{7,5},{8,10},{9,11},{10,... | collective-permute-start | bytes 1228808 | tf_op jit(solution)/shard_map/ppermute | solution.py:86
  23.9 1.8 %collective-permute-start.4 = (f32[10,80,128]{2,1,0:T(8,128)S(1)}, f32[10,80,128]{2,1,0:T(8,128)S(1)}, u32[]{:S(2)}, u32[]{:S(2)}) collective-permute-start(f32[10,80,128]{2,1,0:T(8,128)S(1)} %collective-permute-done.2.refs_1_), channel_id=1, source_target_pairs={{0,2},{1,3},{2,0},{3,1},{4,6},{5,7},{6,4},{7,5},{8,10},{9,11},{10,... | collective-permute-start | bytes 1228808 | tf_op jit(solution)/shard_map/ppermute | solution.py:86
  34.5 18.4 %collective-permute-start.7 = (f32[2,20,64,128]{3,2,1,0:T(8,128)S(1)}, f32[2,20,64,128]{3,2,1,0:T(8,128)S(1)}, u32[]{:S(2)}, u32[]{:S(2)}) collective-permute-start(f32[2,20,64,128]{3,2,1,0:T(8,128)S(1)} %get-tuple-element.45), channel_id=1, source_target_pairs={{0,2},{1,3},{2,0},{3,1},{4,6},{5,7},{6,4},{7,5},{8,10},{9,11},{10,... | collective-permute-start | bytes 3932168 | tf_op jit(solution)/shard_map/ppermute | solution.py:86
  46.1 1.7 %collective-permute-start.8 = (f32[10,64,128]{2,1,0:T(8,128)S(1)}, f32[10,64,128]{2,1,0:T(8,128)S(1)}, u32[]{:S(2)}, u32[]{:S(2)}) collective-permute-start(f32[10,64,128]{2,1,0:T(8,128)S(1)} %get-tuple-element.50), channel_id=1, source_target_pairs={{0,2},{1,3},{2,0},{3,1},{4,6},{5,7},{6,4},{7,5},{8,10},{9,11},{10,... | collective-permute-start | bytes 983048 | tf_op jit(solution)/shard_map/ppermute | solution.py:86
  47.9 26.9 %collective-permute-start.11 = (f32[10,56,128]{2,1,0:T(8,128)S(1)}, f32[10,56,128]{2,1,0:T(8,128)S(1)}, u32[]{:S(2)}, u32[]{:S(2)}) collective-permute-start(f32[10,56,128]{2,1,0:T(8,128)S(1)} %get-tuple-element.53), channel_id=1, source_target_pairs={{0,24},{1,25},{2,26},{3,27},{4,28},{5,29},{6,30},{7,31}} | collective-permute-start | bytes 860168 | tf_op jit(solution)/shard_map/ppermute | solution.py:86
  48.6 26.2 %collective-permute-start.10 = (f32[10,48,128]{2,1,0:T(8,128)S(1)}, f32[10,48,128]{2,1,0:T(8,128)S(1)}, u32[]{:S(2)}, u32[]{:S(2)}) collective-permute-start(f32[10,48,128]{2,1,0:T(8,128)S(1)} %get-tuple-element.52), channel_id=1, source_target_pairs={{0,16},{1,17},{2,18},{3,19},{4,20},{5,21},{6,22},{7,23},{8,24},{9,... | collective-permute-start | bytes 737288 | tf_op jit(solution)/shard_map/ppermute | solution.py:86
  49.9 24.9 %collective-permute-start.9 = (f32[10,40,128]{2,1,0:T(8,128)S(1)}, f32[10,40,128]{2,1,0:T(8,128)S(1)}, u32[]{:S(2)}, u32[]{:S(2)}) collective-permute-start(f32[10,40,128]{2,1,0:T(8,128)S(1)} %get-tuple-element.51), channel_id=1, source_target_pairs={{0,8},{1,9},{2,10},{3,11},{4,12},{5,13},{6,14},{7,15},{8,16},{9,17... | collective-permute-start | bytes 614408 | tf_op jit(solution)/shard_map/ppermute | solution.py:86
  77.3 1.9 %collective-permute-start.12 = (f32[20,48,128]{2,1,0:T(8,128)S(1)}, f32[20,48,128]{2,1,0:T(8,128)S(1)}, u32[]{:S(2)}, u32[]{:S(2)}) collective-permute-start(f32[20,48,128]{2,1,0:T(8,128)S(1)} %start_kernel.1.share), channel_id=1, source_target_pairs={{0,2},{1,3},{2,0},{3,1},{4,6},{5,7},{6,4},{7,5},{8,10},{9,11},{10,... | collective-permute-start | bytes 1474568 | tf_op jit(solution)/shard_map/ppermute | solution.py:86
  81.2 6.4 %collective-permute-start.13 = (f32[10,32,128]{2,1,0:T(8,128)S(1)}, f32[10,32,128]{2,1,0:T(8,128)S(1)}, u32[]{:S(2)}, u32[]{:S(2)}) collective-permute-start(f32[10,32,128]{2,1,0:T(8,128)S(1)} %get-tuple-element.56), channel_id=1, source_target_pairs={{0,4},{1,5},{2,6},{3,7},{4,0},{5,1},{6,2},{7,3},{8,12},{9,13},{10,... | collective-permute-start | bytes 491528 | tf_op jit(solution)/shard_map/ppermute | solution.py:86
  82.5 7.1 %collective-permute-start.14 = (f32[10,32,128]{2,1,0:T(8,128)S(1)}, f32[10,32,128]{2,1,0:T(8,128)S(1)}, u32[]{:S(2)}, u32[]{:S(2)}) collective-permute-start(f32[10,32,128]{2,1,0:T(8,128)S(1)} %get-tuple-element.57), channel_id=1, source_target_pairs={{0,1},{1,0},{2,3},{3,2},{4,5},{5,4},{6,7},{7,6},{8,9},{9,8},{10,11... | collective-permute-start | bytes 491528 | tf_op jit(solution)/shard_map/ppermute | solution.py:86
  83.2 9.0 %collective-permute-start.15 = (f32[10,32,128]{2,1,0:T(8,128)S(1)}, f32[10,32,128]{2,1,0:T(8,128)S(1)}, u32[]{:S(2)}, u32[]{:S(2)}) collective-permute-start(f32[10,32,128]{2,1,0:T(8,128)S(1)} %get-tuple-element.58), channel_id=1, source_target_pairs={{0,5},{1,4},{2,7},{3,6},{4,1},{5,0},{6,3},{7,2},{8,13},{9,12},{10,... | collective-permute-start | bytes 491528 | tf_op jit(solution)/shard_map/ppermute | solution.py:86

commit v4 on v3

--- a/solution.py
+++ b/solution.py
@@ -167,7 +167,8 @@
             for layer in range(plan.layers):
                 if layer % 2 == 0:
                     moved = pltpu.matmul_pop(sums[which][layer // 2])
-                    shift(later, later_set, layer // 2)
+                    if later is not None:
+                        shift(later, later_set, layer // 2)
                 part = moved[layer % 2 * TILE : (layer % 2 + 1) * TILE]
                 high = source[layer + 2, here, :]
                 x_low = source[layer + 1, pl.ds(row + TILE - 1, TILE), :]
@@ -185,27 +186,12 @@
                 target[layer + 1, here, :] = fresh
                 low, mid = mid, high
 
-        sets = next(k for k in range(SETS, 1, -1) if strips % k == 0 or k == 2)
-        ahead = sets - 1
-
-        def bounded(index):
-            return jnp.minimum(index, strips - 1)
-
+        ahead = min(SETS - 1, strips)
         for index in range(ahead):
             for pair in range(count):
-                shift(bounded(index), index, pair)
-
-        def some(index, _):
-            for which in range(sets):
-                strip(
-                    bounded(index * sets + which), which, bounded(index * sets + which + ahead), (which + ahead) % sets
-                )
-            return 0
-
-        lax.fori_loop(0, -(-strips // sets), some, 0)
-        for index in range(ahead):
-            for pair in range(count):
-                pltpu.matmul_pop(sums[index][pair])
+                shift(index, index, pair)
+        for index in range(strips):
+            strip(index, index % SETS, index + ahead if index + ahead < strips else None, (index + ahead) % SETS)
 
     return step
 
@@ -214,13 +200,28 @@
     return lambda layer, row: field[layer + 1, pl.ds(pl.multiple_of(row + TILE, TILE), TILE), :]
 
 
+def repeat(step, now, spare, halos, scale):
+    for _, same in itertools.groupby(halos, key=rounded):
+        same = list(same)
+
+        def twice(_, carry, halo=same[0], now=now, spare=spare):
+            step(now, spare, halo, scale)
+            step(spare, now, halo, scale)
+            return carry
+
+        if len(same) > 1:
+            lax.fori_loop(0, len(same) // 2, twice, 0)
+        if len(same) % 2:
+            step(now, spare, same[-1], scale)
+            now, spare = spare, now
+    return now, spare
+
+
 def fine(step, source, one, two, halo, minus=None):
-    now, turn = source, (one, two)
-    for index in range(STEPS):
-        last = index == STEPS - 1
-        step(now, turn[index % 2], halo - 1 - index, 1.0, minus=minus if last else None)
-        now = turn[index % 2]
-    return now
+    step(source, one, halo - 1, 1.0)
+    now, spare = repeat(step, one, two, range(halo - 2, halo - STEPS, -1), 1.0)
+    step(now, spare, halo - STEPS, 1.0, minus=minus)
+    return spare
 
 
 def clear(plan, *fields):
@@ -403,11 +404,9 @@
         def body(sums):
             step = stepper(plan, place, coeff, sums)
             clear(plan, ahead, one)
-            now, turn, reach = seed, (ahead, one), STEPS + plan.n_t - 1
-            for index in range(GROUP - 1):
-                reach -= 1
-                step(now, turn[index % 2], reach, RATIO)
-                now = turn[index % 2]
+            reach = STEPS + plan.n_t - 2
+            step(seed, ahead, reach, RATIO)
+            now, _ = repeat(step, ahead, one, range(reach - 1, reach - GROUP + 1, -1), RATIO)
             if now is one:
                 ahead[...] = one[...]
 
@@ -474,16 +473,10 @@
     core = place.core
     clear(plan, one, two, three)
     middle = pl.ds(pl.multiple_of(place.inner(plan.mid) + TILE, TILE), plan.width_of(plan.mid))
+    chunk = pl.ds(pl.multiple_of(place.inner(0) + TILE, TILE), plan.chunk)
 
     def body(sums):
         step = stepper(plan, place, coeff, sums)
-
-        def term(source, coarse, other, reach, out, halo):
-            step(source, coarse, reach - 1, RATIO)
-            result = fine(step, source, other, source, reach, minus=field_at(coarse))
-            rows = pl.ds(pl.multiple_of(place.inner(halo) + TILE, TILE), plan.width_of(halo))
-            for layer in range(plan.layers):
-                out[layer] = result[layer + 1, rows, :]
 
         def load(block, target):
             @pl.when(core == block % 2)
@@ -495,25 +488,31 @@
                 for layer in range(plan.layers):
                     target[layer + 1, middle, :] = flipped[block // 2, layer]
 
-        def block_term(block):
+        def slot_terms(slot, _):
+            last = 2 * slot + core
             load(0, one)
-            left = STEPS + block - 1
-            now, spare = one, two
-            for before in range(1, block):
-                load(before, three)
-                left -= 1
-                step(now, spare, left, RATIO, plus=field_at(three))
-                now, spare = spare, now
-            term(now, three, spare, left, terms.at[block // 2], 0)
-
-        for block in range(GROUP):
-
-            @pl.when(core == block % 2)
-            def _(block=block):
-                if block == 0:
-                    terms[0] = jnp.zeros_like(terms[0])
-                else:
-                    block_term(block)
+            for before in range(1, GROUP - 1):
+
+                @pl.when(before < last)
+                def _(before=before):
+                    load(before, three)
+                    step(one, two, STEPS + GROUP - 2 - before, RATIO, plus=field_at(three))
+                    one[...] = two[...]
+
+            @pl.when(last > 0)
+            def _():
+                step(one, three, STEPS - 1, RATIO)
+                result = fine(step, one, two, one, STEPS, minus=field_at(three))
+                for layer in range(plan.layers):
+                    terms[slot, layer] = result[layer + 1, chunk, :]
+
+            @pl.when(last == 0)
+            def _():
+                terms[0] = jnp.zeros_like(terms[0])
+
+            return 0
+
+        lax.fori_loop(0, plan.pairs, slot_terms, 0)
 
         started = (place.z == 0) & (core == 0)
 
@@ -552,9 +551,7 @@
                     index = 1 + place.core * plan.side + layer
                     now[index, rows, :] = now[index, rows, :] + totals[distance - 1][layer]
                 if distance > 1:
-                    for turn in range(GROUP):
-                        source, target = (now, spare) if turn % 2 == 0 else (spare, now)
-                        step(source, target, reach - 1 - turn, RATIO)
+                    repeat(step, now, spare, range(reach - 1, reach - 1 - GROUP, -1), RATIO)
 
         rows = pl.ds(pl.multiple_of(place.inner(TILE) + TILE, TILE), plan.width_of(TILE))
         for layer in range(plan.layers):
@@ -655,8 +652,8 @@
         plan, own_cut_kernel, 60, [piece, window, (4, *piece)], [], guess, initial, diffusivity, velocity, copies=4, whole=4
     )
     coeffs, inits, beside = got[:sides], got[sides : 2 * sides], got[2 * sides :]
-    got = lax.optimization_barrier((*coeffs, *beside, *own_sent))
-    coeffs, beside, own_sent = got[:sides], got[sides:-sides], got[-sides:]
+    got = lax.optimization_barrier((*coeffs, *own_sent, *beside))
+    coeffs, own_sent, beside = got[:sides], got[sides : 2 * sides], got[2 * sides :]
     mixed = call(plan, mix_kernel, 0.3, [(plan.pairs, *piece)] * sides, [], *own_sent, *beside)
     distant = [plan.send(part, ds=ds) for ds, part in enumerate(mixed, 1)]
     swapped = []

time: 93.6 us -> 90.7 us (0.969)
  Pallas kernels: 29.8 us -> 25.8 us
    pallas_call x12, Pallas kernels: 29.8 us -> 25.8 us  [call(): pl.pallas_call(functools.partial(kernel, plan), out_shape=[held(shape, jn...]
    ppermute x16, waiting for transfers between devices: 49.4 us -> 50.3 us  [send(): return lax.ppermute(value, ('tm', 'space'), pairs)]
  transfers between devices with their start and end apart: 16 -> 16, of which waited for: 9 -> 9; matrix products, arithmetic and copies ran while one was open for 0% -> 0% of each run, Pallas kernels for 24% -> 22%
where the time goes in v4:
time: 90.7 us; the launch traced here: 90.4 us
  waiting for transfers between devices  50.3 us (55%)
  Pallas kernels  25.8 us (28%)
  starting transfers between devices  14 us (15%)
    ppermute x16, waiting for transfers between devices, send(): return lax.ppermute(value, ('tm', 'space'), pairs)  50.3 us
    pallas_call x12, Pallas kernels, call(): pl.pallas_call(functools.partial(kernel, plan), out_shape=[held(shape, jn...  25.8 us
    ppermute x16, starting transfers between devices, send(): return lax.ppermute(value, ('tm', 'space'), pairs)  14 us
  transfers between devices with their start and end apart: 16, of which 9 were waited for; matrix products, arithmetic and copies ran while one was open for 0% of the time, Pallas kernels for 22%

profile of v4, /device:TPU:18, one launch (start us, length us, event | category | flops | bytes accessed | tf_op | source)
XLA Modules:
  0.0 90.4 jit_solution(9822683531814962675)
XLA Ops:
  0.0 1.3 %first_cut_kernel.1 = (f32[10,80,128]{2,1,0:T(8,128)S(1)}, f32[10,96,128]{2,1,0:T(8,128)S(1)}, f32[10,88,128]{2,1,0:T(8,128)S(1)}) custom-call(f32[1,10,128,128]{3,2,1,0:T(8,128)} %guess.5, f32[10,128,128]{2,1,0:T(8,128)} %initial.3, f32[10,128,128]{2,1,0:T(8,128)} %diff.3, f32[3,10,128,128]{3,2,1,0:T(8,128)} %vel.3), custom_call_target="tpu_custom_call" | custom-call | bytes 7200000 | tf_op jit(solution)/shard_map/first_cut_kernel/pallas_call | solution.py:614
  1.3 1.6 %collective-permute-start.1 = (f32[10,88,128]{2,1,0:T(8,128)S(1)}, f32[10,88,128]{2,1,0:T(8,128)S(1)}, u32[]{:S(2)}, u32[]{:S(2)}) collective-permute-start(f32[10,88,128]{2,1,0:T(8,128)S(1)} %get-tuple-element.35), channel_id=1, source_target_pairs={{0,4},{1,5},{2,6},{3,7},{4,0},{5,1},{6,2},{7,3},{8,12},{9,13},{10,... | collective-permute-start | bytes 1351688 | tf_op jit(solution)/shard_map/ppermute | solution.py:86
  2.9 0.5 collective-permute-start
  3.4 1.0 %second_cut_kernel.1.refs_0_ = f32[10,80,128]{2,1,0:T(8,128)S(1)} custom-call(f32[1,10,128,128]{3,2,1,0:T(8,128)} %guess.5), custom_call_target="tpu_custom_call" | custom-call | bytes 3600000 | tf_op jit(solution)/shard_map/second_cut_kernel/pallas_call | solution.py:614
  4.5 9.4 %collective-permute-done.refs_0_ = f32[10,80,128]{2,1,0:T(8,128)S(1)} collective-permute-done((f32[10,80,128]{2,1,0:T(8,128)S(1)}, f32[10,80,128]{2,1,0:T(8,128)S(1)}, u32[]{:S(2)}, u32[]{:S(2)}) %collective-permute-start) | collective-permute-done | bytes 409632 | tf_op jit(solution)/shard_map/ppermute | solution.py:86
  13.8 0.0 collective-permute-done.1.refs_1_.refs_0_
  13.8 1.6 %collective-permute-start.2 = (f32[10,80,128]{2,1,0:T(8,128)S(1)}, f32[10,80,128]{2,1,0:T(8,128)S(1)}, u32[]{:S(2)}, u32[]{:S(2)}) collective-permute-start(f32[10,80,128]{2,1,0:T(8,128)S(1)} %collective-permute-done.refs_0_), channel_id=1, source_target_pairs={{0,8},{1,9},{2,10},{3,11},{4,12},{5,13},{6,14},{7,15},{8,0},{9,1},... | collective-permute-start | bytes 1228808 | tf_op jit(solution)/shard_map/ppermute | solution.py:86
  15.4 0.1 mix_kernel.1
  15.5 0.6 collective-permute-start.6
  16.1 0.7 collective-permute-start.5
  16.8 0.1 collective-permute-start.3
  16.8 7.0 %collective-permute-done.2.refs_1_ = f32[10,80,128]{2,1,0:T(8,128)S(1)} collective-permute-done((f32[10,80,128]{2,1,0:T(8,128)S(1)}, f32[10,80,128]{2,1,0:T(8,128)S(1)}, u32[]{:S(2)}, u32[]{:S(2)}) %collective-permute-start.2) | collective-permute-done | bytes 409632 | tf_op jit(solution)/shard_map/ppermute | solution.py:86
  23.9 0.0 collective-permute-start.4
  23.9 1.7 %own_cut_kernel.1 = (f32[10,80,128]{2,1,0:T(8,128)S(1)}, f32[10,96,128]{2,1,0:T(8,128)S(1)}, f32[4,10,80,128]{3,2,1,0:T(8,128)S(1)}) custom-call(f32[1,10,128,128]{3,2,1,0:T(8,128)} %guess.5, f32[10,128,128]{2,1,0:T(8,128)} %initial.3, f32[10,128,128]{2,1,0:T(8,128)} %diff.3, f32[3,10,128,128]{3,2,1,0:T(8,128)} %vel.3), custom_call_target="tpu_custom_call" | custom-call | bytes 216000000 | tf_op jit(solution)/shard_map/own_cut_kernel/pallas_call | solution.py:614
  25.6 0.0 collective-permute-done.5.refs_4_
  25.6 0.0 collective-permute-done.3.refs_2_
  25.6 0.0 collective-permute-done.4.refs_3_
  25.6 1.1 %weight_kernel.1 = (f32[7,20,80,128]{3,2,1,0:T(8,128)S(1)}, f32[22,96,128]{2,1,0:T(8,128)S(1)}, f32[22,96,128]{2,1,0:T(8,128)S(1)}) custom-call(f32[4,10,80,128]{3,2,1,0:T(8,128)S(1)} %get-tuple-element.32.coeff_own, f32[10,96,128]{2,1,0:T(8,128)S(1)} %get-tuple-element.33.window, f32[10,80,128]{2,1,0:T(8,128)S(1)} %collective-permute-done.refs_0_, ...), custom_call_target="tpu_custom_call" | custom-call | bytes 10800000 | tf_op jit(solution)/shard_map/weight_kernel/pallas_call | solution.py:614
  26.7 7.3 %collective-permute-done.6.refs_1_ = f32[2,10,80,128]{3,2,1,0:T(8,128)S(1)} collective-permute-done((f32[2,10,80,128]{3,2,1,0:T(8,128)S(1)}, f32[2,10,80,128]{3,2,1,0:T(8,128)S(1)}, u32[]{:S(2)}, u32[]{:S(2)}) %collective-permute-start.6) | collective-permute-done | bytes 819232 | tf_op jit(solution)/shard_map/ppermute | solution.py:86
  34.1 0.4 field_kernel.1
  34.5 0.1 collective-permute-start.7
  34.5 9.5 %total_kernel.1 = (f32[10,64,128]{2,1,0:T(8,128)S(1)}, f32[10,64,128]{2,1,0:T(8,128)S(1)}) custom-call(f32[7,20,80,128]{3,2,1,0:T(8,128)S(1)} %get-tuple-element.41.coeff, f32[22,96,128]{2,1,0:T(8,128)S(1)} %get-tuple-element.48.ahead, f32[2,22,96,128]{3,2,1,0:T(8,128)S(1)} %get-tuple-element.44.fields), custom_call_target="tpu_custom_call" | custom-call | bytes 54000000 | tf_op jit(solution)/shard_map/total_kernel/pallas_call | solution.py:614
  44.1 0.1 collective-permute-start.8
  44.2 1.6 %collective-permute-done.8.got = f32[10,64,128]{2,1,0:T(8,128)S(1)} collective-permute-done((f32[10,64,128]{2,1,0:T(8,128)S(1)}, f32[10,64,128]{2,1,0:T(8,128)S(1)}, u32[]{:S(2)}, u32[]{:S(2)}) %collective-permute-start.8) | collective-permute-done | bytes 327712 | tf_op jit(solution)/shard_map/ppermute | solution.py:86
  45.8 0.1 part_kernel.1
  45.9 0.7 collective-permute-start.11
  46.5 1.3 %collective-permute-start.10 = (f32[10,48,128]{2,1,0:T(8,128)S(1)}, f32[10,48,128]{2,1,0:T(8,128)S(1)}, u32[]{:S(2)}, u32[]{:S(2)}) collective-permute-start(f32[10,48,128]{2,1,0:T(8,128)S(1)} %get-tuple-element.52), channel_id=1, source_target_pairs={{0,16},{1,17},{2,18},{3,19},{4,20},{5,21},{6,22},{7,23},{8,24},{9,... | collective-permute-start | bytes 737288 | tf_op jit(solution)/shard_map/ppermute | solution.py:86
  47.9 3.2 %collective-permute-start.9 = (f32[10,40,128]{2,1,0:T(8,128)S(1)}, f32[10,40,128]{2,1,0:T(8,128)S(1)}, u32[]{:S(2)}, u32[]{:S(2)}) collective-permute-start(f32[10,40,128]{2,1,0:T(8,128)S(1)} %get-tuple-element.51), channel_id=1, source_target_pairs={{0,8},{1,9},{2,10},{3,11},{4,12},{5,13},{6,14},{7,15},{8,16},{9,17... | collective-permute-start | bytes 614408 | tf_op jit(solution)/shard_map/ppermute | solution.py:86
  51.0 0.0 collective-permute-done.7.flipped
  51.0 6.1 %term_kernel.1 = (f32[2,20,32,128]{3,2,1,0:T(8,128)S(1)}, f32[20,48,128]{2,1,0:T(8,128)S(1)}) custom-call(f32[7,20,80,128]{3,2,1,0:T(8,128)S(1)} %get-tuple-element.41.coeff, f32[2,22,96,128]{3,2,1,0:T(8,128)S(1)} %get-tuple-element.44.fields, f32[2,20,64,128]{3,2,1,0:T(8,128)S(1)} %collective-permute-done.7.flipped, f32[22,96,128]{2,1,0:T(8,128)S(1)} %get-tuple-element.46.seed), custom_call_target="tpu_custom_call" | custom-call | bytes 54000000 | tf_op jit(solution)/shard_map/term_kernel/pallas_call | solution.py:614
  57.1 15.7 %collective-permute-done.9.refs_0_ = f32[10,40,128]{2,1,0:T(8,128)S(1)} collective-permute-done((f32[10,40,128]{2,1,0:T(8,128)S(1)}, f32[10,40,128]{2,1,0:T(8,128)S(1)}, u32[]{:S(2)}, u32[]{:S(2)}) %collective-permute-start.9) | collective-permute-done | bytes 204832 | tf_op jit(solution)/shard_map/ppermute | solution.py:86
  72.8 0.0 collective-permute-done.10.refs_1_
  72.8 0.0 collective-permute-done.11.refs_2_
  72.8 2.1 %start_kernel.1.share = f32[20,48,128]{2,1,0:T(8,128)S(1)} custom-call(f32[7,20,80,128]{3,2,1,0:T(8,128)S(1)} %get-tuple-element.41.coeff, f32[20,48,128]{2,1,0:T(8,128)S(1)} %get-tuple-element.47.begun, f32[10,40,128]{2,1,0:T(8,128)S(1)} %collective-permute-done.9.refs_0_, f32[10,48,128]{2,1,0:T(8,128)S(1)} %collective-permute-done.10.refs_1_, ...), custom_call_target="tpu_custom_call" | custom-call | bytes 21600000 | tf_op jit(solution)/shard_map/start_kernel/pallas_call | solution.py:614
  74.9 0.1 collective-permute-start.12
  75.0 1.9 %collective-permute-done.12.other = f32[20,48,128]{2,1,0:T(8,128)S(1)} collective-permute-done((f32[20,48,128]{2,1,0:T(8,128)S(1)}, f32[20,48,128]{2,1,0:T(8,128)S(1)}, u32[]{:S(2)}, u32[]{:S(2)}) %collective-permute-start.12) | collective-permute-done | bytes 491552 | tf_op jit(solution)/shard_map/ppermute | solution.py:86
  76.8 1.5 %end_kernel.1 = (f32[10,32,128]{2,1,0:T(8,128)S(1)}, f32[10,32,128]{2,1,0:T(8,128)S(1)}, f32[10,32,128]{2,1,0:T(8,128)S(1)}, f32[10,32,128]{2,1,0:T(8,128)S(1)}) custom-call(f32[7,20,80,128]{3,2,1,0:T(8,128)S(1)} %get-tuple-element.41.coeff, f32[20,48,128]{2,1,0:T(8,128)S(1)} %start_kernel.1.share, f32[20,48,128]{2,1,0:T(8,128)S(1)} %collective-permute-done.12.other, ...), custom_call_target="tpu_custom_call" | custom-call | bytes 10800000 | tf_op jit(solution)/shard_map/end_kernel/pallas_call | solution.py:614
  78.4 1.3 %collective-permute-start.13 = (f32[10,32,128]{2,1,0:T(8,128)S(1)}, f32[10,32,128]{2,1,0:T(8,128)S(1)}, u32[]{:S(2)}, u32[]{:S(2)}) collective-permute-start(f32[10,32,128]{2,1,0:T(8,128)S(1)} %get-tuple-element.56), channel_id=1, source_target_pairs={{0,4},{1,5},{2,6},{3,7},{4,0},{5,1},{6,2},{7,3},{8,12},{9,13},{10,... | collective-permute-start | bytes 491528 | tf_op jit(solution)/shard_map/ppermute | solution.py:86
  79.7 0.7 collective-permute-start.14
  80.4 1.5 %collective-permute-start.15 = (f32[10,32,128]{2,1,0:T(8,128)S(1)}, f32[10,32,128]{2,1,0:T(8,128)S(1)}, u32[]{:S(2)}, u32[]{:S(2)}) collective-permute-start(f32[10,32,128]{2,1,0:T(8,128)S(1)} %get-tuple-element.58), channel_id=1, source_target_pairs={{0,5},{1,4},{2,7},{3,6},{4,1},{5,0},{6,3},{7,2},{8,13},{9,12},{10,... | collective-permute-start | bytes 491528 | tf_op jit(solution)/shard_map/ppermute | solution.py:86
  82.0 2.8 %collective-permute-done.13.refs_1_ = f32[10,32,128]{2,1,0:T(8,128)S(1)} collective-permute-done((f32[10,32,128]{2,1,0:T(8,128)S(1)}, f32[10,32,128]{2,1,0:T(8,128)S(1)}, u32[]{:S(2)}, u32[]{:S(2)}) %collective-permute-start.13) | collective-permute-done | bytes 163872 | tf_op jit(solution)/shard_map/ppermute | solution.py:86
  84.7 2.1 %collective-permute-done.14.refs_2_ = f32[10,32,128]{2,1,0:T(8,128)S(1)} collective-permute-done((f32[10,32,128]{2,1,0:T(8,128)S(1)}, f32[10,32,128]{2,1,0:T(8,128)S(1)}, u32[]{:S(2)}, u32[]{:S(2)}) %collective-permute-start.14) | collective-permute-done | bytes 163872 | tf_op jit(solution)/shard_map/ppermute | solution.py:86
  86.8 2.6 %collective-permute-done.15.refs_3_ = f32[10,32,128]{2,1,0:T(8,128)S(1)} collective-permute-done((f32[10,32,128]{2,1,0:T(8,128)S(1)}, f32[10,32,128]{2,1,0:T(8,128)S(1)}, u32[]{:S(2)}, u32[]{:S(2)}) %collective-permute-start.15) | collective-permute-done | bytes 163872 | tf_op jit(solution)/shard_map/ppermute | solution.py:86
  89.4 0.9 place_kernel.1
Async XLA Ops:
  1.3 12.5 %collective-permute-start.1 = (f32[10,88,128]{2,1,0:T(8,128)S(1)}, f32[10,88,128]{2,1,0:T(8,128)S(1)}, u32[]{:S(2)}, u32[]{:S(2)}) collective-permute-start(f32[10,88,128]{2,1,0:T(8,128)S(1)} %get-tuple-element.35), channel_id=1, source_target_pairs={{0,4},{1,5},{2,6},{3,7},{4,0},{5,1},{6,2},{7,3},{8,12},{9,13},{10,... | collective-permute-start | bytes 1351688 | tf_op jit(solution)/shard_map/ppermute | solution.py:86
  2.9 10.9 %collective-permute-start = (f32[10,80,128]{2,1,0:T(8,128)S(1)}, f32[10,80,128]{2,1,0:T(8,128)S(1)}, u32[]{:S(2)}, u32[]{:S(2)}) collective-permute-start(f32[10,80,128]{2,1,0:T(8,128)S(1)} %get-tuple-element.34), channel_id=1, source_target_pairs={{0,1},{1,0},{2,3},{3,2},{4,5},{5,4},{6,7},{7,6},{8,9},{9,8},{10,11... | collective-permute-start | bytes 1228808 | tf_op jit(solution)/shard_map/ppermute | solution.py:86
  13.8 10.0 %collective-permute-start.2 = (f32[10,80,128]{2,1,0:T(8,128)S(1)}, f32[10,80,128]{2,1,0:T(8,128)S(1)}, u32[]{:S(2)}, u32[]{:S(2)}) collective-permute-start(f32[10,80,128]{2,1,0:T(8,128)S(1)} %collective-permute-done.refs_0_), channel_id=1, source_target_pairs={{0,8},{1,9},{2,10},{3,11},{4,12},{5,13},{6,14},{7,15},{8,0},{9,1},... | collective-permute-start | bytes 1228808 | tf_op jit(solution)/shard_map/ppermute | solution.py:86
  15.5 18.6 %collective-permute-start.6 = (f32[2,10,80,128]{3,2,1,0:T(8,128)S(1)}, f32[2,10,80,128]{3,2,1,0:T(8,128)S(1)}, u32[]{:S(2)}, u32[]{:S(2)}) collective-permute-start(f32[2,10,80,128]{3,2,1,0:T(8,128)S(1)} %mix_kernel.1), channel_id=1, source_target_pairs={{0,1},{1,0},{2,3},{3,2},{4,5},{5,4},{6,7},{7,6},{8,9},{9,8},{10,11... | collective-permute-start | bytes 2457608 | tf_op jit(solution)/shard_map/ppermute | solution.py:86
  16.1 9.5 %collective-permute-start.5 = (f32[10,96,128]{2,1,0:T(8,128)S(1)}, f32[10,96,128]{2,1,0:T(8,128)S(1)}, u32[]{:S(2)}, u32[]{:S(2)}) collective-permute-start(f32[10,96,128]{2,1,0:T(8,128)S(1)} %get-tuple-element.37), channel_id=1, source_target_pairs={{24,1},{25,0},{28,5},{29,4}} | collective-permute-start | bytes 1474568 | tf_op jit(solution)/shard_map/ppermute | solution.py:86
  16.8 8.8 %collective-permute-start.3 = (f32[10,80,128]{2,1,0:T(8,128)S(1)}, f32[10,80,128]{2,1,0:T(8,128)S(1)}, u32[]{:S(2)}, u32[]{:S(2)}) collective-permute-start(f32[10,80,128]{2,1,0:T(8,128)S(1)} %collective-permute-done.refs_0_), channel_id=1, source_target_pairs={{0,2},{1,3},{2,0},{3,1},{4,6},{5,7},{6,4},{7,5},{8,10},{9,11},{10,... | collective-permute-start | bytes 1228808 | tf_op jit(solution)/shard_map/ppermute | solution.py:86
  23.9 1.8 %collective-permute-start.4 = (f32[10,80,128]{2,1,0:T(8,128)S(1)}, f32[10,80,128]{2,1,0:T(8,128)S(1)}, u32[]{:S(2)}, u32[]{:S(2)}) collective-permute-start(f32[10,80,128]{2,1,0:T(8,128)S(1)} %collective-permute-done.2.refs_1_), channel_id=1, source_target_pairs={{0,2},{1,3},{2,0},{3,1},{4,6},{5,7},{6,4},{7,5},{8,10},{9,11},{10,... | collective-permute-start | bytes 1228808 | tf_op jit(solution)/shard_map/ppermute | solution.py:86
  34.5 16.6 %collective-permute-start.7 = (f32[2,20,64,128]{3,2,1,0:T(8,128)S(1)}, f32[2,20,64,128]{3,2,1,0:T(8,128)S(1)}, u32[]{:S(2)}, u32[]{:S(2)}) collective-permute-start(f32[2,20,64,128]{3,2,1,0:T(8,128)S(1)} %get-tuple-element.45), channel_id=1, source_target_pairs={{0,2},{1,3},{2,0},{3,1},{4,6},{5,7},{6,4},{7,5},{8,10},{9,11},{10,... | collective-permute-start | bytes 3932168 | tf_op jit(solution)/shard_map/ppermute | solution.py:86
  44.1 1.7 %collective-permute-start.8 = (f32[10,64,128]{2,1,0:T(8,128)S(1)}, f32[10,64,128]{2,1,0:T(8,128)S(1)}, u32[]{:S(2)}, u32[]{:S(2)}) collective-permute-start(f32[10,64,128]{2,1,0:T(8,128)S(1)} %get-tuple-element.50), channel_id=1, source_target_pairs={{0,2},{1,3},{2,0},{3,1},{4,6},{5,7},{6,4},{7,5},{8,10},{9,11},{10,... | collective-permute-start | bytes 983048 | tf_op jit(solution)/shard_map/ppermute | solution.py:86
  45.9 26.9 %collective-permute-start.11 = (f32[10,56,128]{2,1,0:T(8,128)S(1)}, f32[10,56,128]{2,1,0:T(8,128)S(1)}, u32[]{:S(2)}, u32[]{:S(2)}) collective-permute-start(f32[10,56,128]{2,1,0:T(8,128)S(1)} %get-tuple-element.53), channel_id=1, source_target_pairs={{0,24},{1,25},{2,26},{3,27},{4,28},{5,29},{6,30},{7,31}} | collective-permute-start | bytes 860168 | tf_op jit(solution)/shard_map/ppermute | solution.py:86
  46.5 26.2 %collective-permute-start.10 = (f32[10,48,128]{2,1,0:T(8,128)S(1)}, f32[10,48,128]{2,1,0:T(8,128)S(1)}, u32[]{:S(2)}, u32[]{:S(2)}) collective-permute-start(f32[10,48,128]{2,1,0:T(8,128)S(1)} %get-tuple-element.52), channel_id=1, source_target_pairs={{0,16},{1,17},{2,18},{3,19},{4,20},{5,21},{6,22},{7,23},{8,24},{9,... | collective-permute-start | bytes 737288 | tf_op jit(solution)/shard_map/ppermute | solution.py:86
  47.9 24.9 %collective-permute-start.9 = (f32[10,40,128]{2,1,0:T(8,128)S(1)}, f32[10,40,128]{2,1,0:T(8,128)S(1)}, u32[]{:S(2)}, u32[]{:S(2)}) collective-permute-start(f32[10,40,128]{2,1,0:T(8,128)S(1)} %get-tuple-element.51), channel_id=1, source_target_pairs={{0,8},{1,9},{2,10},{3,11},{4,12},{5,13},{6,14},{7,15},{8,16},{9,17... | collective-permute-start | bytes 614408 | tf_op jit(solution)/shard_map/ppermute | solution.py:86
  74.9 1.9 %collective-permute-start.12 = (f32[20,48,128]{2,1,0:T(8,128)S(1)}, f32[20,48,128]{2,1,0:T(8,128)S(1)}, u32[]{:S(2)}, u32[]{:S(2)}) collective-permute-start(f32[20,48,128]{2,1,0:T(8,128)S(1)} %start_kernel.1.share), channel_id=1, source_target_pairs={{0,2},{1,3},{2,0},{3,1},{4,6},{5,7},{6,4},{7,5},{8,10},{9,11},{10,... | collective-permute-start | bytes 1474568 | tf_op jit(solution)/shard_map/ppermute | solution.py:86
  78.4 6.3 %collective-permute-start.13 = (f32[10,32,128]{2,1,0:T(8,128)S(1)}, f32[10,32,128]{2,1,0:T(8,128)S(1)}, u32[]{:S(2)}, u32[]{:S(2)}) collective-permute-start(f32[10,32,128]{2,1,0:T(8,128)S(1)} %get-tuple-element.56), channel_id=1, source_target_pairs={{0,4},{1,5},{2,6},{3,7},{4,0},{5,1},{6,2},{7,3},{8,12},{9,13},{10,... | collective-permute-start | bytes 491528 | tf_op jit(solution)/shard_map/ppermute | solution.py:86
  79.7 7.1 %collective-permute-start.14 = (f32[10,32,128]{2,1,0:T(8,128)S(1)}, f32[10,32,128]{2,1,0:T(8,128)S(1)}, u32[]{:S(2)}, u32[]{:S(2)}) collective-permute-start(f32[10,32,128]{2,1,0:T(8,128)S(1)} %get-tuple-element.57), channel_id=1, source_target_pairs={{0,1},{1,0},{2,3},{3,2},{4,5},{5,4},{6,7},{7,6},{8,9},{9,8},{10,11... | collective-permute-start | bytes 491528 | tf_op jit(solution)/shard_map/ppermute | solution.py:86
  80.4 9.0 %collective-permute-start.15 = (f32[10,32,128]{2,1,0:T(8,128)S(1)}, f32[10,32,128]{2,1,0:T(8,128)S(1)}, u32[]{:S(2)}, u32[]{:S(2)}) collective-permute-start(f32[10,32,128]{2,1,0:T(8,128)S(1)} %get-tuple-element.58), channel_id=1, source_target_pairs={{0,5},{1,4},{2,7},{3,6},{4,1},{5,0},{6,3},{7,2},{8,13},{9,12},{10,... | collective-permute-start | bytes 491528 | tf_op jit(solution)/shard_map/ppermute | solution.py:86

commit v5 on v4

--- a/solution.py
+++ b/solution.py
@@ -148,6 +148,7 @@
     def step(source, target, halo, scale, plus=None, minus=None):
         first = place.inner(halo)
         strips = plan.width_of(halo) // TILE
+        own = 0 if scale == 1.0 else 7
 
         def rows(index):
             return pl.multiple_of(first + index * TILE, TILE)
@@ -173,12 +174,12 @@
                 high = source[layer + 2, here, :]
                 x_low = source[layer + 1, pl.ds(row + TILE - 1, TILE), :]
                 x_high = source[layer + 1, pl.ds(row + TILE + 1, TILE), :]
-                change = (coeff[0, layer, inner, :] * mid + coeff[1, layer, inner, :] * low) + (
+                change = (coeff[own, layer, inner, :] * mid + coeff[1, layer, inner, :] * low) + (
                     coeff[2, layer, inner, :] * high + coeff[3, layer, inner, :] * x_low
                 )
                 change = change + (coeff[4, layer, inner, :] * x_high + coeff[5, layer, inner, :] * part[:, : plan.lanes])
                 change = change + coeff[6, layer, inner, :] * part[:, plan.lanes :]
-                fresh = mid + change if scale == 1.0 else mid + scale * change
+                fresh = change if scale == 1.0 else scale * change
                 if plus is not None:
                     fresh = fresh + plus(layer, row)
                 if minus is not None:
@@ -373,7 +374,8 @@
                     above = jnp.where(lane == plan.lanes - 1, 0.0, above)
                 coeff[1 + 2 * k, index] = below
                 coeff[2 + 2 * k, index] = above
-            coeff[0, index] = -total
+            coeff[0, index] = 1.0 - total
+            coeff[7, index] = 1.0 / RATIO - total
             return 0
 
         lax.fori_loop(0, plan.depth, layer_weights, 0)
@@ -533,6 +535,7 @@
 
 def start_kernel(plan, coeff, begun, *refs):
     *totals, out, one, two = refs
+    totals = totals[::-1]
     place = Place(plan)
     clear(plan, one, two)
 
@@ -668,7 +671,7 @@
         plan,
         weight_kernel,
         3,
-        [(7, plan.layers, width, lanes), box, box],
+        [(8, plan.layers, width, lanes), box, box],
         [(sides, 4, *piece), box],
         coeff_own,
         initial_own,
@@ -697,7 +700,7 @@
         keep,
         plan.send(give, flip=True),
     )
-    mine = [plan.send(part, dz=distance) for distance, part in enumerate(parts, 1)]
+    mine = [plan.send(parts[distance - 1], dz=distance) for distance in range(len(parts), 0, -1)]
     terms, begun = call(
         plan,
         term_kernel,

time: 90.7 us -> 90.2 us (level)
  transfers between devices with their start and end apart: 16 -> 16, of which waited for: 9 -> 9; matrix products, arithmetic and copies ran while one was open for 0% -> 0% of each run, Pallas kernels for 22% -> 21%
where the time goes in v5:
time: 90.2 us; the launch traced here: 89.9 us
  waiting for transfers between devices  50.5 us (56%)
  Pallas kernels  25.1 us (28%)
  starting transfers between devices  13.9 us (15%)
    ppermute x16, waiting for transfers between devices, send(): return lax.ppermute(value, ('tm', 'space'), pairs)  50.5 us
    pallas_call x12, Pallas kernels, call(): pl.pallas_call(functools.partial(kernel, plan), out_shape=[held(shape, jn...  25.1 us
    ppermute x16, starting transfers between devices, send(): return lax.ppermute(value, ('tm', 'space'), pairs)  13.9 us
  transfers between devices with their start and end apart: 16, of which 9 were waited for; matrix products, arithmetic and copies ran while one was open for 0% of the time, Pallas kernels for 21%

profile of v5, /device:TPU:18, one launch (start us, length us, event | category | flops | bytes accessed | tf_op | source)
XLA Modules:
  0.0 89.9 jit_solution(11959295432535138658)
XLA Ops:
  0.0 1.3 %first_cut_kernel.1 = (f32[10,80,128]{2,1,0:T(8,128)S(1)}, f32[10,96,128]{2,1,0:T(8,128)S(1)}, f32[10,88,128]{2,1,0:T(8,128)S(1)}) custom-call(f32[1,10,128,128]{3,2,1,0:T(8,128)} %guess.5, f32[10,128,128]{2,1,0:T(8,128)} %initial.3, f32[10,128,128]{2,1,0:T(8,128)} %diff.3, f32[3,10,128,128]{3,2,1,0:T(8,128)} %vel.3), custom_call_target="tpu_custom_call" | custom-call | bytes 7200000 | tf_op jit(solution)/shard_map/first_cut_kernel/pallas_call | solution.py:617
  1.3 1.6 %collective-permute-start.1 = (f32[10,88,128]{2,1,0:T(8,128)S(1)}, f32[10,88,128]{2,1,0:T(8,128)S(1)}, u32[]{:S(2)}, u32[]{:S(2)}) collective-permute-start(f32[10,88,128]{2,1,0:T(8,128)S(1)} %get-tuple-element.35), channel_id=1, source_target_pairs={{0,4},{1,5},{2,6},{3,7},{4,0},{5,1},{6,2},{7,3},{8,12},{9,13},{10,... | collective-permute-start | bytes 1351688 | tf_op jit(solution)/shard_map/ppermute | solution.py:86
  2.9 0.5 collective-permute-start
  3.4 1.0 %second_cut_kernel.1.refs_0_ = f32[10,80,128]{2,1,0:T(8,128)S(1)} custom-call(f32[1,10,128,128]{3,2,1,0:T(8,128)} %guess.5), custom_call_target="tpu_custom_call" | custom-call | bytes 3600000 | tf_op jit(solution)/shard_map/second_cut_kernel/pallas_call | solution.py:617
  4.5 9.4 %collective-permute-done.refs_0_ = f32[10,80,128]{2,1,0:T(8,128)S(1)} collective-permute-done((f32[10,80,128]{2,1,0:T(8,128)S(1)}, f32[10,80,128]{2,1,0:T(8,128)S(1)}, u32[]{:S(2)}, u32[]{:S(2)}) %collective-permute-start) | collective-permute-done | bytes 409632 | tf_op jit(solution)/shard_map/ppermute | solution.py:86
  13.8 0.0 collective-permute-done.1.refs_1_.refs_0_
  13.8 1.6 %collective-permute-start.2 = (f32[10,80,128]{2,1,0:T(8,128)S(1)}, f32[10,80,128]{2,1,0:T(8,128)S(1)}, u32[]{:S(2)}, u32[]{:S(2)}) collective-permute-start(f32[10,80,128]{2,1,0:T(8,128)S(1)} %collective-permute-done.refs_0_), channel_id=1, source_target_pairs={{0,8},{1,9},{2,10},{3,11},{4,12},{5,13},{6,14},{7,15},{8,0},{9,1},... | collective-permute-start | bytes 1228808 | tf_op jit(solution)/shard_map/ppermute | solution.py:86
  15.4 0.1 mix_kernel.1
  15.5 0.6 collective-permute-start.6
  16.1 0.7 collective-permute-start.5
  16.8 0.1 collective-permute-start.3
  16.8 7.0 %collective-permute-done.2.refs_1_ = f32[10,80,128]{2,1,0:T(8,128)S(1)} collective-permute-done((f32[10,80,128]{2,1,0:T(8,128)S(1)}, f32[10,80,128]{2,1,0:T(8,128)S(1)}, u32[]{:S(2)}, u32[]{:S(2)}) %collective-permute-start.2) | collective-permute-done | bytes 409632 | tf_op jit(solution)/shard_map/ppermute | solution.py:86
  23.9 0.0 collective-permute-start.4
  23.9 1.7 %own_cut_kernel.1 = (f32[10,80,128]{2,1,0:T(8,128)S(1)}, f32[10,96,128]{2,1,0:T(8,128)S(1)}, f32[4,10,80,128]{3,2,1,0:T(8,128)S(1)}) custom-call(f32[1,10,128,128]{3,2,1,0:T(8,128)} %guess.5, f32[10,128,128]{2,1,0:T(8,128)} %initial.3, f32[10,128,128]{2,1,0:T(8,128)} %diff.3, f32[3,10,128,128]{3,2,1,0:T(8,128)} %vel.3), custom_call_target="tpu_custom_call" | custom-call | bytes 216000000 | tf_op jit(solution)/shard_map/own_cut_kernel/pallas_call | solution.py:617
  25.6 0.0 collective-permute-done.5.refs_4_
  25.6 0.0 collective-permute-done.3.refs_2_
  25.6 0.0 collective-permute-done.4.refs_3_
  25.6 1.1 %weight_kernel.1 = (f32[8,20,80,128]{3,2,1,0:T(8,128)S(1)}, f32[22,96,128]{2,1,0:T(8,128)S(1)}, f32[22,96,128]{2,1,0:T(8,128)S(1)}) custom-call(f32[4,10,80,128]{3,2,1,0:T(8,128)S(1)} %get-tuple-element.32.coeff_own, f32[10,96,128]{2,1,0:T(8,128)S(1)} %get-tuple-element.33.window, f32[10,80,128]{2,1,0:T(8,128)S(1)} %collective-permute-done.refs_0_, ...), custom_call_target="tpu_custom_call" | custom-call | bytes 10800000 | tf_op jit(solution)/shard_map/weight_kernel/pallas_call | solution.py:617
  26.7 7.3 %collective-permute-done.6.refs_1_ = f32[2,10,80,128]{3,2,1,0:T(8,128)S(1)} collective-permute-done((f32[2,10,80,128]{3,2,1,0:T(8,128)S(1)}, f32[2,10,80,128]{3,2,1,0:T(8,128)S(1)}, u32[]{:S(2)}, u32[]{:S(2)}) %collective-permute-start.6) | collective-permute-done | bytes 819232 | tf_op jit(solution)/shard_map/ppermute | solution.py:86
  34.1 0.4 field_kernel.1
  34.5 0.1 collective-permute-start.7
  34.5 9.1 %total_kernel.1 = (f32[10,64,128]{2,1,0:T(8,128)S(1)}, f32[10,64,128]{2,1,0:T(8,128)S(1)}) custom-call(f32[8,20,80,128]{3,2,1,0:T(8,128)S(1)} %get-tuple-element.41.coeff, f32[22,96,128]{2,1,0:T(8,128)S(1)} %get-tuple-element.48.ahead, f32[2,22,96,128]{3,2,1,0:T(8,128)S(1)} %get-tuple-element.44.fields), custom_call_target="tpu_custom_call" | custom-call | bytes 54000000 | tf_op jit(solution)/shard_map/total_kernel/pallas_call | solution.py:617
  43.6 0.1 collective-permute-start.8
  43.7 1.6 %collective-permute-done.8.got = f32[10,64,128]{2,1,0:T(8,128)S(1)} collective-permute-done((f32[10,64,128]{2,1,0:T(8,128)S(1)}, f32[10,64,128]{2,1,0:T(8,128)S(1)}, u32[]{:S(2)}, u32[]{:S(2)}) %collective-permute-start.8) | collective-permute-done | bytes 327712 | tf_op jit(solution)/shard_map/ppermute | solution.py:86
  45.3 0.1 part_kernel.1
  45.4 0.7 collective-permute-start.9
  46.1 1.3 %collective-permute-start.10 = (f32[10,48,128]{2,1,0:T(8,128)S(1)}, f32[10,48,128]{2,1,0:T(8,128)S(1)}, u32[]{:S(2)}, u32[]{:S(2)}) collective-permute-start(f32[10,48,128]{2,1,0:T(8,128)S(1)} %get-tuple-element.52), channel_id=1, source_target_pairs={{0,16},{1,17},{2,18},{3,19},{4,20},{5,21},{6,22},{7,23},{8,24},{9,... | collective-permute-start | bytes 737288 | tf_op jit(solution)/shard_map/ppermute | solution.py:86
  47.4 3.2 %collective-permute-start.11 = (f32[10,40,128]{2,1,0:T(8,128)S(1)}, f32[10,40,128]{2,1,0:T(8,128)S(1)}, u32[]{:S(2)}, u32[]{:S(2)}) collective-permute-start(f32[10,40,128]{2,1,0:T(8,128)S(1)} %get-tuple-element.53), channel_id=1, source_target_pairs={{0,8},{1,9},{2,10},{3,11},{4,12},{5,13},{6,14},{7,15},{8,16},{9,17... | collective-permute-start | bytes 614408 | tf_op jit(solution)/shard_map/ppermute | solution.py:86
  50.6 0.0 collective-permute-done.7.flipped
  50.6 5.9 %term_kernel.1 = (f32[2,20,32,128]{3,2,1,0:T(8,128)S(1)}, f32[20,48,128]{2,1,0:T(8,128)S(1)}) custom-call(f32[8,20,80,128]{3,2,1,0:T(8,128)S(1)} %get-tuple-element.41.coeff, f32[2,22,96,128]{3,2,1,0:T(8,128)S(1)} %get-tuple-element.44.fields, f32[2,20,64,128]{3,2,1,0:T(8,128)S(1)} %collective-permute-done.7.flipped, f32[22,96,128]{2,1,0:T(8,128)S(1)} %get-tuple-element.46.seed), custom_call_target="tpu_custom_call" | custom-call | bytes 54000000 | tf_op jit(solution)/shard_map/term_kernel/pallas_call | solution.py:617
  56.5 15.8 %collective-permute-done.11.refs_2_ = f32[10,40,128]{2,1,0:T(8,128)S(1)} collective-permute-done((f32[10,40,128]{2,1,0:T(8,128)S(1)}, f32[10,40,128]{2,1,0:T(8,128)S(1)}, u32[]{:S(2)}, u32[]{:S(2)}) %collective-permute-start.11) | collective-permute-done | bytes 204832 | tf_op jit(solution)/shard_map/ppermute | solution.py:86
  72.4 0.0 collective-permute-done.10.refs_1_
  72.4 0.0 collective-permute-done.9.refs_0_
  72.4 2.1 %start_kernel.1.share = f32[20,48,128]{2,1,0:T(8,128)S(1)} custom-call(f32[8,20,80,128]{3,2,1,0:T(8,128)S(1)} %get-tuple-element.41.coeff, f32[20,48,128]{2,1,0:T(8,128)S(1)} %get-tuple-element.47.begun, f32[10,56,128]{2,1,0:T(8,128)S(1)} %collective-permute-done.9.refs_0_, f32[10,48,128]{2,1,0:T(8,128)S(1)} %collective-permute-done.10.refs_1_, ...), custom_call_target="tpu_custom_call" | custom-call | bytes 21600000 | tf_op jit(solution)/shard_map/start_kernel/pallas_call | solution.py:617
  74.4 0.1 collective-permute-start.12
  74.5 1.9 %collective-permute-done.12.other = f32[20,48,128]{2,1,0:T(8,128)S(1)} collective-permute-done((f32[20,48,128]{2,1,0:T(8,128)S(1)}, f32[20,48,128]{2,1,0:T(8,128)S(1)}, u32[]{:S(2)}, u32[]{:S(2)}) %collective-permute-start.12) | collective-permute-done | bytes 491552 | tf_op jit(solution)/shard_map/ppermute | solution.py:86
  76.4 1.5 %end_kernel.1 = (f32[10,32,128]{2,1,0:T(8,128)S(1)}, f32[10,32,128]{2,1,0:T(8,128)S(1)}, f32[10,32,128]{2,1,0:T(8,128)S(1)}, f32[10,32,128]{2,1,0:T(8,128)S(1)}) custom-call(f32[8,20,80,128]{3,2,1,0:T(8,128)S(1)} %get-tuple-element.41.coeff, f32[20,48,128]{2,1,0:T(8,128)S(1)} %start_kernel.1.share, f32[20,48,128]{2,1,0:T(8,128)S(1)} %collective-permute-done.12.other, ...), custom_call_target="tpu_custom_call" | custom-call | bytes 10800000 | tf_op jit(solution)/shard_map/end_kernel/pallas_call | solution.py:617
  77.9 1.4 %collective-permute-start.13 = (f32[10,32,128]{2,1,0:T(8,128)S(1)}, f32[10,32,128]{2,1,0:T(8,128)S(1)}, u32[]{:S(2)}, u32[]{:S(2)}) collective-permute-start(f32[10,32,128]{2,1,0:T(8,128)S(1)} %get-tuple-element.56), channel_id=1, source_target_pairs={{0,4},{1,5},{2,6},{3,7},{4,0},{5,1},{6,2},{7,3},{8,12},{9,13},{10,... | collective-permute-start | bytes 491528 | tf_op jit(solution)/shard_map/ppermute | solution.py:86
  79.2 0.7 collective-permute-start.14
  79.9 1.5 %collective-permute-start.15 = (f32[10,32,128]{2,1,0:T(8,128)S(1)}, f32[10,32,128]{2,1,0:T(8,128)S(1)}, u32[]{:S(2)}, u32[]{:S(2)}) collective-permute-start(f32[10,32,128]{2,1,0:T(8,128)S(1)} %get-tuple-element.58), channel_id=1, source_target_pairs={{0,5},{1,4},{2,7},{3,6},{4,1},{5,0},{6,3},{7,2},{8,13},{9,12},{10,... | collective-permute-start | bytes 491528 | tf_op jit(solution)/shard_map/ppermute | solution.py:86
  81.4 2.8 %collective-permute-done.13.refs_1_ = f32[10,32,128]{2,1,0:T(8,128)S(1)} collective-permute-done((f32[10,32,128]{2,1,0:T(8,128)S(1)}, f32[10,32,128]{2,1,0:T(8,128)S(1)}, u32[]{:S(2)}, u32[]{:S(2)}) %collective-permute-start.13) | collective-permute-done | bytes 163872 | tf_op jit(solution)/shard_map/ppermute | solution.py:86
  84.2 2.1 %collective-permute-done.14.refs_2_ = f32[10,32,128]{2,1,0:T(8,128)S(1)} collective-permute-done((f32[10,32,128]{2,1,0:T(8,128)S(1)}, f32[10,32,128]{2,1,0:T(8,128)S(1)}, u32[]{:S(2)}, u32[]{:S(2)}) %collective-permute-start.14) | collective-permute-done | bytes 163872 | tf_op jit(solution)/shard_map/ppermute | solution.py:86
  86.3 2.6 %collective-permute-done.15.refs_3_ = f32[10,32,128]{2,1,0:T(8,128)S(1)} collective-permute-done((f32[10,32,128]{2,1,0:T(8,128)S(1)}, f32[10,32,128]{2,1,0:T(8,128)S(1)}, u32[]{:S(2)}, u32[]{:S(2)}) %collective-permute-start.15) | collective-permute-done | bytes 163872 | tf_op jit(solution)/shard_map/ppermute | solution.py:86
  88.9 0.9 place_kernel.1
Async XLA Ops:
  1.3 12.5 %collective-permute-start.1 = (f32[10,88,128]{2,1,0:T(8,128)S(1)}, f32[10,88,128]{2,1,0:T(8,128)S(1)}, u32[]{:S(2)}, u32[]{:S(2)}) collective-permute-start(f32[10,88,128]{2,1,0:T(8,128)S(1)} %get-tuple-element.35), channel_id=1, source_target_pairs={{0,4},{1,5},{2,6},{3,7},{4,0},{5,1},{6,2},{7,3},{8,12},{9,13},{10,... | collective-permute-start | bytes 1351688 | tf_op jit(solution)/shard_map/ppermute | solution.py:86
  2.9 10.9 %collective-permute-start = (f32[10,80,128]{2,1,0:T(8,128)S(1)}, f32[10,80,128]{2,1,0:T(8,128)S(1)}, u32[]{:S(2)}, u32[]{:S(2)}) collective-permute-start(f32[10,80,128]{2,1,0:T(8,128)S(1)} %get-tuple-element.34), channel_id=1, source_target_pairs={{0,1},{1,0},{2,3},{3,2},{4,5},{5,4},{6,7},{7,6},{8,9},{9,8},{10,11... | collective-permute-start | bytes 1228808 | tf_op jit(solution)/shard_map/ppermute | solution.py:86
  13.8 10.0 %collective-permute-start.2 = (f32[10,80,128]{2,1,0:T(8,128)S(1)}, f32[10,80,128]{2,1,0:T(8,128)S(1)}, u32[]{:S(2)}, u32[]{:S(2)}) collective-permute-start(f32[10,80,128]{2,1,0:T(8,128)S(1)} %collective-permute-done.refs_0_), channel_id=1, source_target_pairs={{0,8},{1,9},{2,10},{3,11},{4,12},{5,13},{6,14},{7,15},{8,0},{9,1},... | collective-permute-start | bytes 1228808 | tf_op jit(solution)/shard_map/ppermute | solution.py:86
  15.5 18.6 %collective-permute-start.6 = (f32[2,10,80,128]{3,2,1,0:T(8,128)S(1)}, f32[2,10,80,128]{3,2,1,0:T(8,128)S(1)}, u32[]{:S(2)}, u32[]{:S(2)}) collective-permute-start(f32[2,10,80,128]{3,2,1,0:T(8,128)S(1)} %mix_kernel.1), channel_id=1, source_target_pairs={{0,1},{1,0},{2,3},{3,2},{4,5},{5,4},{6,7},{7,6},{8,9},{9,8},{10,11... | collective-permute-start | bytes 2457608 | tf_op jit(solution)/shard_map/ppermute | solution.py:86
  16.1 9.5 %collective-permute-start.5 = (f32[10,96,128]{2,1,0:T(8,128)S(1)}, f32[10,96,128]{2,1,0:T(8,128)S(1)}, u32[]{:S(2)}, u32[]{:S(2)}) collective-permute-start(f32[10,96,128]{2,1,0:T(8,128)S(1)} %get-tuple-element.37), channel_id=1, source_target_pairs={{24,1},{25,0},{28,5},{29,4}} | collective-permute-start | bytes 1474568 | tf_op jit(solution)/shard_map/ppermute | solution.py:86
  16.8 8.8 %collective-permute-start.3 = (f32[10,80,128]{2,1,0:T(8,128)S(1)}, f32[10,80,128]{2,1,0:T(8,128)S(1)}, u32[]{:S(2)}, u32[]{:S(2)}) collective-permute-start(f32[10,80,128]{2,1,0:T(8,128)S(1)} %collective-permute-done.refs_0_), channel_id=1, source_target_pairs={{0,2},{1,3},{2,0},{3,1},{4,6},{5,7},{6,4},{7,5},{8,10},{9,11},{10,... | collective-permute-start | bytes 1228808 | tf_op jit(solution)/shard_map/ppermute | solution.py:86
  23.9 1.8 %collective-permute-start.4 = (f32[10,80,128]{2,1,0:T(8,128)S(1)}, f32[10,80,128]{2,1,0:T(8,128)S(1)}, u32[]{:S(2)}, u32[]{:S(2)}) collective-permute-start(f32[10,80,128]{2,1,0:T(8,128)S(1)} %collective-permute-done.2.refs_1_), channel_id=1, source_target_pairs={{0,2},{1,3},{2,0},{3,1},{4,6},{5,7},{6,4},{7,5},{8,10},{9,11},{10,... | collective-permute-start | bytes 1228808 | tf_op jit(solution)/shard_map/ppermute | solution.py:86
  34.5 16.1 %collective-permute-start.7 = (f32[2,20,64,128]{3,2,1,0:T(8,128)S(1)}, f32[2,20,64,128]{3,2,1,0:T(8,128)S(1)}, u32[]{:S(2)}, u32[]{:S(2)}) collective-permute-start(f32[2,20,64,128]{3,2,1,0:T(8,128)S(1)} %get-tuple-element.45), channel_id=1, source_target_pairs={{0,2},{1,3},{2,0},{3,1},{4,6},{5,7},{6,4},{7,5},{8,10},{9,11},{10,... | collective-permute-start | bytes 3932168 | tf_op jit(solution)/shard_map/ppermute | solution.py:86
  43.6 1.7 %collective-permute-start.8 = (f32[10,64,128]{2,1,0:T(8,128)S(1)}, f32[10,64,128]{2,1,0:T(8,128)S(1)}, u32[]{:S(2)}, u32[]{:S(2)}) collective-permute-start(f32[10,64,128]{2,1,0:T(8,128)S(1)} %get-tuple-element.50), channel_id=1, source_target_pairs={{0,2},{1,3},{2,0},{3,1},{4,6},{5,7},{6,4},{7,5},{8,10},{9,11},{10,... | collective-permute-start | bytes 983048 | tf_op jit(solution)/shard_map/ppermute | solution.py:86
  45.4 26.9 %collective-permute-start.9 = (f32[10,56,128]{2,1,0:T(8,128)S(1)}, f32[10,56,128]{2,1,0:T(8,128)S(1)}, u32[]{:S(2)}, u32[]{:S(2)}) collective-permute-start(f32[10,56,128]{2,1,0:T(8,128)S(1)} %get-tuple-element.51), channel_id=1, source_target_pairs={{0,24},{1,25},{2,26},{3,27},{4,28},{5,29},{6,30},{7,31}} | collective-permute-start | bytes 860168 | tf_op jit(solution)/shard_map/ppermute | solution.py:86
  46.1 26.2 %collective-permute-start.10 = (f32[10,48,128]{2,1,0:T(8,128)S(1)}, f32[10,48,128]{2,1,0:T(8,128)S(1)}, u32[]{:S(2)}, u32[]{:S(2)}) collective-permute-start(f32[10,48,128]{2,1,0:T(8,128)S(1)} %get-tuple-element.52), channel_id=1, source_target_pairs={{0,16},{1,17},{2,18},{3,19},{4,20},{5,21},{6,22},{7,23},{8,24},{9,... | collective-permute-start | bytes 737288 | tf_op jit(solution)/shard_map/ppermute | solution.py:86
  47.4 24.9 %collective-permute-start.11 = (f32[10,40,128]{2,1,0:T(8,128)S(1)}, f32[10,40,128]{2,1,0:T(8,128)S(1)}, u32[]{:S(2)}, u32[]{:S(2)}) collective-permute-start(f32[10,40,128]{2,1,0:T(8,128)S(1)} %get-tuple-element.53), channel_id=1, source_target_pairs={{0,8},{1,9},{2,10},{3,11},{4,12},{5,13},{6,14},{7,15},{8,16},{9,17... | collective-permute-start | bytes 614408 | tf_op jit(solution)/shard_map/ppermute | solution.py:86
  74.4 1.9 %collective-permute-start.12 = (f32[20,48,128]{2,1,0:T(8,128)S(1)}, f32[20,48,128]{2,1,0:T(8,128)S(1)}, u32[]{:S(2)}, u32[]{:S(2)}) collective-permute-start(f32[20,48,128]{2,1,0:T(8,128)S(1)} %start_kernel.1.share), channel_id=1, source_target_pairs={{0,2},{1,3},{2,0},{3,1},{4,6},{5,7},{6,4},{7,5},{8,10},{9,11},{10,... | collective-permute-start | bytes 1474568 | tf_op jit(solution)/shard_map/ppermute | solution.py:86
  77.9 6.3 %collective-permute-start.13 = (f32[10,32,128]{2,1,0:T(8,128)S(1)}, f32[10,32,128]{2,1,0:T(8,128)S(1)}, u32[]{:S(2)}, u32[]{:S(2)}) collective-permute-start(f32[10,32,128]{2,1,0:T(8,128)S(1)} %get-tuple-element.56), channel_id=1, source_target_pairs={{0,4},{1,5},{2,6},{3,7},{4,0},{5,1},{6,2},{7,3},{8,12},{9,13},{10,... | collective-permute-start | bytes 491528 | tf_op jit(solution)/shard_map/ppermute | solution.py:86
  79.2 7.1 %collective-permute-start.14 = (f32[10,32,128]{2,1,0:T(8,128)S(1)}, f32[10,32,128]{2,1,0:T(8,128)S(1)}, u32[]{:S(2)}, u32[]{:S(2)}) collective-permute-start(f32[10,32,128]{2,1,0:T(8,128)S(1)} %get-tuple-element.57), channel_id=1, source_target_pairs={{0,1},{1,0},{2,3},{3,2},{4,5},{5,4},{6,7},{7,6},{8,9},{9,8},{10,11... | collective-permute-start | bytes 491528 | tf_op jit(solution)/shard_map/ppermute | solution.py:86
  79.9 9.0 %collective-permute-start.15 = (f32[10,32,128]{2,1,0:T(8,128)S(1)}, f32[10,32,128]{2,1,0:T(8,128)S(1)}, u32[]{:S(2)}, u32[]{:S(2)}) collective-permute-start(f32[10,32,128]{2,1,0:T(8,128)S(1)} %get-tuple-element.58), channel_id=1, source_target_pairs={{0,5},{1,4},{2,7},{3,6},{4,1},{5,0},{6,3},{7,2},{8,13},{9,12},{10,... | collective-permute-start | bytes 491528 | tf_op jit(solution)/shard_map/ppermute | solution.py:86
